TPU v7x, 32 devices: a whole 2x2x4 slice. The times are simulated.
32 devices in a mesh: row: 2 (over y), col: 16 (over z, x, core).
Axes of the slice: x: 2, y: 2, z: 4, core: 2. Of those that a mesh axis runs over, the one named last changes fastest.
Arguments:
- first_factor_strip: bfloat16 [1024, 2048], P('row', 'col'), may hold values from -16 to 16
- second_factor_strip: bfloat16 [2048, 6144], P('row', 'col'), may hold values from -0.125 to 0.125
- first_factor_support: int32 [8, 16], P('row', 'col'), may hold values 0 or 1
- second_factor_support: int32 [16, 48], P('row', 'col'), may hold values 0 or 1
- retained_blocks: int32 [8, 48], P('row', 'col'), may hold values 0 or 1
- target_bands: int32 [2, 16, 12, 1], P('row', 'col'), may hold values from 0 to 1; in each aligned block of 12 rows (0 to 11, 12 to 23, ..., all dimensions but the last counted through in order) at most 6 rows name the same one
Outputs:
- stochastic_result: bfloat16 [1024, 6144], P('row', 'col')
- redistributed_result: bfloat16 [3072, 2048], P('row', 'col')
Inputs may be any that keep to these rules, and one draw needn't show every extreme that they name: `target_bands`: among the tiles of one block no destination is named more than 6 times, and in some block one destination is named exactly 6 times.
All inputs are finite; a program needn't handle non-finite values. No bound on the sum of `first_factor_support` or of `second_factor_support` or of `retained_blocks` on one device may be relied on, other than what follows from the above.
Results may differ from a plain program's by a relative error of at most 0.001.
Values may be sent and summed in bfloat16 or wider, within the bound.
No kernel may reach another device: no remote copies, remote signals or barrier semaphores. Data moves between devices by JAX's collectives and lax.ppermute only.
A program may use at most 64 MiB of HBM per device.

v0:
```python
import jax
import jax.numpy as jnp
from jax import lax
from jax.sharding import PartitionSpec as P

BLOCK_EDGE = 128


def squaring_pass(values, pattern):
    row_tiles, col_tiles = pattern.shape
    shaped = values.reshape(row_tiles, BLOCK_EDGE, col_tiles, BLOCK_EDGE)
    return (shaped * pattern[:, None, :, None].astype(values.dtype)).reshape(values.shape)


def body(
    first_factor_strip,
    second_factor_strip,
    first_factor_support,
    second_factor_support,
    retained_blocks,
    target_bands,
):
    a_eff = squaring_pass(first_factor_strip, first_factor_support)
    b_eff = squaring_pass(second_factor_strip, second_factor_support)
    a_whole = lax.all_gather(a_eff, "col", axis=1, tiled=True)
    multiplied_blocks = jnp.dot(
        a_whole,
        lax.all_gather(b_eff, "row", axis=0, tiled=True),
        preferred_element_type=jnp.float32,
    )
    powered_blocks = squaring_pass(multiplied_blocks * multiplied_blocks, retained_blocks)
    totals = lax.psum(jnp.sum(powered_blocks, axis=0), "row")
    block_bands = lax.axis_size("row")
    all_rows = powered_blocks.shape[0] * block_bands
    stochastic_result = (powered_blocks / (totals / all_rows + 1e-05)).astype(jnp.bfloat16)
    tile_rows = stochastic_result.shape[0] // BLOCK_EDGE
    tile_cols = stochastic_result.shape[1] // BLOCK_EDGE
    tile_count = tile_rows * tile_cols
    berth_limit = max(2, (tile_count + block_bands - 1) // block_bands)
    tile_stack = stochastic_result.reshape(tile_rows, BLOCK_EDGE, tile_cols, BLOCK_EDGE).transpose(
        0, 2, 1, 3
    )
    tile_stack = tile_stack.reshape(tile_count, BLOCK_EDGE * BLOCK_EDGE)
    targets = target_bands.reshape(tile_count)
    same_target = targets[:, None] == targets[None, :]
    earlier = jnp.arange(tile_count)[None, :] < jnp.arange(tile_count)[:, None]
    slot_rank = jnp.sum((same_target & earlier).astype(jnp.int32), axis=1)
    position = targets * berth_limit + slot_rank
    selector = (jnp.arange(block_bands * berth_limit)[:, None] == position[None, :]).astype(
        jnp.bfloat16
    )
    outgoing = jnp.dot(selector, tile_stack, preferred_element_type=jnp.float32).astype(
        jnp.bfloat16
    )
    outgoing = outgoing.reshape(block_bands, berth_limit, BLOCK_EDGE, BLOCK_EDGE)
    delivered_blocks = lax.all_to_all(outgoing, "row", split_axis=0, concat_axis=0, tiled=True)
    redistributed_result = delivered_blocks.reshape(
        block_bands * berth_limit * BLOCK_EDGE, BLOCK_EDGE
    )
    return (stochastic_result, redistributed_result)


def solution(mesh):
    placed = (
        P("row", "col"),
        P("row", "col"),
        P("row", "col"),
        P("row", "col"),
        P("row", "col"),
        P("row", "col", None, None),
    )
    return jax.shard_map(
        body,
        mesh=mesh,
        in_specs=placed,
        out_specs=(P("row", "col"), P("row", "col")),
        check_vma=False,
    )
```

profile of v0, /device:TPU:0, one launch (start us, length us, event | category | flops | bytes accessed | tf_op | source)
XLA Modules:
  0.0 110.5 jit_solution(8982542127868047999)
XLA Ops:
  7.2 0.0 all-gather.5.cloned.1.call-start
  7.2 0.7 convert_element_type.31
  7.9 1.4 %copy.14 = bf16[1024,384]{0,1:T(8,128)(2,1)S(1)} copy(bf16[1024,384]{1,0:T(8,128)(2,1)} %param.7) | data formatting | bytes 1572864 | tf_op args[1]
  9.3 0.0 copy-start.3
  9.3 0.0 copy-start.1
  9.3 0.0 copy-start.2
  9.3 0.2 mul.51
  9.5 1.0 bitcast_multiply_fusion
  10.5 0.0 all-gather.5.cloned.1.call-update
  10.5 0.0 all-gather.3.cloned.1.call-start
  10.6 0.0 copy-done.3
  10.6 0.1 broadcast_bitcast_fusion
  10.7 0.0 copy-done.1
  10.7 0.8 broadcast_multiply_fusion
  11.5 0.0 copy-start.4
  11.5 0.0 all-gather.3.cloned.1.call-update
  11.5 0.0 copy-done.2
  11.5 0.1 copy.15
  11.6 0.2 mul.55
  11.8 0.1 copy.25
  11.8 0.3 copy.16
  12.1 0.0 copy-done.4
  12.1 0.2 convert_reduce_fusion
  12.3 28.3 %all-gather.5.cloned.1.call-done = bf16[2048,384]{0,1:T(8,128)(2,1)} async-done(((bf16[1024,384]{0,1:T(8,128)(2,1)}), bf16[2048,384]{0,1:T(8,128)(2,1)}) %all-gather.5.cloned.1.call-update) | async-done | bytes 1572880 | tf_op jit(solution)/shard_map/all_gather | solution.py:28
  40.6 44.0 %all-gather.3.cloned.1.call-done = bf16[512,2048]{1,0:T(8,128)(2,1)} async-done(((bf16[512,128]{1,0:T(8,128)(2,1)}), bf16[512,2048]{1,0:T(8,128)(2,1)}) %all-gather.3.cloned.1.call-update) | async-done | bytes 2097168 | tf_op jit(solution)/shard_map/all_gather | solution.py:25
  84.5 3.3 %fusion.3 = (f32[384]{0:T(512)S(1)}, f32[512,384]{1,0:T(8,128)S(1)}) fusion(f32[512,384]{1,0:T(8,128)S(1)} %copy.16, bf16[512,2048]{1,0:T(8,128)(2,1)} %all-gather.3.cloned.1.call-done, bf16[2048,384]{0,1:T(8,128)(2,1)} %all-gather.5.cloned.1.call-done), kind=kOutput, calls=%fused_computation.16 | convolution fusion | flops 805895808 | bytes 5244416 | tf_op jit(solution)/shard_map/dot_general | solution.py:26
  87.9 4.9 %psum.7 = f32[384]{0:T(512)S(1)} all-reduce(f32[384]{0:T(512)S(1)} %get-tuple-element.2), channel_id=1, replica_groups=mesh['row'=2,'col'=16] {'row'}, use_global_device_ids=true, to_apply=%region_1.0 | all-reduce | flops 384 | bytes 3072 | tf_op jit(solution)/shard_map/psum | solution.py:32
  92.8 0.1 divide_convert_fusion
  92.9 0.0 copy-start
  92.9 0.2 copy.17
  93.1 0.1 reshape.57
  93.2 0.3 copy.18
  93.5 0.1 pad
  93.6 0.3 copy.21
  93.9 0.0 copy-done
  94.0 0.3 convolution_convert_fusion
  94.2 0.1 copy.22
  94.4 8.5 %all_to_all.5 = bf16[2,6,128,128]{3,2,1,0:T(8,128)(2,1)S(1)} all-to-all(bf16[2,6,128,128]{3,2,1,0:T(8,128)(2,1)S(1)} %bitcast.43), channel_id=1, replica_groups=mesh['row'=2,'col'=16] {'row'}, dimensions={0} | all-to-all | bytes 786432 | tf_op jit(solution)/shard_map/all_to_all | solution.py:56
  102.9 0.7 copy.27
  (5 shorter events, 0.0 us)
Async XLA Ops:
  7.2 33.4 %all-gather.5.cloned.1.call-start = ((), (), s32[]{:S(2)}) async-start(), calls=%async_computation.2 | async-start | bytes 2359296 | tf_op jit(solution)/shard_map/all_gather | solution.py:28
  9.3 1.3 %copy-start.3 = (s32[4,1]{0,1:T(1,128)S(1)}, s32[4,1]{0,1:T(1,128)}, u32[]{:S(2)}) copy-start(s32[4,1]{0,1:T(1,128)} %param.8) | copy-start | bytes 52
  9.3 1.4 %copy-start.1 = (bf16[512,128]{1,0:T(8,128)(2,1)S(1)}, bf16[512,128]{1,0:T(8,128)(2,1)}, u32[]{:S(2)}) copy-start(bf16[512,128]{1,0:T(8,128)(2,1)} %param.6) | copy-start | bytes 393220
  9.3 2.2 %copy-start.2 = (s32[4,3]{1,0:T(4,128)S(1)}, s32[4,3]{1,0:T(4,128)}, u32[]{:S(2)}) copy-start(s32[4,3]{1,0:T(4,128)} %param.10) | copy-start | bytes 148
  10.5 74.0 %all-gather.3.cloned.1.call-start = ((), (), s32[]{:S(2)}) async-start(), calls=%async_computation.1 | async-start | bytes 2228224 | tf_op jit(solution)/shard_map/all_gather | solution.py:25
  11.5 0.7 copy-start.4
  92.9 1.1 copy-start
Sparse Core Ops, SparseCore 0:
  10.6 29.8 all-gather.4
  43.3 41.1 all-gather.2
where the time goes:
time: 111 us; the launch traced here: 110 us
  waiting for transfers between devices  72.3 us (65%)
  between operations  14.2 us (13%)
  blocking collectives  13.5 us (12%)
  local copies, waits for them, and re-layouts  4.13 us (4%)
  matrix products  3.6 us (3%)
  other arithmetic  2.73 us (2%)
    all_gather x1, waiting for transfers between devices, body(): a_whole = lax.all_gather(a_eff, 'col', axis=1, tiled=True)  44 us
    all_gather x1, waiting for transfers between devices, body(): lax.all_gather(b_eff, 'row', axis=0, tiled=True)  28.3 us
    all_to_all x1, blocking collectives, body(): lax.all_to_all(outgoing, 'row', split_axis=0, concat_axis=0, tiled=True)  8.52 us
    psum x1, blocking collectives, body(): totals = lax.psum(jnp.sum(powered_blocks, axis=0), 'row')  4.94 us
    dot_general x1, matrix products, body(): jnp.dot(a_whole, lax.all_gather(b_eff, 'row', axis=0, tiled=True), prefer...  3.32 us
    unnamed x17, local copies, waits for them, and re-layouts  2.75 us
  transfers between devices with their start and end apart: 2, of which 2 were waited for; matrix products, arithmetic and copies ran while one was open for 1% of the time, Pallas kernels for 0%

commit v1 on v0

v1 whole, which is shorter than its diff:
```python
import functools

import jax
import jax.numpy as jnp
from jax import lax
from jax.experimental import pallas as pl
from jax.experimental.pallas import tpu as pltpu
from jax.sharding import PartitionSpec as P

EDGE = 128
VMEM = pltpu.VMEM
SMEM = pltpu.SMEM
LIMIT = 48 * 1024 * 1024


def squaring_pass(values, pattern):
    row_tiles, col_tiles = pattern.shape
    shaped = values.reshape(row_tiles, EDGE, col_tiles, EDGE)
    return (shaped * pattern[:, None, :, None].astype(values.dtype)).reshape(values.shape)


def berths(tile_count, bands):
    return max(2, (tile_count + bands - 1) // bands)


def body_any(a, b, a_support, b_support, retained, target_bands):
    a_whole = lax.all_gather(squaring_pass(a, a_support), "col", axis=1, tiled=True)
    b_whole = lax.all_gather(squaring_pass(b, b_support), "row", axis=0, tiled=True)
    product = jnp.dot(a_whole, b_whole, preferred_element_type=jnp.float32)
    inflated = squaring_pass(product * product, retained)
    totals = lax.psum(jnp.sum(inflated, axis=0), "row")
    bands = lax.axis_size("row")
    all_rows = inflated.shape[0] * bands
    result = (inflated / (totals / all_rows + 1e-05)).astype(jnp.bfloat16)
    tile_rows, tile_cols = retained.shape
    tile_count = tile_rows * tile_cols
    limit = berths(tile_count, bands)
    stack = result.reshape(tile_rows, EDGE, tile_cols, EDGE).transpose(0, 2, 1, 3)
    stack = stack.reshape(tile_count, EDGE * EDGE)
    targets = target_bands.reshape(tile_count)
    same_target = targets[:, None] == targets[None, :]
    earlier = jnp.arange(tile_count)[None, :] < jnp.arange(tile_count)[:, None]
    rank = jnp.sum((same_target & earlier).astype(jnp.int32), axis=1)
    position = targets * limit + rank
    selector = (jnp.arange(bands * limit)[:, None] == position[None, :]).astype(jnp.bfloat16)
    outgoing = jnp.dot(selector, stack, preferred_element_type=jnp.float32).astype(jnp.bfloat16)
    outgoing = outgoing.reshape(bands, limit, EDGE, EDGE)
    delivered = lax.all_to_all(outgoing, "row", split_axis=0, concat_axis=0, tiled=True)
    return result, delivered.reshape(bands * limit * EDGE, EDGE)


def mask_kernel(support, a, out):
    for r in range(support.shape[0]):
        rows = pl.ds(r * EDGE, EDGE)
        out[rows, :] = a[rows, :] * support[r].astype(jnp.float32).astype(a.dtype)


def product_kernel(where, own_support, other_support, retained, b_own, b_other, *refs):
    *pieces, inflated, totals, b_scratch = refs
    tiles = b_own.shape[0] // EDGE
    cols = b_own.shape[1] // EDGE
    i, j = where[0], where[1]
    for half, support, b in ((i, own_support, b_own), (1 - i, other_support, b_other)):
        for q in range(tiles):
            m = lax.bitwise_xor(j, half * tiles + q)
            for c in range(cols):
                lanes = pl.ds(c * EDGE, EDGE)
                keep = support[q * cols + c].astype(jnp.float32).astype(b.dtype)
                b_scratch[m, :, lanes] = b[q * EDGE:(q + 1) * EDGE, lanes] * keep
    a = jnp.concatenate([p[...] for p in pieces], axis=1)
    b = b_scratch[...].reshape(-1, b_own.shape[1])
    product = jnp.dot(a, b, preferred_element_type=jnp.float32)
    squares = product * product
    rows = a.shape[0] // EDGE
    total = [None] * cols
    for r in range(rows):
        for c in range(cols):
            keep = retained[r * cols + c].astype(jnp.float32)
            tile = squares[r * EDGE:(r + 1) * EDGE, c * EDGE:(c + 1) * EDGE] * keep
            inflated[pl.ds(r * EDGE, EDGE), pl.ds(c * EDGE, EDGE)] = tile
            part = jnp.sum(tile.reshape(EDGE // 8, 8, EDGE), axis=0)
            total[c] = part if r == 0 else total[c] + part
    for c in range(cols):
        totals[:, pl.ds(c * EDGE, EDGE)] = total[c]


def finish_kernel(all_rows, limit, where, targets, inflated, own, other, result, placed, outgoing):
    cols = inflated.shape[1] // EDGE
    rows = inflated.shape[0] // EDGE
    i = where[0]
    total = jnp.sum(own[...] + other[...], axis=0, keepdims=True)
    scale = 1.0 / (total / all_rows + 1e-05)
    if 2 * limit != rows * cols:
        placed[...] = jnp.zeros_like(placed)
        outgoing[...] = jnp.zeros_like(outgoing)
    kept = jnp.int32(0)
    sent = jnp.int32(0)
    for t in range(rows * cols):
        r, c = t // cols, t % cols
        lanes = slice(c * EDGE, (c + 1) * EDGE)
        tile = inflated[r * EDGE:(r + 1) * EDGE, lanes] * scale[:, lanes]
        tile = tile.astype(jnp.bfloat16)
        result[r * EDGE:(r + 1) * EDGE, lanes] = tile
        stays = targets[t] == i

        @pl.when(stays)
        def _():
            placed[i * limit + kept] = tile

        @pl.when(jnp.logical_not(stays))
        def _():
            outgoing[sent] = tile

        one = stays.astype(jnp.int32)
        kept = kept + one
        sent = sent + 1 - one


def body_pair(a, b, a_support, b_support, retained, target_bands):
    n_col = lax.axis_size("col")
    swap = [(0, 1), (1, 0)]
    i, j = lax.axis_index("row"), lax.axis_index("col")
    where = jnp.stack([i, j]).astype(jnp.int32)

    def across(values, mask):
        return lax.ppermute(values, "col", [(k, k ^ mask) for k in range(n_col)])

    b_other = lax.ppermute(b, "row", swap)
    own_support = b_support.reshape(-1)
    other_support = lax.ppermute(b_support, "row", swap).reshape(-1)
    whole = pl.BlockSpec(memory_space=VMEM)
    scalars = pl.BlockSpec(memory_space=SMEM)
    a_eff = pl.pallas_call(
        mask_kernel,
        out_shape=jax.ShapeDtypeStruct(a.shape, a.dtype),
        in_specs=[scalars, whole],
        out_specs=whole,
        name="mask_left",
    )(a_support.reshape(-1), a)

    pieces = {0: a_eff}
    bits = [k for k in (1 << e for e in range(n_col.bit_length())) if 2 < k < n_col]
    for bit in reversed(bits):
        pieces[bit] = across(a_eff, bit)
    pieces[2] = across(a_eff, 2)
    for m in range(4, n_col, 4):
        if m not in pieces:
            low = m & -m
            pieces[m] = across(pieces[m ^ low], low)
    for m in range(4, n_col, 4):
        pieces[m | 2] = across(pieces[m], 2)
    order = sorted(pieces)
    for m in order:
        pieces[m | 1] = across(pieces[m], 1)
    stacked = [pieces[m] for m in range(n_col)]

    rows, columns = a.shape[0], b.shape[1]
    inflated, totals = pl.pallas_call(
        product_kernel,
        out_shape=(
            jax.ShapeDtypeStruct((rows, columns), jnp.float32),
            jax.ShapeDtypeStruct((8, columns), jnp.float32),
        ),
        in_specs=[scalars] * 4 + [whole] * (2 + n_col),
        out_specs=(whole, whole),
        scratch_shapes=[VMEM((n_col, EDGE, columns), b.dtype)],
        compiler_params=pltpu.CompilerParams(vmem_limit_bytes=LIMIT),
        name="expand_inflate",
    )(where, own_support, other_support, retained.reshape(-1), b, b_other, *stacked)

    other_totals = lax.ppermute(totals, "row", swap)
    tile_count = retained.shape[0] * retained.shape[1]
    limit = berths(tile_count, 2)
    result, placed, outgoing = pl.pallas_call(
        functools.partial(finish_kernel, 2 * rows, limit),
        out_shape=(
            jax.ShapeDtypeStruct((rows, columns), jnp.bfloat16),
            jax.ShapeDtypeStruct((2 * limit, EDGE, EDGE), jnp.bfloat16),
            jax.ShapeDtypeStruct((limit, EDGE, EDGE), jnp.bfloat16),
        ),
        in_specs=[scalars] * 2 + [whole] * 3,
        out_specs=(whole, whole, whole),
        compiler_params=pltpu.CompilerParams(vmem_limit_bytes=LIMIT),
        name="normalise_place",
    )(where, target_bands.reshape(-1), inflated, totals, other_totals)
    arrived = lax.ppermute(outgoing, "row", swap)
    placed = lax.dynamic_update_slice(placed, arrived, ((1 - i) * limit, 0, 0))
    return result, placed.reshape(2 * limit * EDGE, EDGE)


def solution(mesh):
    n_row, n_col = mesh.shape["row"], mesh.shape["col"]
    paired = n_row == 2 and n_col >= 4 and n_col & (n_col - 1) == 0
    placed = (P("row", "col"),) * 5 + (P("row", "col", None, None),)
    return jax.shard_map(
        body_pair if paired else body_any,
        mesh=mesh,
        in_specs=placed,
        out_specs=(P("row", "col"), P("row", "col")),
        check_vma=False,
    )
```

time: 111 us -> 54 us (0.49)
  waiting for transfers between devices: 72.3 us -> 24.9 us
  starting transfers between devices: 0.08 us -> 18.3 us
  between operations: 14.2 us -> 0.69 us
  blocking collectives: 13.5 us -> 0 us
  Pallas kernels: 0 us -> 5.32 us
  matrix products: 3.6 us -> 0 us
  other arithmetic: 2.73 us -> 0.07 us
    all_gather x2 -> x0, waiting for transfers between devices: 72.2 us -> none  [the longest x1 44 us: body(): a_whole = lax.all_gather(a_eff, 'col', axis=1, tiled=True)]
    ppermute x0 -> x19, waiting for transfers between devices: none -> 24.9 us  [the longest x1 10 us: body_pair(): other_support = lax.ppermute(b_support, 'row', swap).reshape(-1)]
    ppermute x0 -> x19, starting transfers between devices: none -> 18.3 us  [the longest x15 11.6 us: across(): return lax.ppermute(values, 'col', [(k, k ^ mask) for k in range(n_col)])]
    all_to_all x1 -> x0, blocking collectives: 8.52 us -> none  [body(): lax.all_to_all(outgoing, 'row', split_axis=0, concat_axis=0, tiled=True)]
    pallas_call x0 -> x3, Pallas kernels: none -> 5.32 us  [the longest x1 2.12 us: body_pair(): pl.pallas_call(product_kernel, out_shape=(jax.ShapeDtypeStruct((rows, col...]
    psum x1 -> x0, blocking collectives: 4.94 us -> none  [body(): totals = lax.psum(jnp.sum(powered_blocks, axis=0), 'row')]
    dot_general x2 -> x0, matrix products: 3.6 us -> none  [the longest x1 3.32 us: body(): jnp.dot(a_whole, lax.all_gather(b_eff, 'row', axis=0, tiled=True), prefer...]
    mul x2 -> x0, other arithmetic: 1.78 us -> none  [squaring_pass(): shaped * pattern[:, None, :, None].astype(values.dtype)]
  transfers between devices with their start and end apart: 2 -> 19, of which waited for: 2 -> 8; matrix products, arithmetic and copies ran while one was open for 1% -> 1% of each run, Pallas kernels for 0% -> 3%
where the time goes in v1:
time: 54 us; the launch traced here: 53.8 us
  waiting for transfers between devices  24.9 us (46%)
  starting transfers between devices  18.3 us (34%)
  Pallas kernels  5.32 us (10%)
  local copies, waits for them, and re-layouts  4.47 us (8%)
  between operations  0.69 us (1%)
    ppermute x15, starting transfers between devices, across(): return lax.ppermute(values, 'col', [(k, k ^ mask) for k in range(n_col)])  11.6 us
    ppermute x1, waiting for transfers between devices, body_pair(): other_support = lax.ppermute(b_support, 'row', swap).reshape(-1)  10 us
    ppermute x15, waiting for transfers between devices, across(): return lax.ppermute(values, 'col', [(k, k ^ mask) for k in range(n_col)])  8.23 us
    ppermute x1, waiting for transfers between devices, body_pair(): arrived = lax.ppermute(outgoing, 'row', swap)  4.5 us
    unnamed x11, local copies, waits for them, and re-layouts  3.46 us
    ppermute x1, starting transfers between devices, body_pair(): b_other = lax.ppermute(b, 'row', swap)  3.03 us
    ppermute x1, waiting for transfers between devices, body_pair(): other_totals = lax.ppermute(totals, 'row', swap)  2.18 us
    pallas_call x1, Pallas kernels, body_pair(): pl.pallas_call(product_kernel, out_shape=(jax.ShapeDtypeStruct((rows, col...  2.12 us
  transfers between devices with their start and end apart: 19, of which 8 were waited for; matrix products, arithmetic and copies ran while one was open for 1% of the time, Pallas kernels for 3%

profile of v1, /device:TPU:0, one launch (start us, length us, event | category | flops | bytes accessed | tf_op | source)
XLA Modules:
  0.0 53.8 jit_solution(15538830885775113336)
XLA Ops:
  0.6 3.0 %collective-permute-start.1 = (bf16[1024,384]{1,0:T(8,128)(2,1)}, bf16[1024,384]{1,0:T(8,128)(2,1)S(1)}, u32[]{:S(2)}, u32[]{:S(2)}) collective-permute-start(bf16[1024,384]{1,0:T(8,128)(2,1)} %b_own.1), channel_id=1, source_target_pairs={{0,16},{16,0},{1,17},{17,1},{2,18},{18,2},{3,19},{19,3},{4,20},{20... | collective-permute-start | bytes 2359304 | tf_op jit(solution)/shard_map/ppermute | solution.py:128
  3.7 1.6 %mask_left.1.refs_0_ = bf16[512,128]{1,0:T(8,128)(2,1)} custom-call(s32[4]{0:T(128)} %bitcast.6, bf16[512,128]{1,0:T(8,128)(2,1)} %a.1), custom_call_target="tpu_custom_call" | custom-call | tf_op jit(solution)/shard_map/mask_left/pallas_call | solution.py:133
  5.3 2.6 %collective-permute-start.9 = (bf16[512,128]{1,0:T(8,128)(2,1)}, bf16[512,128]{1,0:T(8,128)(2,1)S(1)}, u32[]{:S(2)}, u32[]{:S(2)}) collective-permute-start(bf16[512,128]{1,0:T(8,128)(2,1)} %mask_left.1.refs_0_), channel_id=1, source_target_pairs={{0,8},{1,9},{2,10},{3,11},{4,12},{5,13},{6,14},{7,15},{8,0},{9,1},... | collective-permute-start | bytes 393224 | tf_op jit(solution)/shard_map/ppermute | solution.py:126
  7.9 1.6 %collective-permute-start.5 = (bf16[512,128]{1,0:T(8,128)(2,1)}, bf16[512,128]{1,0:T(8,128)(2,1)S(1)}, u32[]{:S(2)}, u32[]{:S(2)}) collective-permute-start(bf16[512,128]{1,0:T(8,128)(2,1)} %mask_left.1.refs_0_), channel_id=1, source_target_pairs={{0,4},{1,5},{2,6},{3,7},{4,0},{5,1},{6,2},{7,3},{8,12},{9,13},{10,... | collective-permute-start | bytes 393224 | tf_op jit(solution)/shard_map/ppermute | solution.py:126
  9.4 1.5 %collective-permute-start.3 = (bf16[512,128]{1,0:T(8,128)(2,1)}, bf16[512,128]{1,0:T(8,128)(2,1)S(1)}, u32[]{:S(2)}, u32[]{:S(2)}) collective-permute-start(bf16[512,128]{1,0:T(8,128)(2,1)} %mask_left.1.refs_0_), channel_id=1, source_target_pairs={{0,2},{1,3},{2,0},{3,1},{4,6},{5,7},{6,4},{7,5},{8,10},{9,11},{10,... | collective-permute-start | bytes 393224 | tf_op jit(solution)/shard_map/ppermute | solution.py:126
  10.9 0.5 collective-permute-start
  11.4 10.0 %collective-permute-done = s32[8,3]{0,1:T(4,128)S(1)} collective-permute-done((s32[8,3]{0,1:T(4,128)S(1)}, s32[8,3]{0,1:T(4,128)S(1)}, u32[]{:S(2)}, u32[]{:S(2)}) %collective-permute-start) | collective-permute-done | bytes 128 | tf_op jit(solution)/shard_map/ppermute | solution.py:130
  21.5 0.0 collective-permute-start.2
  21.5 0.0 collective-permute-done.9.refs_8_
  21.5 1.8 %collective-permute-start.13 = (bf16[512,128]{1,0:T(8,128)(2,1)S(1)}, bf16[512,128]{1,0:T(8,128)(2,1)S(1)}, u32[]{:S(2)}, u32[]{:S(2)}) collective-permute-start(bf16[512,128]{1,0:T(8,128)(2,1)S(1)} %collective-permute-done.9.refs_8_), channel_id=1, source_target_pairs={{0,4},{1,5},{2,6},{3,7},{4,0},{5,1},{6,2},{7,3},{8,12},{9,13},{10,... | collective-permute-start | bytes 393224 | tf_op jit(solution)/shard_map/ppermute | solution.py:126
  23.3 0.0 collective-permute-done.5.refs_4_
  23.3 1.5 %collective-permute-start.11 = (bf16[512,128]{1,0:T(8,128)(2,1)S(1)}, bf16[512,128]{1,0:T(8,128)(2,1)S(1)}, u32[]{:S(2)}, u32[]{:S(2)}) collective-permute-start(bf16[512,128]{1,0:T(8,128)(2,1)S(1)} %collective-permute-done.9.refs_8_), channel_id=1, source_target_pairs={{0,2},{1,3},{2,0},{3,1},{4,6},{5,7},{6,4},{7,5},{8,10},{9,11},{10,... | collective-permute-start | bytes 393224 | tf_op jit(solution)/shard_map/ppermute | solution.py:126
  24.8 0.0 collective-permute-done.3.refs_2_
  24.8 0.0 collective-permute-start.10
  24.8 0.0 collective-permute-done.2.refs_1_
  24.8 0.6 %collective-permute-start.7 = (bf16[512,128]{1,0:T(8,128)(2,1)S(1)}, bf16[512,128]{1,0:T(8,128)(2,1)S(1)}, u32[]{:S(2)}, u32[]{:S(2)}) collective-permute-start(bf16[512,128]{1,0:T(8,128)(2,1)S(1)} %collective-permute-done.5.refs_4_), channel_id=1, source_target_pairs={{0,2},{1,3},{2,0},{3,1},{4,6},{5,7},{6,4},{7,5},{8,10},{9,11},{10,... | collective-permute-start | bytes 393224 | tf_op jit(solution)/shard_map/ppermute | solution.py:126
  25.4 2.1 %collective-permute-done.13.refs_12_ = bf16[512,128]{1,0:T(8,128)(2,1)S(1)} collective-permute-done((bf16[512,128]{1,0:T(8,128)(2,1)S(1)}, bf16[512,128]{1,0:T(8,128)(2,1)S(1)}, u32[]{:S(2)}, u32[]{:S(2)}) %collective-permute-start.13) | collective-permute-done | bytes 131104 | tf_op jit(solution)/shard_map/ppermute | solution.py:126
  27.4 0.0 collective-permute-start.6
  27.4 2.2 %collective-permute-done.11.refs_10_ = bf16[512,128]{1,0:T(8,128)(2,1)S(1)} collective-permute-done((bf16[512,128]{1,0:T(8,128)(2,1)S(1)}, bf16[512,128]{1,0:T(8,128)(2,1)S(1)}, u32[]{:S(2)}, u32[]{:S(2)}) %collective-permute-start.11) | collective-permute-done | bytes 131104 | tf_op jit(solution)/shard_map/ppermute | solution.py:126
  29.6 0.0 collective-permute-done.10.refs_9_
  29.6 1.5 %collective-permute-start.15 = (bf16[512,128]{1,0:T(8,128)(2,1)S(1)}, bf16[512,128]{1,0:T(8,128)(2,1)S(1)}, u32[]{:S(2)}, u32[]{:S(2)}) collective-permute-start(bf16[512,128]{1,0:T(8,128)(2,1)S(1)} %collective-permute-done.13.refs_12_), channel_id=1, source_target_pairs={{0,2},{1,3},{2,0},{3,1},{4,6},{5,7},{6,4},{7,5},{8,10},{9,11},{10,... | collective-permute-start | bytes 393224 | tf_op jit(solution)/shard_map/ppermute | solution.py:126
  31.1 0.6 %collective-permute-done.7.refs_6_ = bf16[512,128]{1,0:T(8,128)(2,1)S(1)} collective-permute-done((bf16[512,128]{1,0:T(8,128)(2,1)S(1)}, bf16[512,128]{1,0:T(8,128)(2,1)S(1)}, u32[]{:S(2)}, u32[]{:S(2)}) %collective-permute-start.7) | collective-permute-done | bytes 131104 | tf_op jit(solution)/shard_map/ppermute | solution.py:126
  31.7 0.0 collective-permute-start.14
  31.7 0.0 collective-permute-done.6.refs_5_
  31.7 0.5 collective-permute-start.12
  32.2 0.0 collective-permute-done.4.refs_3_
  32.2 0.1 collective-permute-start.8
  32.3 3.2 %collective-permute-done.15.refs_14_ = bf16[512,128]{1,0:T(8,128)(2,1)S(1)} collective-permute-done((bf16[512,128]{1,0:T(8,128)(2,1)S(1)}, bf16[512,128]{1,0:T(8,128)(2,1)S(1)}, u32[]{:S(2)}, u32[]{:S(2)}) %collective-permute-start.15) | collective-permute-done | bytes 131104 | tf_op jit(solution)/shard_map/ppermute | solution.py:126
  35.5 0.1 copy.10
  35.6 0.7 %copy-done.4 = s32[4,3]{1,0:T(4,128)S(1)} copy-done((s32[4,3]{1,0:T(4,128)S(1)}, s32[4,3]{1,0:T(4,128)}, u32[]{:S(2)}) %copy-start.4) | copy-done | bytes 72
  36.3 0.1 reshape.25.retained
  36.4 0.1 reshape.23.own_support
  36.4 0.1 pad_add_fusion.where
  36.5 0.1 copy.11
  36.6 0.1 reshape.24.other_support
  36.7 0.0 collective-permute-done.14.refs_13_
  36.7 0.2 collective-permute-done.16.refs_15_
  36.9 0.0 collective-permute-done.1.b_other
  36.9 1.1 %copy-done = bf16[1024,384]{1,0:T(8,128)(2,1)S(1)} copy-done((bf16[1024,384]{1,0:T(8,128)(2,1)S(1)}, bf16[1024,384]{1,0:T(8,128)(2,1)}, u32[]{:S(2)}) %copy-start) | copy-done | bytes 786456
  38.0 0.9 %copy-done.1 = bf16[512,128]{1,0:T(8,128)(2,1)S(1)} copy-done((bf16[512,128]{1,0:T(8,128)(2,1)S(1)}, bf16[512,128]{1,0:T(8,128)(2,1)}, u32[]{:S(2)}) %copy-start.1) | copy-done | bytes 131096
  38.9 2.1 %expand_inflate.1 = (f32[512,384]{1,0:T(8,128)S(1)}, f32[8,384]{1,0:T(8,128)S(1)}) custom-call(s32[2]{0:T(128)S(1)} %pad_add_fusion.where, s32[24]{0:T(128)S(1)} %reshape.23.own_support, s32[24]{0:T(128)S(1)} %reshape.24.other_support, s32[12]{0:T(128)S(1)} %reshape.25.retained, bf16[1024,384]{1,0:T(8,128)(2,1)S(1)} %copy-done, ...), custom_call_target="tpu_custom_call" | custom-call | tf_op jit(solution)/shard_map/expand_inflate/pallas_call | solution.py:158
  41.0 1.6 %collective-permute-start.17 = (f32[8,384]{1,0:T(8,128)S(1)}, f32[8,384]{1,0:T(8,128)S(1)}, u32[]{:S(2)}, u32[]{:S(2)}) collective-permute-start(f32[8,384]{1,0:T(8,128)S(1)} %get-tuple-element.8.own), channel_id=1, source_target_pairs={{0,16},{16,0},{1,17},{17,1},{2,18},{18,2},{3,19},{19,3},{4,20},{20... | collective-permute-start | bytes 36872 | tf_op jit(solution)/shard_map/ppermute | solution.py:171
  42.6 2.2 %collective-permute-done.17.other = f32[8,384]{1,0:T(8,128)S(1)} collective-permute-done((f32[8,384]{1,0:T(8,128)S(1)}, f32[8,384]{1,0:T(8,128)S(1)}, u32[]{:S(2)}, u32[]{:S(2)}) %collective-permute-start.17) | collective-permute-done | bytes 12320 | tf_op jit(solution)/shard_map/ppermute | solution.py:171
  44.8 0.7 %copy-done.2 = s32[1,1,12,1]{2,3,1,0:T(1,128)S(1)} copy-done((s32[1,1,12,1]{2,3,1,0:T(1,128)S(1)}, s32[1,1,12,1]{2,3,1,0:T(1,128)}, u32[]{:S(2)}) %copy-start.2) | copy-done | bytes 72
  45.5 1.6 %normalise_place.1 = (bf16[512,384]{1,0:T(8,128)(2,1)}, bf16[12,128,128]{2,1,0:T(8,128)(2,1)}, bf16[6,128,128]{2,1,0:T(8,128)(2,1)S(1)}) custom-call(s32[2]{0:T(128)S(1)} %pad_add_fusion.where, s32[12]{0:T(128)S(1)} %bitcast.5, f32[512,384]{1,0:T(8,128)S(1)} %get-tuple-element.7.inflated, f32[8,384]{1,0:T(8,128)S(1)} %get-tuple-element.8.own, ...), custom_call_target="tpu_custom_call" | custom-call | tf_op jit(solution)/shard_map/normalise_place/pallas_call | solution.py:174
  47.1 1.5 %collective-permute-start.18 = (bf16[6,128,128]{2,1,0:T(8,128)(2,1)S(1)}, bf16[6,128,128]{2,1,0:T(8,128)(2,1)S(1)}, u32[]{:S(2)}, u32[]{:S(2)}) collective-permute-start(bf16[6,128,128]{2,1,0:T(8,128)(2,1)S(1)} %get-tuple-element.11), channel_id=1, source_target_pairs={{0,16},{16,0},{1,17},{17,1},{2,18},{18,2},{3,19},{19,3},{4,20},{20... | collective-permute-start | bytes 589832 | tf_op jit(solution)/shard_map/ppermute | solution.py:186
  48.6 4.5 %collective-permute-done.18 = bf16[6,128,128]{2,1,0:T(8,128)(2,1)S(1)} collective-permute-done((bf16[6,128,128]{2,1,0:T(8,128)(2,1)S(1)}, bf16[6,128,128]{2,1,0:T(8,128)(2,1)S(1)}, u32[]{:S(2)}, u32[]{:S(2)}) %collective-permute-start.18) | collective-permute-done | bytes 196640 | tf_op jit(solution)/shard_map/ppermute | solution.py:186
  53.1 0.7 %constant_dynamic-update-slice_fusion = bf16[12,128,128]{2,1,0:T(8,128)(2,1)} fusion(bf16[12,128,128]{2,1,0:T(8,128)(2,1)} %get-tuple-element.10, bf16[6,128,128]{2,1,0:T(8,128)(2,1)S(1)} %collective-permute-done.18, s32[]{:T(128)S(6)} %select_n.3), kind=kLoop, calls=%fused_computation.1 | loop fusion | bytes 393220 | tf_op jit(solution)/shard_map/dynamic_update_slice | solution.py:187
  (10 shorter events, 0.0 us)
Async XLA Ops:
  0.6 36.2 %collective-permute-start.1 = (bf16[1024,384]{1,0:T(8,128)(2,1)}, bf16[1024,384]{1,0:T(8,128)(2,1)S(1)}, u32[]{:S(2)}, u32[]{:S(2)}) collective-permute-start(bf16[1024,384]{1,0:T(8,128)(2,1)} %b_own.1), channel_id=1, source_target_pairs={{0,16},{16,0},{1,17},{17,1},{2,18},{18,2},{3,19},{19,3},{4,20},{20... | collective-permute-start | bytes 2359304 | tf_op jit(solution)/shard_map/ppermute | solution.py:128
  3.7 7.3 %copy-start.3 = (s32[8,3]{0,1:T(4,128)S(1)}, s32[8,3]{0,1:T(4,128)}, u32[]{:S(2)}) copy-start(s32[8,3]{0,1:T(4,128)} %param.9) | copy-start | bytes 292
  5.3 16.2 %collective-permute-start.9 = (bf16[512,128]{1,0:T(8,128)(2,1)}, bf16[512,128]{1,0:T(8,128)(2,1)S(1)}, u32[]{:S(2)}, u32[]{:S(2)}) collective-permute-start(bf16[512,128]{1,0:T(8,128)(2,1)} %mask_left.1.refs_0_), channel_id=1, source_target_pairs={{0,8},{1,9},{2,10},{3,11},{4,12},{5,13},{6,14},{7,15},{8,0},{9,1},... | collective-permute-start | bytes 393224 | tf_op jit(solution)/shard_map/ppermute | solution.py:126
  7.9 15.4 %collective-permute-start.5 = (bf16[512,128]{1,0:T(8,128)(2,1)}, bf16[512,128]{1,0:T(8,128)(2,1)S(1)}, u32[]{:S(2)}, u32[]{:S(2)}) collective-permute-start(bf16[512,128]{1,0:T(8,128)(2,1)} %mask_left.1.refs_0_), channel_id=1, source_target_pairs={{0,4},{1,5},{2,6},{3,7},{4,0},{5,1},{6,2},{7,3},{8,12},{9,13},{10,... | collective-permute-start | bytes 393224 | tf_op jit(solution)/shard_map/ppermute | solution.py:126
  9.4 15.3 %collective-permute-start.3 = (bf16[512,128]{1,0:T(8,128)(2,1)}, bf16[512,128]{1,0:T(8,128)(2,1)S(1)}, u32[]{:S(2)}, u32[]{:S(2)}) collective-permute-start(bf16[512,128]{1,0:T(8,128)(2,1)} %mask_left.1.refs_0_), channel_id=1, source_target_pairs={{0,2},{1,3},{2,0},{3,1},{4,6},{5,7},{6,4},{7,5},{8,10},{9,11},{10,... | collective-permute-start | bytes 393224 | tf_op jit(solution)/shard_map/ppermute | solution.py:126
  10.9 10.5 %collective-permute-start = (s32[8,3]{0,1:T(4,128)S(1)}, s32[8,3]{0,1:T(4,128)S(1)}, u32[]{:S(2)}, u32[]{:S(2)}) collective-permute-start(s32[8,3]{0,1:T(4,128)S(1)} %copy-done.3), channel_id=1, source_target_pairs={{0,16},{16,0},{1,17},{17,1},{2,18},{18,2},{3,19},{19,3},{4,20},{20... | collective-permute-start | bytes 296 | tf_op jit(solution)/shard_map/ppermute | solution.py:130
  21.5 3.3 %collective-permute-start.2 = (bf16[512,128]{1,0:T(8,128)(2,1)}, bf16[512,128]{1,0:T(8,128)(2,1)S(1)}, u32[]{:S(2)}, u32[]{:S(2)}) collective-permute-start(bf16[512,128]{1,0:T(8,128)(2,1)} %mask_left.1.refs_0_), channel_id=1, source_target_pairs={{0,1},{1,0},{2,3},{3,2},{4,5},{5,4},{6,7},{7,6},{8,9},{9,8},{10,11... | collective-permute-start | bytes 393224 | tf_op jit(solution)/shard_map/ppermute | solution.py:126
  21.5 6.0 %collective-permute-start.13 = (bf16[512,128]{1,0:T(8,128)(2,1)S(1)}, bf16[512,128]{1,0:T(8,128)(2,1)S(1)}, u32[]{:S(2)}, u32[]{:S(2)}) collective-permute-start(bf16[512,128]{1,0:T(8,128)(2,1)S(1)} %collective-permute-done.9.refs_8_), channel_id=1, source_target_pairs={{0,4},{1,5},{2,6},{3,7},{4,0},{5,1},{6,2},{7,3},{8,12},{9,13},{10,... | collective-permute-start | bytes 393224 | tf_op jit(solution)/shard_map/ppermute | solution.py:126
  23.3 6.3 %collective-permute-start.11 = (bf16[512,128]{1,0:T(8,128)(2,1)S(1)}, bf16[512,128]{1,0:T(8,128)(2,1)S(1)}, u32[]{:S(2)}, u32[]{:S(2)}) collective-permute-start(bf16[512,128]{1,0:T(8,128)(2,1)S(1)} %collective-permute-done.9.refs_8_), channel_id=1, source_target_pairs={{0,2},{1,3},{2,0},{3,1},{4,6},{5,7},{6,4},{7,5},{8,10},{9,11},{10,... | collective-permute-start | bytes 393224 | tf_op jit(solution)/shard_map/ppermute | solution.py:126
  24.8 4.8 %collective-permute-start.10 = (bf16[512,128]{1,0:T(8,128)(2,1)S(1)}, bf16[512,128]{1,0:T(8,128)(2,1)S(1)}, u32[]{:S(2)}, u32[]{:S(2)}) collective-permute-start(bf16[512,128]{1,0:T(8,128)(2,1)S(1)} %collective-permute-done.9.refs_8_), channel_id=1, source_target_pairs={{0,1},{1,0},{2,3},{3,2},{4,5},{5,4},{6,7},{7,6},{8,9},{9,8},{10,11... | collective-permute-start | bytes 393224 | tf_op jit(solution)/shard_map/ppermute | solution.py:126
  24.8 6.9 %collective-permute-start.7 = (bf16[512,128]{1,0:T(8,128)(2,1)S(1)}, bf16[512,128]{1,0:T(8,128)(2,1)S(1)}, u32[]{:S(2)}, u32[]{:S(2)}) collective-permute-start(bf16[512,128]{1,0:T(8,128)(2,1)S(1)} %collective-permute-done.5.refs_4_), channel_id=1, source_target_pairs={{0,2},{1,3},{2,0},{3,1},{4,6},{5,7},{6,4},{7,5},{8,10},{9,11},{10,... | collective-permute-start | bytes 393224 | tf_op jit(solution)/shard_map/ppermute | solution.py:126
  27.4 4.3 %collective-permute-start.6 = (bf16[512,128]{1,0:T(8,128)(2,1)S(1)}, bf16[512,128]{1,0:T(8,128)(2,1)S(1)}, u32[]{:S(2)}, u32[]{:S(2)}) collective-permute-start(bf16[512,128]{1,0:T(8,128)(2,1)S(1)} %collective-permute-done.5.refs_4_), channel_id=1, source_target_pairs={{0,1},{1,0},{2,3},{3,2},{4,5},{5,4},{6,7},{7,6},{8,9},{9,8},{10,11... | collective-permute-start | bytes 393224 | tf_op jit(solution)/shard_map/ppermute | solution.py:126
  29.6 2.6 %collective-permute-start.4 = (bf16[512,128]{1,0:T(8,128)(2,1)S(1)}, bf16[512,128]{1,0:T(8,128)(2,1)S(1)}, u32[]{:S(2)}, u32[]{:S(2)}) collective-permute-start(bf16[512,128]{1,0:T(8,128)(2,1)S(1)} %collective-permute-done.3.refs_2_), channel_id=1, source_target_pairs={{0,1},{1,0},{2,3},{3,2},{4,5},{5,4},{6,7},{7,6},{8,9},{9,8},{10,11... | collective-permute-start | bytes 393224 | tf_op jit(solution)/shard_map/ppermute | solution.py:126
  29.6 5.9 %collective-permute-start.15 = (bf16[512,128]{1,0:T(8,128)(2,1)S(1)}, bf16[512,128]{1,0:T(8,128)(2,1)S(1)}, u32[]{:S(2)}, u32[]{:S(2)}) collective-permute-start(bf16[512,128]{1,0:T(8,128)(2,1)S(1)} %collective-permute-done.13.refs_12_), channel_id=1, source_target_pairs={{0,2},{1,3},{2,0},{3,1},{4,6},{5,7},{6,4},{7,5},{8,10},{9,11},{10,... | collective-permute-start | bytes 393224 | tf_op jit(solution)/shard_map/ppermute | solution.py:126
  31.7 5.0 %collective-permute-start.14 = (bf16[512,128]{1,0:T(8,128)(2,1)S(1)}, bf16[512,128]{1,0:T(8,128)(2,1)S(1)}, u32[]{:S(2)}, u32[]{:S(2)}) collective-permute-start(bf16[512,128]{1,0:T(8,128)(2,1)S(1)} %collective-permute-done.13.refs_12_), channel_id=1, source_target_pairs={{0,1},{1,0},{2,3},{3,2},{4,5},{5,4},{6,7},{7,6},{8,9},{9,8},{10,11... | collective-permute-start | bytes 393224 | tf_op jit(solution)/shard_map/ppermute | solution.py:126
  31.7 5.0 %collective-permute-start.12 = (bf16[512,128]{1,0:T(8,128)(2,1)S(1)}, bf16[512,128]{1,0:T(8,128)(2,1)S(1)}, u32[]{:S(2)}, u32[]{:S(2)}) collective-permute-start(bf16[512,128]{1,0:T(8,128)(2,1)S(1)} %collective-permute-done.11.refs_10_), channel_id=1, source_target_pairs={{0,1},{1,0},{2,3},{3,2},{4,5},{5,4},{6,7},{7,6},{8,9},{9,8},{10,11... | collective-permute-start | bytes 393224 | tf_op jit(solution)/shard_map/ppermute | solution.py:126
  32.2 4.5 %collective-permute-start.8 = (bf16[512,128]{1,0:T(8,128)(2,1)S(1)}, bf16[512,128]{1,0:T(8,128)(2,1)S(1)}, u32[]{:S(2)}, u32[]{:S(2)}) collective-permute-start(bf16[512,128]{1,0:T(8,128)(2,1)S(1)} %collective-permute-done.7.refs_6_), channel_id=1, source_target_pairs={{0,1},{1,0},{2,3},{3,2},{4,5},{5,4},{6,7},{7,6},{8,9},{9,8},{10,11... | collective-permute-start | bytes 393224 | tf_op jit(solution)/shard_map/ppermute | solution.py:126
  35.5 1.3 %collective-permute-start.16 = (bf16[512,128]{1,0:T(8,128)(2,1)S(1)}, bf16[512,128]{1,0:T(8,128)(2,1)S(1)}, u32[]{:S(2)}, u32[]{:S(2)}) collective-permute-start(bf16[512,128]{1,0:T(8,128)(2,1)S(1)} %collective-permute-done.15.refs_14_), channel_id=1, source_target_pairs={{0,1},{1,0},{2,3},{3,2},{4,5},{5,4},{6,7},{7,6},{8,9},{9,8},{10,11... | collective-permute-start | bytes 393224 | tf_op jit(solution)/shard_map/ppermute | solution.py:126
  35.6 0.7 %copy-start.4 = (s32[4,3]{1,0:T(4,128)S(1)}, s32[4,3]{1,0:T(4,128)}, u32[]{:S(2)}) copy-start(s32[4,3]{1,0:T(4,128)} %param.10) | copy-start | bytes 148
  36.9 1.1 %copy-start = (bf16[1024,384]{1,0:T(8,128)(2,1)S(1)}, bf16[1024,384]{1,0:T(8,128)(2,1)}, u32[]{:S(2)}) copy-start(bf16[1024,384]{1,0:T(8,128)(2,1)} %b_own.1) | copy-start | bytes 2359300
  38.0 0.9 %copy-start.1 = (bf16[512,128]{1,0:T(8,128)(2,1)S(1)}, bf16[512,128]{1,0:T(8,128)(2,1)}, u32[]{:S(2)}) copy-start(bf16[512,128]{1,0:T(8,128)(2,1)} %mask_left.1.refs_0_) | copy-start | bytes 393220
  41.0 3.8 %collective-permute-start.17 = (f32[8,384]{1,0:T(8,128)S(1)}, f32[8,384]{1,0:T(8,128)S(1)}, u32[]{:S(2)}, u32[]{:S(2)}) collective-permute-start(f32[8,384]{1,0:T(8,128)S(1)} %get-tuple-element.8.own), channel_id=1, source_target_pairs={{0,16},{16,0},{1,17},{17,1},{2,18},{18,2},{3,19},{19,3},{4,20},{20... | collective-permute-start | bytes 36872 | tf_op jit(solution)/shard_map/ppermute | solution.py:171
  44.8 0.7 %copy-start.2 = (s32[1,1,12,1]{2,3,1,0:T(1,128)S(1)}, s32[1,1,12,1]{2,3,1,0:T(1,128)}, u32[]{:S(2)}) copy-start(s32[1,1,12,1]{2,3,1,0:T(1,128)} %param.11) | copy-start | bytes 148
  47.1 6.0 %collective-permute-start.18 = (bf16[6,128,128]{2,1,0:T(8,128)(2,1)S(1)}, bf16[6,128,128]{2,1,0:T(8,128)(2,1)S(1)}, u32[]{:S(2)}, u32[]{:S(2)}) collective-permute-start(bf16[6,128,128]{2,1,0:T(8,128)(2,1)S(1)} %get-tuple-element.11), channel_id=1, source_target_pairs={{0,16},{16,0},{1,17},{17,1},{2,18},{18,2},{3,19},{19,3},{4,20},{20... | collective-permute-start | bytes 589832 | tf_op jit(solution)/shard_map/ppermute | solution.py:186

commit v2 on v1

v2 whole, which is shorter than its diff:
```python
import functools

import jax
import jax.numpy as jnp
from jax import lax
from jax.experimental import pallas as pl
from jax.experimental.pallas import tpu as pltpu
from jax.sharding import PartitionSpec as P

EDGE = 128
VMEM = pltpu.VMEM
SMEM = pltpu.SMEM
LIMIT = 48 * 1024 * 1024
STEPS = 65535.0
HALF = 32768
TINY = 1e-23


def squaring_pass(values, pattern):
    row_tiles, col_tiles = pattern.shape
    shaped = values.reshape(row_tiles, EDGE, col_tiles, EDGE)
    return (shaped * pattern[:, None, :, None].astype(values.dtype)).reshape(values.shape)


def berths(tile_count, bands):
    return max(2, (tile_count + bands - 1) // bands)


def body_any(a, b, a_support, b_support, retained, target_bands):
    a_whole = lax.all_gather(squaring_pass(a, a_support), "col", axis=1, tiled=True)
    b_whole = lax.all_gather(squaring_pass(b, b_support), "row", axis=0, tiled=True)
    product = jnp.dot(a_whole, b_whole, preferred_element_type=jnp.float32)
    inflated = squaring_pass(product * product, retained)
    totals = lax.psum(jnp.sum(inflated, axis=0), "row")
    bands = lax.axis_size("row")
    all_rows = inflated.shape[0] * bands
    result = (inflated / (totals / all_rows + 1e-05)).astype(jnp.bfloat16)
    tile_rows, tile_cols = retained.shape
    tile_count = tile_rows * tile_cols
    limit = berths(tile_count, bands)
    stack = result.reshape(tile_rows, EDGE, tile_cols, EDGE).transpose(0, 2, 1, 3)
    stack = stack.reshape(tile_count, EDGE * EDGE)
    targets = target_bands.reshape(tile_count)
    same_target = targets[:, None] == targets[None, :]
    earlier = jnp.arange(tile_count)[None, :] < jnp.arange(tile_count)[:, None]
    rank = jnp.sum((same_target & earlier).astype(jnp.int32), axis=1)
    position = targets * limit + rank
    selector = (jnp.arange(bands * limit)[:, None] == position[None, :]).astype(jnp.bfloat16)
    outgoing = jnp.dot(selector, stack, preferred_element_type=jnp.float32).astype(jnp.bfloat16)
    outgoing = outgoing.reshape(bands, limit, EDGE, EDGE)
    delivered = lax.all_to_all(outgoing, "row", split_axis=0, concat_axis=0, tiled=True)
    return result, delivered.reshape(bands * limit * EDGE, EDGE)


def gather_product_kernel(mine, theirs, b_own, b_other, *refs):
    *pieces, product, b_last, b_scratch, b_local, sem = refs
    copy = pltpu.make_async_copy(b_own, b_local, sem)
    copy.start()
    tiles = b_local.shape[0] // EDGE
    cols = b_local.shape[1] // EDGE
    i, j = mine[0], mine[1]
    for half, support, b in ((1 - i, theirs, b_other), (i, mine, b_local)):
        if b is b_local:
            copy.wait()
        for q in range(tiles):
            m = lax.bitwise_xor(j, half * tiles + q)
            for c in range(cols):
                lanes = pl.ds(c * EDGE, EDGE)
                keep = support[2 + q * cols + c].astype(jnp.float32).astype(b.dtype)
                b_scratch[m, :, lanes] = b[q * EDGE:(q + 1) * EDGE, lanes] * keep
    n = len(pieces)
    a = jnp.concatenate([p[...] for p in pieces], axis=1)
    b = b_scratch[:n].reshape(n * EDGE, -1)
    product[...] = jnp.dot(a, b, preferred_element_type=jnp.float32)
    b_last[...] = b_scratch[n:].reshape(b_last.shape)


def inflate_kernel(offsets, mine, part, b_last, even, odd, product, stats, codes):
    retained, targets = offsets
    a = jnp.concatenate([even[...], odd[...]], axis=1)
    whole = part[...] + jnp.dot(a, b_last[...], preferred_element_type=jnp.float32)
    rows, cols = whole.shape[0] // EDGE, whole.shape[1] // EDGE
    tops = []
    for c in range(cols):
        lanes = pl.ds(c * EDGE, EDGE)
        total = top = None
        for r in range(rows):
            keep = mine[retained + r * cols + c].astype(jnp.float32)
            tile = jnp.abs(whole[r * EDGE:(r + 1) * EDGE, c * EDGE:(c + 1) * EDGE]) * keep
            product[pl.ds(r * EDGE, EDGE), lanes] = tile
            stacked = tile.reshape(EDGE // 8, 8, EDGE)
            sums, peak = jnp.sum(stacked * stacked, axis=0), jnp.max(stacked, axis=0)
            total = sums if r == 0 else total + sums
            top = peak if r == 0 else jnp.maximum(top, peak)
        stats[pl.ds(0, 8), lanes] = total
        stats[pl.ds(8, 8), lanes] = top
        top = jnp.max(top, axis=0, keepdims=True)
        tops.append(jnp.where(top > TINY, STEPS / jnp.maximum(top, TINY), 0.0))
    if codes.shape[0] * 2 != rows * cols:
        codes[...] = jnp.full_like(codes, -HALF)
    sent = jnp.int32(0)
    for t in range(rows * cols):
        r, c = t // cols, t % cols
        leaves = mine[targets + t] != mine[0]

        @pl.when(leaves)
        def _():
            tile = product[pl.ds(r * EDGE, EDGE), pl.ds(c * EDGE, EDGE)]
            steps = (tile * tops[c] + 0.5).astype(jnp.int32) - HALF
            codes[sent] = steps.astype(codes.dtype)

        sent = sent + leaves.astype(jnp.int32)


def finish_kernel(all_rows, targets, limit, mine, theirs, product, own, other, result, placed, step, scale):
    rows, cols = product.shape[0] // EDGE, product.shape[1] // EDGE
    i = mine[0]
    total = jnp.sum(own[0:8, :] + other[0:8, :], axis=0, keepdims=True)
    inverse = 1.0 / (total / all_rows + 1e-05)
    top = jnp.max(other[8:16, :], axis=0, keepdims=True) / STEPS
    if 2 * limit != rows * cols:
        placed[...] = jnp.zeros_like(placed)
        step[...] = jnp.zeros_like(step)
        scale[...] = jnp.zeros_like(scale)
    kept = jnp.int32(0)
    come = jnp.int32(0)
    for t in range(rows * cols):
        r, c = t // cols, t % cols
        lanes = slice(c * EDGE, (c + 1) * EDGE)
        tile = product[r * EDGE:(r + 1) * EDGE, lanes]
        tile = (tile * tile * inverse[:, lanes]).astype(result.dtype)
        result[r * EDGE:(r + 1) * EDGE, lanes] = tile
        stays = mine[targets + t] == i
        comes = theirs[targets + t] == i

        @pl.when(stays)
        def _():
            placed[i * limit + kept] = tile

        @pl.when(comes)
        def _():
            step[come] = top[:, lanes]
            scale[come] = inverse[:, lanes]

        kept = kept + stays.astype(jnp.int32)
        come = come + comes.astype(jnp.int32)


def body_pair(a, b, a_support, b_support, retained, target_bands):
    n_col = lax.axis_size("col")
    swap = [(0, 1), (1, 0)]
    i, j = lax.axis_index("row"), lax.axis_index("col")
    rows, columns = a.shape[0], b.shape[1]
    tile_count = retained.shape[0] * retained.shape[1]
    limit = berths(tile_count, 2)
    retained_at = 2 + b_support.size
    targets_at = retained_at + tile_count

    def across(values, mask):
        return lax.ppermute(values, "col", [(k, k ^ mask) for k in range(n_col)])

    b_other = lax.ppermute(b, "row", swap)
    a_eff = squaring_pass(a, a_support)
    high = n_col // 2
    pieces = {0: a_eff}
    bits = [1 << e for e in range(n_col.bit_length()) if 2 < 1 << e < n_col]
    for bit in reversed(bits):
        pieces[bit] = across(a_eff, bit)
    pieces[2] = across(a_eff, 2)
    for m in range(4, n_col, 4):
        if m not in pieces:
            low = m & -m
            pieces[m] = across(pieces[m ^ low], low)
    for m in range(4, n_col, 4):
        pieces[m | 2] = across(pieces[m], 2)
    for m in sorted(pieces):
        pieces[m | 1] = across(pieces[m], 1)
    pieces = [pieces[m] for m in range(n_col)]

    mine = jnp.concatenate(
        [
            jnp.stack([i, j]).astype(jnp.int32),
            b_support.reshape(-1),
            retained.reshape(-1),
            target_bands.reshape(-1),
        ]
    )
    late, _ = lax.optimization_barrier((mine, pieces[high]))
    theirs = lax.ppermute(late, "row", swap)

    whole = pl.BlockSpec(memory_space=VMEM)
    scalars = pl.BlockSpec(memory_space=SMEM)
    params = pltpu.CompilerParams(vmem_limit_bytes=LIMIT)
    part, b_last = pl.pallas_call(
        gather_product_kernel,
        out_shape=(
            jax.ShapeDtypeStruct((rows, columns), jnp.float32),
            jax.ShapeDtypeStruct((2 * EDGE, columns), b.dtype),
        ),
        in_specs=[scalars] * 2 + [pl.BlockSpec(memory_space=pl.ANY)] + [whole] * (n_col - 1),
        out_specs=(whole, whole),
        scratch_shapes=[
            VMEM((n_col, EDGE, columns), b.dtype),
            VMEM(b.shape, b.dtype),
            pltpu.SemaphoreType.DMA,
        ],
        compiler_params=params,
        name="gather_product",
    )(mine, theirs, b, b_other, *pieces[:-2])

    product, stats, codes = pl.pallas_call(
        functools.partial(inflate_kernel, (retained_at, targets_at)),
        out_shape=(
            jax.ShapeDtypeStruct((rows, columns), jnp.float32),
            jax.ShapeDtypeStruct((16, columns), jnp.float32),
            jax.ShapeDtypeStruct((limit, EDGE, EDGE), jnp.int16),
        ),
        in_specs=[scalars] + [whole] * 4,
        out_specs=(whole, whole, whole),
        compiler_params=params,
        name="inflate",
    )(mine, part, b_last, *pieces[-2:])

    other_stats = lax.ppermute(stats, "row", swap)
    arrived = lax.ppermute(codes, "row", swap)
    result, placed, step, scale = pl.pallas_call(
        functools.partial(finish_kernel, 2 * rows, targets_at, limit),
        out_shape=(
            jax.ShapeDtypeStruct((rows, columns), jnp.bfloat16),
            jax.ShapeDtypeStruct((2 * limit, EDGE, EDGE), jnp.bfloat16),
            jax.ShapeDtypeStruct((limit, 1, EDGE), jnp.float32),
            jax.ShapeDtypeStruct((limit, 1, EDGE), jnp.float32),
        ),
        in_specs=[scalars] * 2 + [whole] * 3,
        out_specs=(whole,) * 4,
        compiler_params=params,
        name="finish",
    )(mine, theirs, product, stats, other_stats)
    values = (arrived.astype(jnp.float32) + HALF) * step
    values = (values * values * scale).astype(jnp.bfloat16)
    placed = lax.dynamic_update_slice(placed, values, ((1 - i) * limit, 0, 0))
    return result, placed.reshape(2 * limit * EDGE, EDGE)


def solution(mesh):
    n_row, n_col = mesh.shape["row"], mesh.shape["col"]
    paired = n_row == 2 and n_col >= 4 and n_col & (n_col - 1) == 0
    placed = (P("row", "col"),) * 5 + (P("row", "col", None, None),)
    return jax.shard_map(
        body_pair if paired else body_any,
        mesh=mesh,
        in_specs=placed,
        out_specs=(P("row", "col"), P("row", "col")),
        check_vma=False,
    )
```

time: 54 us -> 43.4 us (0.80)
  waiting for transfers between devices: 24.9 us -> 15.2 us
  other arithmetic: 0.07 us -> 2.48 us
  starting transfers between devices: 18.3 us -> 16.6 us
  local copies, waits for them, and re-layouts: 4.47 us -> 3.46 us
  Pallas kernels: 5.32 us -> 4.71 us
    ppermute x3, waiting for transfers between devices: 16.7 us -> 7.47 us  [the longest x1 3.03 us: body_pair(): theirs = lax.ppermute(late, 'row', swap)]
    mul x0 -> x1, other arithmetic: none -> 1.03 us  [squaring_pass(): shaped * pattern[:, None, :, None].astype(values.dtype)]
    ppermute x3, starting transfers between devices: 3.62 us -> 2.63 us  [the longest x1 1.1 us: body_pair(): other_stats = lax.ppermute(stats, 'row', swap)]
    dynamic_update_slice x0 -> x1, other arithmetic: none -> 0.79 us  [body_pair(): placed = lax.dynamic_update_slice(placed, values, ((1 - i) * limit, 0, 0))]
    ppermute x15, starting transfers between devices: 11.6 us -> 10.9 us  [across(): return lax.ppermute(values, 'col', [(k, k ^ mask) for k in range(n_col)])]
    dynamic_update_slice x1 -> x0, local copies, waits for them, and re-layouts: 0.69 us -> none  [body_pair(): placed = lax.dynamic_update_slice(placed, arrived, ((1 - i) * limit, 0, 0))]
    convert_element_type x0 -> x1, other arithmetic: none -> 0.66 us  [squaring_pass(): pattern[:, None, :, None].astype(values.dtype)]
    pallas_call x3, Pallas kernels: 5.32 us -> 4.71 us  [the longest x1 2.06 us: body_pair(): pl.pallas_call(gather_product_kernel, out_shape=(jax.ShapeDtypeStruct((ro...]
  transfers between devices with their start and end apart: 19 -> 19, of which waited for: 8 -> 6; matrix products, arithmetic and copies ran while one was open for 1% -> 5% of each run, Pallas kernels for 3% -> 8%
where the time goes in v2:
time: 43.4 us; the launch traced here: 43.2 us
  starting transfers between devices  16.6 us (38%)
  waiting for transfers between devices  15.2 us (35%)
  Pallas kernels  4.71 us (11%)
  local copies, waits for them, and re-layouts  3.46 us (8%)
  other arithmetic  2.48 us (6%)
  between operations  0.72 us (2%)
    ppermute x15, starting transfers between devices, across(): return lax.ppermute(values, 'col', [(k, k ^ mask) for k in range(n_col)])  10.9 us
    ppermute x15, waiting for transfers between devices, across(): return lax.ppermute(values, 'col', [(k, k ^ mask) for k in range(n_col)])  7.78 us
    unnamed x10, local copies, waits for them, and re-layouts  3.15 us
    ppermute x1, waiting for transfers between devices, body_pair(): theirs = lax.ppermute(late, 'row', swap)  3.03 us
    ppermute x1, starting transfers between devices, body_pair(): b_other = lax.ppermute(b, 'row', swap)  3.03 us
    ppermute x1, waiting for transfers between devices, body_pair(): arrived = lax.ppermute(codes, 'row', swap)  2.64 us
    pallas_call x1, Pallas kernels, body_pair(): pl.pallas_call(gather_product_kernel, out_shape=(jax.ShapeDtypeStruct((ro...  2.06 us
    ppermute x1, waiting for transfers between devices, body_pair(): other_stats = lax.ppermute(stats, 'row', swap)  1.8 us
  transfers between devices with their start and end apart: 19, of which 6 were waited for; matrix products, arithmetic and copies ran while one was open for 5% of the time, Pallas kernels for 8%

profile of v2, /device:TPU:0, one launch (start us, length us, event | category | flops | bytes accessed | tf_op | source)
XLA Modules:
  0.0 43.2 jit_solution(4021458659882423953)
XLA Ops:
  0.6 3.0 %collective-permute-start.2 = (bf16[1024,384]{1,0:T(8,128)(2,1)}, bf16[1024,384]{1,0:T(8,128)(2,1)S(1)}, u32[]{:S(2)}, u32[]{:S(2)}) collective-permute-start(bf16[1024,384]{1,0:T(8,128)(2,1)} %b_own.1), channel_id=1, source_target_pairs={{0,16},{16,0},{1,17},{17,1},{2,18},{18,2},{3,19},{19,3},{4,20},{20... | collective-permute-start | bytes 2359304 | tf_op jit(solution)/shard_map/ppermute | solution.py:162
  3.7 0.7 %convert_bitcast_fusion = bf16[4]{0:T(256)(128)(2,1)S(1)} fusion(s32[4,1]{0,1:T(1,128)} %param.8), kind=kLoop, calls=%fused_computation.5 | loop fusion | flops 4 | bytes 24 | tf_op jit(solution)/shard_map/convert_element_type | solution.py:22
  4.3 0.1 broadcast_bitcast_fusion
  4.4 1.0 %broadcast_multiply_fusion.refs_0_ = bf16[512,128]{1,0:T(8,128)(2,1)S(1)} fusion(bf16[512,128]{1,0:T(8,128)(2,1)} %param.6, bf16[512]{0:T(512)(128)(2,1)S(1)} %broadcast_bitcast_fusion), kind=kLoop, calls=%fused_computation.2 | loop fusion | flops 65536 | bytes 263168 | tf_op jit(solution)/shard_map/mul | solution.py:22
  5.4 2.7 %collective-permute-start = (bf16[512,128]{1,0:T(8,128)(2,1)S(1)}, bf16[512,128]{1,0:T(8,128)(2,1)S(1)}, u32[]{:S(2)}, u32[]{:S(2)}) collective-permute-start(bf16[512,128]{1,0:T(8,128)(2,1)S(1)} %broadcast_multiply_fusion.refs_0_), channel_id=1, source_target_pairs={{0,8},{1,9},{2,10},{3,11},{4,12},{5,13},{6,14},{7,15},{8,0},{9,1},... | collective-permute-start | bytes 393224 | tf_op jit(solution)/shard_map/ppermute | solution.py:160
  8.1 1.6 %collective-permute-start.6 = (bf16[512,128]{1,0:T(8,128)(2,1)S(1)}, bf16[512,128]{1,0:T(8,128)(2,1)S(1)}, u32[]{:S(2)}, u32[]{:S(2)}) collective-permute-start(bf16[512,128]{1,0:T(8,128)(2,1)S(1)} %broadcast_multiply_fusion.refs_0_), channel_id=1, source_target_pairs={{0,4},{1,5},{2,6},{3,7},{4,0},{5,1},{6,2},{7,3},{8,12},{9,13},{10,... | collective-permute-start | bytes 393224 | tf_op jit(solution)/shard_map/ppermute | solution.py:160
  9.7 1.5 %collective-permute-start.4 = (bf16[512,128]{1,0:T(8,128)(2,1)S(1)}, bf16[512,128]{1,0:T(8,128)(2,1)S(1)}, u32[]{:S(2)}, u32[]{:S(2)}) collective-permute-start(bf16[512,128]{1,0:T(8,128)(2,1)S(1)} %broadcast_multiply_fusion.refs_0_), channel_id=1, source_target_pairs={{0,2},{1,3},{2,0},{3,1},{4,6},{5,7},{6,4},{7,5},{8,10},{9,11},{10,... | collective-permute-start | bytes 393224 | tf_op jit(solution)/shard_map/ppermute | solution.py:160
  11.2 0.0 collective-permute-start.3
  11.2 3.1 %collective-permute-done.refs_8_ = bf16[512,128]{1,0:T(8,128)(2,1)S(1)} collective-permute-done((bf16[512,128]{1,0:T(8,128)(2,1)S(1)}, bf16[512,128]{1,0:T(8,128)(2,1)S(1)}, u32[]{:S(2)}, u32[]{:S(2)}) %collective-permute-start) | collective-permute-done | bytes 131104 | tf_op jit(solution)/shard_map/ppermute | solution.py:160
  14.3 0.6 %collective-permute-start.13 = (bf16[512,128]{1,0:T(8,128)(2,1)S(1)}, bf16[512,128]{1,0:T(8,128)(2,1)S(1)}, u32[]{:S(2)}, u32[]{:S(2)}) collective-permute-start(bf16[512,128]{1,0:T(8,128)(2,1)S(1)} %collective-permute-done.refs_8_), channel_id=1, source_target_pairs={{0,4},{1,5},{2,6},{3,7},{4,0},{5,1},{6,2},{7,3},{8,12},{9,13},{10,... | collective-permute-start | bytes 393224 | tf_op jit(solution)/shard_map/ppermute | solution.py:160
  14.8 0.0 collective-permute-done.6.refs_4_
  14.8 1.5 %collective-permute-start.11 = (bf16[512,128]{1,0:T(8,128)(2,1)S(1)}, bf16[512,128]{1,0:T(8,128)(2,1)S(1)}, u32[]{:S(2)}, u32[]{:S(2)}) collective-permute-start(bf16[512,128]{1,0:T(8,128)(2,1)S(1)} %collective-permute-done.refs_8_), channel_id=1, source_target_pairs={{0,2},{1,3},{2,0},{3,1},{4,6},{5,7},{6,4},{7,5},{8,10},{9,11},{10,... | collective-permute-start | bytes 393224 | tf_op jit(solution)/shard_map/ppermute | solution.py:160
  16.3 0.7 %copy-done.1 = s32[8,3]{0,1:T(4,128)S(1)} copy-done((s32[8,3]{0,1:T(4,128)S(1)}, s32[8,3]{0,1:T(4,128)}, u32[]{:S(2)}) %copy-start.1) | copy-done | bytes 120
  17.0 0.1 copy.9
  17.1 0.1 reshape.32
  17.2 0.6 %copy-done.2 = s32[4,3]{1,0:T(4,128)S(1)} copy-done((s32[4,3]{1,0:T(4,128)S(1)}, s32[4,3]{1,0:T(4,128)}, u32[]{:S(2)}) %copy-start.2) | copy-done | bytes 72
  17.8 0.1 reshape.33
  17.9 0.7 %copy-done.3 = s32[1,1,12,1]{2,3,1,0:T(1,128)S(1)} copy-done((s32[1,1,12,1]{2,3,1,0:T(1,128)S(1)}, s32[1,1,12,1]{2,3,1,0:T(1,128)}, u32[]{:S(2)}) %copy-start.3) | copy-done | bytes 72
  18.5 0.1 concatenate.3.mine
  18.6 0.0 collective-permute-done.3.refs_1_
  18.6 0.5 %collective-permute-start.1 = (s32[50]{0:T(128)S(1)}, s32[50]{0:T(128)S(1)}, u32[]{:S(2)}, u32[]{:S(2)}) collective-permute-start(s32[50]{0:T(128)S(1)} %concatenate.3.mine), channel_id=1, source_target_pairs={{0,16},{16,0},{1,17},{17,1},{2,18},{18,2},{3,19},{19,3},{4,20},{20... | collective-permute-start | bytes 608 | tf_op jit(solution)/shard_map/ppermute | solution.py:189
  19.1 3.0 %collective-permute-done.1.theirs = s32[50]{0:T(128)S(1)} collective-permute-done((s32[50]{0:T(128)S(1)}, s32[50]{0:T(128)S(1)}, u32[]{:S(2)}, u32[]{:S(2)}) %collective-permute-start.1) | collective-permute-done | bytes 232 | tf_op jit(solution)/shard_map/ppermute | solution.py:189
  22.2 1.0 %collective-permute-start.8 = (bf16[512,128]{1,0:T(8,128)(2,1)S(1)}, bf16[512,128]{1,0:T(8,128)(2,1)S(1)}, u32[]{:S(2)}, u32[]{:S(2)}) collective-permute-start(bf16[512,128]{1,0:T(8,128)(2,1)S(1)} %collective-permute-done.6.refs_4_), channel_id=1, source_target_pairs={{0,2},{1,3},{2,0},{3,1},{4,6},{5,7},{6,4},{7,5},{8,10},{9,11},{10,... | collective-permute-start | bytes 393224 | tf_op jit(solution)/shard_map/ppermute | solution.py:160
  23.2 0.0 collective-permute-done.13.refs_12_
  23.2 0.0 collective-permute-start.7
  23.2 0.0 collective-permute-done.11.refs_10_
  23.2 0.5 %collective-permute-start.5 = (bf16[512,128]{1,0:T(8,128)(2,1)S(1)}, bf16[512,128]{1,0:T(8,128)(2,1)S(1)}, u32[]{:S(2)}, u32[]{:S(2)}) collective-permute-start(bf16[512,128]{1,0:T(8,128)(2,1)S(1)} %collective-permute-done.4.refs_2_), channel_id=1, source_target_pairs={{0,1},{1,0},{2,3},{3,2},{4,5},{5,4},{6,7},{7,6},{8,9},{9,8},{10,11... | collective-permute-start | bytes 393224 | tf_op jit(solution)/shard_map/ppermute | solution.py:160
  23.7 0.0 collective-permute-done.10.refs_9_
  23.7 1.0 %collective-permute-start.15 = (bf16[512,128]{1,0:T(8,128)(2,1)S(1)}, bf16[512,128]{1,0:T(8,128)(2,1)S(1)}, u32[]{:S(2)}, u32[]{:S(2)}) collective-permute-start(bf16[512,128]{1,0:T(8,128)(2,1)S(1)} %collective-permute-done.13.refs_12_), channel_id=1, source_target_pairs={{0,2},{1,3},{2,0},{3,1},{4,6},{5,7},{6,4},{7,5},{8,10},{9,11},{10,... | collective-permute-start | bytes 393224 | tf_op jit(solution)/shard_map/ppermute | solution.py:160
  24.7 3.2 %collective-permute-done.8.refs_6_ = bf16[512,128]{1,0:T(8,128)(2,1)S(1)} collective-permute-done((bf16[512,128]{1,0:T(8,128)(2,1)S(1)}, bf16[512,128]{1,0:T(8,128)(2,1)S(1)}, u32[]{:S(2)}, u32[]{:S(2)}) %collective-permute-start.8) | collective-permute-done | bytes 131104 | tf_op jit(solution)/shard_map/ppermute | solution.py:160
  28.0 0.5 %collective-permute-start.12 = (bf16[512,128]{1,0:T(8,128)(2,1)S(1)}, bf16[512,128]{1,0:T(8,128)(2,1)S(1)}, u32[]{:S(2)}, u32[]{:S(2)}) collective-permute-start(bf16[512,128]{1,0:T(8,128)(2,1)S(1)} %collective-permute-done.11.refs_10_), channel_id=1, source_target_pairs={{0,1},{1,0},{2,3},{3,2},{4,5},{5,4},{6,7},{7,6},{8,9},{9,8},{10,11... | collective-permute-start | bytes 393224 | tf_op jit(solution)/shard_map/ppermute | solution.py:160
  28.5 0.1 collective-permute-start.9
  28.6 1.4 %collective-permute-done.15.even = bf16[512,128]{1,0:T(8,128)(2,1)S(1)} collective-permute-done((bf16[512,128]{1,0:T(8,128)(2,1)S(1)}, bf16[512,128]{1,0:T(8,128)(2,1)S(1)}, u32[]{:S(2)}, u32[]{:S(2)}) %collective-permute-start.15) | collective-permute-done | bytes 131104 | tf_op jit(solution)/shard_map/ppermute | solution.py:160
  30.0 0.0 collective-permute-done.14.refs_13_
  30.0 0.0 collective-permute-done.12.refs_11_
  30.0 0.0 collective-permute-done.9.refs_7_
  30.0 0.0 collective-permute-done.2.b_other
  30.0 0.0 copy-start
  30.0 1.1 %copy-done = bf16[1024,384]{1,0:T(8,128)(2,1)S(1)} copy-done((bf16[1024,384]{1,0:T(8,128)(2,1)S(1)}, bf16[1024,384]{1,0:T(8,128)(2,1)}, u32[]{:S(2)}) %copy-start) | copy-done | bytes 786456
  31.1 2.1 %gather_product.1 = (f32[512,384]{1,0:T(8,128)S(1)}, bf16[256,384]{1,0:T(8,128)(2,1)S(1)}) custom-call(s32[50]{0:T(128)S(1)} %concatenate.3.mine, s32[50]{0:T(128)S(1)} %collective-permute-done.1.theirs, bf16[1024,384]{1,0:T(8,128)(2,1)S(1)} %copy-done, bf16[1024,384]{1,0:T(8,128)(2,1)S(1)} %collective-permute-done.2.b_other, ...), custom_call_target="tpu_custom_call" | custom-call | tf_op jit(solution)/shard_map/gather_product/pallas_call | solution.py:194
  33.2 0.0 collective-permute-done.16.odd
  33.2 1.0 %inflate.1 = (f32[512,384]{1,0:T(8,128)S(1)}, f32[16,384]{1,0:T(8,128)S(1)}, s16[6,128,128]{2,1,0:T(8,128)(2,1)S(1)}) custom-call(s32[50]{0:T(128)S(1)} %concatenate.3.mine, f32[512,384]{1,0:T(8,128)S(1)} %get-tuple-element.13.part, bf16[256,384]{1,0:T(8,128)(2,1)S(1)} %get-tuple-element.14.b_last, bf16[512,128]{1,0:T(8,128)(2,1)S(1)} %collective-permute-done.15.even, ...), custom_call_target="tpu_custom_call" | custom-call | tf_op jit(solution)/shard_map/inflate/pallas_call | solution.py:211
  34.3 1.1 %collective-permute-start.17 = (f32[16,384]{1,0:T(8,128)S(1)}, f32[16,384]{1,0:T(8,128)S(1)}, u32[]{:S(2)}, u32[]{:S(2)}) collective-permute-start(f32[16,384]{1,0:T(8,128)S(1)} %get-tuple-element.16.own), channel_id=1, source_target_pairs={{0,16},{16,0},{1,17},{17,1},{2,18},{18,2},{3,19},{19,3},{4,20},{20... | collective-permute-start | bytes 73736 | tf_op jit(solution)/shard_map/ppermute | solution.py:224
  35.4 1.0 %collective-permute-start.18 = (s16[6,128,128]{2,1,0:T(8,128)(2,1)S(1)}, s16[6,128,128]{2,1,0:T(8,128)(2,1)S(1)}, u32[]{:S(2)}, u32[]{:S(2)}) collective-permute-start(s16[6,128,128]{2,1,0:T(8,128)(2,1)S(1)} %get-tuple-element.19), channel_id=1, source_target_pairs={{0,16},{16,0},{1,17},{17,1},{2,18},{18,2},{3,19},{19,3},{4,20},{20... | collective-permute-start | bytes 589832 | tf_op jit(solution)/shard_map/ppermute | solution.py:225
  36.3 1.8 %collective-permute-done.17.other = f32[16,384]{1,0:T(8,128)S(1)} collective-permute-done((f32[16,384]{1,0:T(8,128)S(1)}, f32[16,384]{1,0:T(8,128)S(1)}, u32[]{:S(2)}, u32[]{:S(2)}) %collective-permute-start.17) | collective-permute-done | bytes 24608 | tf_op jit(solution)/shard_map/ppermute | solution.py:224
  38.1 1.6 %finish.1 = (bf16[512,384]{1,0:T(8,128)(2,1)}, bf16[12,128,128]{2,1,0:T(8,128)(2,1)}, f32[6,1,128]{2,1,0:T(1,128)S(1)}, f32[6,1,128]{2,1,0:T(1,128)S(1)}) custom-call(s32[50]{0:T(128)S(1)} %concatenate.3.mine, s32[50]{0:T(128)S(1)} %collective-permute-done.1.theirs, f32[512,384]{1,0:T(8,128)S(1)} %get-tuple-element.15.product, ...), custom_call_target="tpu_custom_call" | custom-call | tf_op jit(solution)/shard_map/finish/pallas_call | solution.py:226
  39.8 2.6 %collective-permute-done.18 = s16[6,128,128]{2,1,0:T(8,128)(2,1)S(1)} collective-permute-done((s16[6,128,128]{2,1,0:T(8,128)(2,1)S(1)}, s16[6,128,128]{2,1,0:T(8,128)(2,1)S(1)}, u32[]{:S(2)}, u32[]{:S(2)}) %collective-permute-start.18) | collective-permute-done | bytes 196640 | tf_op jit(solution)/shard_map/ppermute | solution.py:225
  42.4 0.8 %fusion = bf16[12,128,128]{2,1,0:T(8,128)(2,1)} fusion(bf16[12,128,128]{2,1,0:T(8,128)(2,1)} %get-tuple-element.18, s32[]{:T(128)S(6)} %select_n.3, s16[6,128,128]{2,1,0:T(8,128)(2,1)S(1)} %collective-permute-done.18, f32[6,128]{1,0:T(8,128)S(1)} %get-tuple-element.22, f32[6,128]{1,0:T(8,128)S(1)} %get-tuple-element.23), kind=kLoop, calls=%fused_computation.1 | loop fusion | flops 589824 | bytes 399364 | tf_op jit(solution)/shard_map/dynamic_update_slice | solution.py:241
  (10 shorter events, 0.0 us)
Async XLA Ops:
  0.6 29.4 %collective-permute-start.2 = (bf16[1024,384]{1,0:T(8,128)(2,1)}, bf16[1024,384]{1,0:T(8,128)(2,1)S(1)}, u32[]{:S(2)}, u32[]{:S(2)}) collective-permute-start(bf16[1024,384]{1,0:T(8,128)(2,1)} %b_own.1), channel_id=1, source_target_pairs={{0,16},{16,0},{1,17},{17,1},{2,18},{18,2},{3,19},{19,3},{4,20},{20... | collective-permute-start | bytes 2359304 | tf_op jit(solution)/shard_map/ppermute | solution.py:162
  5.4 8.8 %collective-permute-start = (bf16[512,128]{1,0:T(8,128)(2,1)S(1)}, bf16[512,128]{1,0:T(8,128)(2,1)S(1)}, u32[]{:S(2)}, u32[]{:S(2)}) collective-permute-start(bf16[512,128]{1,0:T(8,128)(2,1)S(1)} %broadcast_multiply_fusion.refs_0_), channel_id=1, source_target_pairs={{0,8},{1,9},{2,10},{3,11},{4,12},{5,13},{6,14},{7,15},{8,0},{9,1},... | collective-permute-start | bytes 393224 | tf_op jit(solution)/shard_map/ppermute | solution.py:160
  8.1 6.8 %collective-permute-start.6 = (bf16[512,128]{1,0:T(8,128)(2,1)S(1)}, bf16[512,128]{1,0:T(8,128)(2,1)S(1)}, u32[]{:S(2)}, u32[]{:S(2)}) collective-permute-start(bf16[512,128]{1,0:T(8,128)(2,1)S(1)} %broadcast_multiply_fusion.refs_0_), channel_id=1, source_target_pairs={{0,4},{1,5},{2,6},{3,7},{4,0},{5,1},{6,2},{7,3},{8,12},{9,13},{10,... | collective-permute-start | bytes 393224 | tf_op jit(solution)/shard_map/ppermute | solution.py:160
  9.7 6.7 %collective-permute-start.4 = (bf16[512,128]{1,0:T(8,128)(2,1)S(1)}, bf16[512,128]{1,0:T(8,128)(2,1)S(1)}, u32[]{:S(2)}, u32[]{:S(2)}) collective-permute-start(bf16[512,128]{1,0:T(8,128)(2,1)S(1)} %broadcast_multiply_fusion.refs_0_), channel_id=1, source_target_pairs={{0,2},{1,3},{2,0},{3,1},{4,6},{5,7},{6,4},{7,5},{8,10},{9,11},{10,... | collective-permute-start | bytes 393224 | tf_op jit(solution)/shard_map/ppermute | solution.py:160
  11.2 7.4 %collective-permute-start.3 = (bf16[512,128]{1,0:T(8,128)(2,1)S(1)}, bf16[512,128]{1,0:T(8,128)(2,1)S(1)}, u32[]{:S(2)}, u32[]{:S(2)}) collective-permute-start(bf16[512,128]{1,0:T(8,128)(2,1)S(1)} %broadcast_multiply_fusion.refs_0_), channel_id=1, source_target_pairs={{0,1},{1,0},{2,3},{3,2},{4,5},{5,4},{6,7},{7,6},{8,9},{9,8},{10,11... | collective-permute-start | bytes 393224 | tf_op jit(solution)/shard_map/ppermute | solution.py:160
  14.3 8.9 %collective-permute-start.13 = (bf16[512,128]{1,0:T(8,128)(2,1)S(1)}, bf16[512,128]{1,0:T(8,128)(2,1)S(1)}, u32[]{:S(2)}, u32[]{:S(2)}) collective-permute-start(bf16[512,128]{1,0:T(8,128)(2,1)S(1)} %collective-permute-done.refs_8_), channel_id=1, source_target_pairs={{0,4},{1,5},{2,6},{3,7},{4,0},{5,1},{6,2},{7,3},{8,12},{9,13},{10,... | collective-permute-start | bytes 393224 | tf_op jit(solution)/shard_map/ppermute | solution.py:160
  14.8 8.4 %collective-permute-start.11 = (bf16[512,128]{1,0:T(8,128)(2,1)S(1)}, bf16[512,128]{1,0:T(8,128)(2,1)S(1)}, u32[]{:S(2)}, u32[]{:S(2)}) collective-permute-start(bf16[512,128]{1,0:T(8,128)(2,1)S(1)} %collective-permute-done.refs_8_), channel_id=1, source_target_pairs={{0,2},{1,3},{2,0},{3,1},{4,6},{5,7},{6,4},{7,5},{8,10},{9,11},{10,... | collective-permute-start | bytes 393224 | tf_op jit(solution)/shard_map/ppermute | solution.py:160
  16.3 7.4 %collective-permute-start.10 = (bf16[512,128]{1,0:T(8,128)(2,1)S(1)}, bf16[512,128]{1,0:T(8,128)(2,1)S(1)}, u32[]{:S(2)}, u32[]{:S(2)}) collective-permute-start(bf16[512,128]{1,0:T(8,128)(2,1)S(1)} %collective-permute-done.refs_8_), channel_id=1, source_target_pairs={{0,1},{1,0},{2,3},{3,2},{4,5},{5,4},{6,7},{7,6},{8,9},{9,8},{10,11... | collective-permute-start | bytes 393224 | tf_op jit(solution)/shard_map/ppermute | solution.py:160
  16.3 0.7 %copy-start.1 = (s32[8,3]{0,1:T(4,128)S(1)}, s32[8,3]{0,1:T(4,128)}, u32[]{:S(2)}) copy-start(s32[8,3]{0,1:T(4,128)} %param.9) | copy-start | bytes 292
  17.1 0.7 %copy-start.2 = (s32[4,3]{1,0:T(4,128)S(1)}, s32[4,3]{1,0:T(4,128)}, u32[]{:S(2)}) copy-start(s32[4,3]{1,0:T(4,128)} %param.10) | copy-start | bytes 148
  17.9 0.7 %copy-start.3 = (s32[1,1,12,1]{2,3,1,0:T(1,128)S(1)}, s32[1,1,12,1]{2,3,1,0:T(1,128)}, u32[]{:S(2)}) copy-start(s32[1,1,12,1]{2,3,1,0:T(1,128)} %param.11) | copy-start | bytes 148
  18.6 3.6 %collective-permute-start.1 = (s32[50]{0:T(128)S(1)}, s32[50]{0:T(128)S(1)}, u32[]{:S(2)}, u32[]{:S(2)}) collective-permute-start(s32[50]{0:T(128)S(1)} %concatenate.3.mine), channel_id=1, source_target_pairs={{0,16},{16,0},{1,17},{17,1},{2,18},{18,2},{3,19},{19,3},{4,20},{20... | collective-permute-start | bytes 608 | tf_op jit(solution)/shard_map/ppermute | solution.py:189
  22.2 5.8 %collective-permute-start.8 = (bf16[512,128]{1,0:T(8,128)(2,1)S(1)}, bf16[512,128]{1,0:T(8,128)(2,1)S(1)}, u32[]{:S(2)}, u32[]{:S(2)}) collective-permute-start(bf16[512,128]{1,0:T(8,128)(2,1)S(1)} %collective-permute-done.6.refs_4_), channel_id=1, source_target_pairs={{0,2},{1,3},{2,0},{3,1},{4,6},{5,7},{6,4},{7,5},{8,10},{9,11},{10,... | collective-permute-start | bytes 393224 | tf_op jit(solution)/shard_map/ppermute | solution.py:160
  23.2 4.8 %collective-permute-start.7 = (bf16[512,128]{1,0:T(8,128)(2,1)S(1)}, bf16[512,128]{1,0:T(8,128)(2,1)S(1)}, u32[]{:S(2)}, u32[]{:S(2)}) collective-permute-start(bf16[512,128]{1,0:T(8,128)(2,1)S(1)} %collective-permute-done.6.refs_4_), channel_id=1, source_target_pairs={{0,1},{1,0},{2,3},{3,2},{4,5},{5,4},{6,7},{7,6},{8,9},{9,8},{10,11... | collective-permute-start | bytes 393224 | tf_op jit(solution)/shard_map/ppermute | solution.py:160
  23.2 5.3 %collective-permute-start.5 = (bf16[512,128]{1,0:T(8,128)(2,1)S(1)}, bf16[512,128]{1,0:T(8,128)(2,1)S(1)}, u32[]{:S(2)}, u32[]{:S(2)}) collective-permute-start(bf16[512,128]{1,0:T(8,128)(2,1)S(1)} %collective-permute-done.4.refs_2_), channel_id=1, source_target_pairs={{0,1},{1,0},{2,3},{3,2},{4,5},{5,4},{6,7},{7,6},{8,9},{9,8},{10,11... | collective-permute-start | bytes 393224 | tf_op jit(solution)/shard_map/ppermute | solution.py:160
  23.7 6.2 %collective-permute-start.15 = (bf16[512,128]{1,0:T(8,128)(2,1)S(1)}, bf16[512,128]{1,0:T(8,128)(2,1)S(1)}, u32[]{:S(2)}, u32[]{:S(2)}) collective-permute-start(bf16[512,128]{1,0:T(8,128)(2,1)S(1)} %collective-permute-done.13.refs_12_), channel_id=1, source_target_pairs={{0,2},{1,3},{2,0},{3,1},{4,6},{5,7},{6,4},{7,5},{8,10},{9,11},{10,... | collective-permute-start | bytes 393224 | tf_op jit(solution)/shard_map/ppermute | solution.py:160
  28.0 2.0 %collective-permute-start.14 = (bf16[512,128]{1,0:T(8,128)(2,1)S(1)}, bf16[512,128]{1,0:T(8,128)(2,1)S(1)}, u32[]{:S(2)}, u32[]{:S(2)}) collective-permute-start(bf16[512,128]{1,0:T(8,128)(2,1)S(1)} %collective-permute-done.13.refs_12_), channel_id=1, source_target_pairs={{0,1},{1,0},{2,3},{3,2},{4,5},{5,4},{6,7},{7,6},{8,9},{9,8},{10,11... | collective-permute-start | bytes 393224 | tf_op jit(solution)/shard_map/ppermute | solution.py:160
  28.0 2.0 %collective-permute-start.12 = (bf16[512,128]{1,0:T(8,128)(2,1)S(1)}, bf16[512,128]{1,0:T(8,128)(2,1)S(1)}, u32[]{:S(2)}, u32[]{:S(2)}) collective-permute-start(bf16[512,128]{1,0:T(8,128)(2,1)S(1)} %collective-permute-done.11.refs_10_), channel_id=1, source_target_pairs={{0,1},{1,0},{2,3},{3,2},{4,5},{5,4},{6,7},{7,6},{8,9},{9,8},{10,11... | collective-permute-start | bytes 393224 | tf_op jit(solution)/shard_map/ppermute | solution.py:160
  28.5 1.5 %collective-permute-start.9 = (bf16[512,128]{1,0:T(8,128)(2,1)S(1)}, bf16[512,128]{1,0:T(8,128)(2,1)S(1)}, u32[]{:S(2)}, u32[]{:S(2)}) collective-permute-start(bf16[512,128]{1,0:T(8,128)(2,1)S(1)} %collective-permute-done.8.refs_6_), channel_id=1, source_target_pairs={{0,1},{1,0},{2,3},{3,2},{4,5},{5,4},{6,7},{7,6},{8,9},{9,8},{10,11... | collective-permute-start | bytes 393224 | tf_op jit(solution)/shard_map/ppermute | solution.py:160
  30.0 3.2 %collective-permute-start.16 = (bf16[512,128]{1,0:T(8,128)(2,1)S(1)}, bf16[512,128]{1,0:T(8,128)(2,1)S(1)}, u32[]{:S(2)}, u32[]{:S(2)}) collective-permute-start(bf16[512,128]{1,0:T(8,128)(2,1)S(1)} %collective-permute-done.15.even), channel_id=1, source_target_pairs={{0,1},{1,0},{2,3},{3,2},{4,5},{5,4},{6,7},{7,6},{8,9},{9,8},{10,11... | collective-permute-start | bytes 393224 | tf_op jit(solution)/shard_map/ppermute | solution.py:160
  30.0 1.1 %copy-start = (bf16[1024,384]{1,0:T(8,128)(2,1)S(1)}, bf16[1024,384]{1,0:T(8,128)(2,1)}, u32[]{:S(2)}) copy-start(bf16[1024,384]{1,0:T(8,128)(2,1)} %b_own.1) | copy-start | bytes 2359300
  34.3 3.9 %collective-permute-start.17 = (f32[16,384]{1,0:T(8,128)S(1)}, f32[16,384]{1,0:T(8,128)S(1)}, u32[]{:S(2)}, u32[]{:S(2)}) collective-permute-start(f32[16,384]{1,0:T(8,128)S(1)} %get-tuple-element.16.own), channel_id=1, source_target_pairs={{0,16},{16,0},{1,17},{17,1},{2,18},{18,2},{3,19},{19,3},{4,20},{20... | collective-permute-start | bytes 73736 | tf_op jit(solution)/shard_map/ppermute | solution.py:224
  35.4 7.0 %collective-permute-start.18 = (s16[6,128,128]{2,1,0:T(8,128)(2,1)S(1)}, s16[6,128,128]{2,1,0:T(8,128)(2,1)S(1)}, u32[]{:S(2)}, u32[]{:S(2)}) collective-permute-start(s16[6,128,128]{2,1,0:T(8,128)(2,1)S(1)} %get-tuple-element.19), channel_id=1, source_target_pairs={{0,16},{16,0},{1,17},{17,1},{2,18},{18,2},{3,19},{19,3},{4,20},{20... | collective-permute-start | bytes 589832 | tf_op jit(solution)/shard_map/ppermute | solution.py:225

commit v3 on v2

v3 whole, which is shorter than its diff:
```python
import functools

import jax
import jax.numpy as jnp
from jax import lax
from jax.experimental import pallas as pl
from jax.experimental.pallas import tpu as pltpu
from jax.sharding import PartitionSpec as P

EDGE = 128
VMEM = pltpu.VMEM
SMEM = pltpu.SMEM
LIMIT = 48 * 1024 * 1024
STEPS = 65535.0
HALF = 32768
TINY = 1e-23
MASK_LIMIT = 60 * 1024 * 1024


def squaring_pass(values, pattern):
    row_tiles, col_tiles = pattern.shape
    shaped = values.reshape(row_tiles, EDGE, col_tiles, EDGE)
    return (shaped * pattern[:, None, :, None].astype(values.dtype)).reshape(values.shape)


def berths(tile_count, bands):
    return max(2, (tile_count + bands - 1) // bands)


def body_any(a, b, a_support, b_support, retained, target_bands):
    a_whole = lax.all_gather(squaring_pass(a, a_support), "col", axis=1, tiled=True)
    b_whole = lax.all_gather(squaring_pass(b, b_support), "row", axis=0, tiled=True)
    product = jnp.dot(a_whole, b_whole, preferred_element_type=jnp.float32)
    inflated = squaring_pass(product * product, retained)
    totals = lax.psum(jnp.sum(inflated, axis=0), "row")
    bands = lax.axis_size("row")
    all_rows = inflated.shape[0] * bands
    result = (inflated / (totals / all_rows + 1e-05)).astype(jnp.bfloat16)
    tile_rows, tile_cols = retained.shape
    tile_count = tile_rows * tile_cols
    limit = berths(tile_count, bands)
    stack = result.reshape(tile_rows, EDGE, tile_cols, EDGE).transpose(0, 2, 1, 3)
    stack = stack.reshape(tile_count, EDGE * EDGE)
    targets = target_bands.reshape(tile_count)
    same_target = targets[:, None] == targets[None, :]
    earlier = jnp.arange(tile_count)[None, :] < jnp.arange(tile_count)[:, None]
    rank = jnp.sum((same_target & earlier).astype(jnp.int32), axis=1)
    position = targets * limit + rank
    selector = (jnp.arange(bands * limit)[:, None] == position[None, :]).astype(jnp.bfloat16)
    outgoing = jnp.dot(selector, stack, preferred_element_type=jnp.float32).astype(jnp.bfloat16)
    outgoing = outgoing.reshape(bands, limit, EDGE, EDGE)
    delivered = lax.all_to_all(outgoing, "row", split_axis=0, concat_axis=0, tiled=True)
    return result, delivered.reshape(bands * limit * EDGE, EDGE)


def mask_kernel(a_support, b_support, a, b, a_out, b_out, a_keep, b_keep, a_local, b_local, sems):
    rows, tiles, cols = a.shape[0] // EDGE, b.shape[0] // EDGE, b.shape[1] // EDGE
    copies = [
        pltpu.make_async_copy(source, local, sems.at[k])
        for k, (source, local) in enumerate(((a_support, a_keep), (b_support, b_keep), (a, a_local), (b, b_local)))
    ]
    for copy in copies:
        copy.start()
    copies[0].wait()
    copies[2].wait()
    for r in range(rows):
        band = slice(r * EDGE, (r + 1) * EDGE)
        a_out[band, :] = a_local[band, :] * a_keep[0, r].astype(jnp.float32).astype(a.dtype)
    copies[1].wait()
    copies[3].wait()
    for q in range(tiles):
        band = slice(q * EDGE, (q + 1) * EDGE)
        for c in range(cols):
            lanes = slice(c * EDGE, (c + 1) * EDGE)
            b_out[band, lanes] = b_local[band, lanes] * b_keep[c, q].astype(jnp.float32).astype(b.dtype)


def gather_product_kernel(where, retained, targets, b_own, b_other, *refs):
    *pieces, product, b_last, ints, b_scratch = refs
    tiles = b_own.shape[0] // EDGE
    cols = b_own.shape[1] // EDGE
    rows = product.shape[0] // EDGE
    n = len(pieces)
    i, j = where[0], where[1]
    ints[0] = i
    for r in range(rows):
        for c in range(cols):
            ints[1 + r * cols + c] = retained[r, c]
            ints[1 + rows * cols + r * cols + c] = targets[0, r * cols + c]
    for half, b in ((i, b_own), (1 - i, b_other)):
        for q in range(tiles):
            m = lax.bitwise_xor(j, half * tiles + q)
            b_scratch[m] = b[q * EDGE:(q + 1) * EDGE, :]
    b = b_scratch[:n].reshape(n * EDGE, -1)
    a = jnp.concatenate([p[...] for p in pieces], axis=1)
    product[...] = jnp.dot(a, b, preferred_element_type=jnp.float32)
    b_last[...] = b_scratch[n:].reshape(b_last.shape)


def inflate_kernel(ints, part, b_last, even, odd, product, stats, codes):
    rows, cols = part.shape[0] // EDGE, part.shape[1] // EDGE
    count = rows * cols
    a = jnp.concatenate([even[...], odd[...]], axis=1)
    whole = part[...] + jnp.dot(a, b_last[...], preferred_element_type=jnp.float32)
    tops = []
    for c in range(cols):
        lanes = pl.ds(c * EDGE, EDGE)
        total = top = None
        for r in range(rows):
            keep = ints[1 + r * cols + c].astype(jnp.float32)
            tile = jnp.abs(whole[r * EDGE:(r + 1) * EDGE, c * EDGE:(c + 1) * EDGE]) * keep
            product[pl.ds(r * EDGE, EDGE), lanes] = tile
            stacked = tile.reshape(EDGE // 8, 8, EDGE)
            sums, peak = jnp.sum(stacked * stacked, axis=0), jnp.max(stacked, axis=0)
            total = sums if r == 0 else total + sums
            top = peak if r == 0 else jnp.maximum(top, peak)
        stats[pl.ds(0, 8), lanes] = total
        stats[pl.ds(8, 8), lanes] = top
        top = jnp.max(top, axis=0, keepdims=True)
        tops.append(jnp.where(top > TINY, STEPS / jnp.maximum(top, TINY), 0.0))
    if codes.shape[0] * 2 != count:
        codes[...] = jnp.full_like(codes, -HALF)
        stats[pl.ds(16, stats.shape[0] - 16), :] = jnp.zeros((stats.shape[0] - 16, cols * EDGE), jnp.float32)
    column = lax.broadcasted_iota(jnp.int32, (1, cols * EDGE), 1) // EDGE
    sent = jnp.int32(0)
    for t in range(count):
        r, c = t // cols, t % cols
        leaves = ints[1 + count + t] != ints[0]

        @pl.when(leaves)
        def _():
            tile = product[pl.ds(r * EDGE, EDGE), pl.ds(c * EDGE, EDGE)]
            steps = (tile * tops[c] + 0.5).astype(jnp.int32) - HALF
            codes[sent] = steps.astype(codes.dtype)
            stats[pl.ds(16 + sent, 1), :] = (column == c).astype(jnp.float32)

        sent = sent + leaves.astype(jnp.int32)


def finish_kernel(all_rows, limit, ints, product, own, other, result, placed, step, scale):
    rows, cols = product.shape[0] // EDGE, product.shape[1] // EDGE
    i = ints[0]
    total = jnp.sum(own[0:8, :] + other[0:8, :], axis=0, keepdims=True)
    inverse = 1.0 / (total / all_rows + 1e-05)
    top = jnp.max(other[8:16, :], axis=0, keepdims=True) / STEPS
    for s in range(limit):
        chosen = other[16 + s:17 + s, :]
        step[s] = sum((chosen * top)[:, c * EDGE:(c + 1) * EDGE] for c in range(cols))
        scale[s] = sum((chosen * inverse)[:, c * EDGE:(c + 1) * EDGE] for c in range(cols))
    if 2 * limit != rows * cols:
        placed[...] = jnp.zeros_like(placed)
    kept = jnp.int32(0)
    for t in range(rows * cols):
        r, c = t // cols, t % cols
        lanes = slice(c * EDGE, (c + 1) * EDGE)
        tile = product[r * EDGE:(r + 1) * EDGE, lanes]
        tile = (tile * tile * inverse[:, lanes]).astype(result.dtype)
        result[r * EDGE:(r + 1) * EDGE, lanes] = tile
        stays = ints[1 + rows * cols + t] == i

        @pl.when(stays)
        def _():
            placed[i * limit + kept] = tile

        kept = kept + stays.astype(jnp.int32)


def body_pair(a, b, a_support, b_support, retained, target_bands):
    n_col = lax.axis_size("col")
    swap = [(0, 1), (1, 0)]
    i, j = lax.axis_index("row"), lax.axis_index("col")
    rows, columns = a.shape[0], b.shape[1]
    tile_count = retained.shape[0] * retained.shape[1]
    limit = berths(tile_count, 2)

    def across(values, mask):
        return lax.ppermute(values, "col", [(k, k ^ mask) for k in range(n_col)])

    whole = pl.BlockSpec(memory_space=VMEM)
    scalars = pl.BlockSpec(memory_space=SMEM)
    params = pltpu.CompilerParams(vmem_limit_bytes=LIMIT)
    a_eff, b_eff = pl.pallas_call(
        mask_kernel,
        out_shape=(pltpu.VMEM(a.shape, a.dtype), pltpu.VMEM(b.shape, b.dtype)),
        in_specs=[pl.BlockSpec(memory_space=pltpu.HBM)] * 4,
        out_specs=(whole, whole),
        scratch_shapes=[
            SMEM(a_support.T.shape, jnp.int32),
            SMEM(b_support.T.shape, jnp.int32),
            VMEM(a.shape, a.dtype),
            VMEM(b.shape, b.dtype),
            pltpu.SemaphoreType.DMA((4,)),
        ],
        compiler_params=pltpu.CompilerParams(vmem_limit_bytes=MASK_LIMIT),
        name="mask_factors",
    )(a_support.T, b_support.T, a, b)
    b_other = lax.ppermute(b_eff, "row", swap)
    pieces = {0: a_eff}
    high = n_col // 2
    for m, base in ((8, 0), (4, 0), (2, 0), (12, 8), (10, 8), (6, 2), (14, 12)):
        pieces[m] = across(pieces[base], m ^ base)
    for m in sorted(pieces):
        if m != n_col - 2:
            pieces[m | 1] = across(pieces[m], 1)

    where = jnp.stack([i, j]).astype(jnp.int32)
    targets = target_bands.reshape(1, tile_count)
    first = n_col - 2
    part, b_last, ints = pl.pallas_call(
        gather_product_kernel,
        out_shape=(
            jax.ShapeDtypeStruct((rows, columns), jnp.float32),
            jax.ShapeDtypeStruct((2 * EDGE, columns), b.dtype),
            jax.ShapeDtypeStruct((1 + 2 * tile_count,), jnp.int32),
        ),
        in_specs=[scalars] * 3 + [whole] * (2 + first),
        out_specs=(whole, whole, scalars),
        scratch_shapes=[
            VMEM((n_col, EDGE, columns), b.dtype),
        ],
        compiler_params=params,
        cost_estimate=pl.CostEstimate(
            flops=2 * rows * columns * n_col * EDGE, bytes_accessed=8 * 1024 * 1024, transcendentals=0
        ),
        name="gather_product",
    )(where, retained, targets, b_eff, b_other, *[pieces[m] for m in range(first)])
    even, part = lax.optimization_barrier((pieces[first], part))
    odd = across(even, 1)

    product, stats, codes = pl.pallas_call(
        inflate_kernel,
        out_shape=(
            jax.ShapeDtypeStruct((rows, columns), jnp.float32),
            jax.ShapeDtypeStruct((16 + (limit + 7) // 8 * 8, columns), jnp.float32),
            jax.ShapeDtypeStruct((limit, EDGE, EDGE), jnp.int16),
        ),
        in_specs=[scalars] + [whole] * 4,
        out_specs=(whole, whole, whole),
        compiler_params=params,
        name="inflate",
    )(ints, part, b_last, even, odd)

    other_stats = lax.ppermute(stats, "row", swap)
    arrived = lax.ppermute(codes, "row", swap)
    result, placed, step, scale = pl.pallas_call(
        functools.partial(finish_kernel, 2 * rows, limit),
        out_shape=(
            jax.ShapeDtypeStruct((rows, columns), jnp.bfloat16),
            jax.ShapeDtypeStruct((2 * limit, EDGE, EDGE), jnp.bfloat16),
            jax.ShapeDtypeStruct((limit, 1, EDGE), jnp.float32),
            jax.ShapeDtypeStruct((limit, 1, EDGE), jnp.float32),
        ),
        in_specs=[scalars] + [whole] * 3,
        out_specs=(whole,) * 4,
        compiler_params=params,
        name="finish",
    )(ints, product, stats, other_stats)
    values = (arrived.astype(jnp.float32) + HALF) * step
    values = (values * values * scale).astype(jnp.bfloat16)
    placed = lax.dynamic_update_slice(placed, values, ((1 - i) * limit, 0, 0))
    return result, placed.reshape(2 * limit * EDGE, EDGE)


def solution(mesh):
    n_row, n_col = mesh.shape["row"], mesh.shape["col"]
    paired = n_row == 2 and n_col >= 16 and n_col & (n_col - 1) == 0
    placed = (P("row", "col"),) * 5 + (P("row", "col", None, None),)
    return jax.shard_map(
        body_pair if paired else body_any,
        mesh=mesh,
        in_specs=placed,
        out_specs=(P("row", "col"), P("row", "col")),
        check_vma=False,
    )
```

time: 43.4 us -> 39.2 us (0.903)
  local copies, waits for them, and re-layouts: 3.46 us -> 0.59 us
  other arithmetic: 2.48 us -> 0.87 us
  Pallas kernels: 4.71 us -> 6.29 us
  waiting for transfers between devices: 15.2 us -> 14.1 us
    ppermute x2 -> x1, waiting for transfers between devices: 3.04 us -> 0.01 us  [body_pair(): b_other = lax.ppermute(b_eff, 'row', swap)]
    unnamed x10 -> x5, local copies, waits for them, and re-layouts: 3.15 us -> 0.59 us
    ppermute x15, waiting for transfers between devices: 7.78 us -> 9.99 us  [across(): return lax.ppermute(values, 'col', [(k, k ^ mask) for k in range(n_col)])]
    pallas_call x2 -> x3, Pallas kernels: 2.65 us -> 4.03 us  [the longest x1 1.57 us: body_pair(): pl.pallas_call(functools.partial(finish_kernel, 2 * rows, limit), out_sha...]
    mul x1 -> x0, other arithmetic: 1.03 us -> none  [squaring_pass(): shaped * pattern[:, None, :, None].astype(values.dtype)]
    ppermute x1, waiting for transfers between devices: 2.64 us -> 1.85 us  [body_pair(): arrived = lax.ppermute(codes, 'row', swap)]
    convert_element_type x1 -> x0, other arithmetic: 0.66 us -> none  [squaring_pass(): pattern[:, None, :, None].astype(values.dtype)]
    ppermute x1, starting transfers between devices: 1.1 us -> 0.5 us  [body_pair(): other_stats = lax.ppermute(stats, 'row', swap)]
  transfers between devices with their start and end apart: 19 -> 18, of which waited for: 6 -> 8; matrix products, arithmetic and copies ran while one was open for 5% -> 0% of each run, Pallas kernels for 8% -> 10%
where the time goes in v3:
time: 39.2 us; the launch traced here: 39.1 us
  starting transfers between devices  16.5 us (42%)
  waiting for transfers between devices  14.1 us (36%)
  Pallas kernels  6.29 us (16%)
  other arithmetic  0.87 us (2%)
  between operations  0.68 us (2%)
  local copies, waits for them, and re-layouts  0.59 us (2%)
    ppermute x15, starting transfers between devices, across(): return lax.ppermute(values, 'col', [(k, k ^ mask) for k in range(n_col)])  11.4 us
    ppermute x15, waiting for transfers between devices, across(): return lax.ppermute(values, 'col', [(k, k ^ mask) for k in range(n_col)])  9.99 us
    ppermute x1, starting transfers between devices, body_pair(): b_other = lax.ppermute(b_eff, 'row', swap)  3.03 us
    ppermute x1, waiting for transfers between devices, body_pair(): other_stats = lax.ppermute(stats, 'row', swap)  2.29 us
    pallas_call x1, Pallas kernels, body_pair(): pl.pallas_call(gather_product_kernel, out_shape=(jax.ShapeDtypeStruct((ro...  2.25 us
    ppermute x1, waiting for transfers between devices, body_pair(): arrived = lax.ppermute(codes, 'row', swap)  1.85 us
    ppermute x1, starting transfers between devices, body_pair(): arrived = lax.ppermute(codes, 'row', swap)  1.59 us
    pallas_call x1, Pallas kernels, body_pair(): pl.pallas_call(functools.partial(finish_kernel, 2 * rows, limit), out_sha...  1.57 us
  transfers between devices with their start and end apart: 18, of which 8 were waited for; matrix products, arithmetic and copies ran while one was open for 0% of the time, Pallas kernels for 10%

profile of v3, /device:TPU:0, one launch (start us, length us, event | category | flops | bytes accessed | tf_op | source)
XLA Modules:
  0.0 39.1 jit_solution(4116853656843250541)
XLA Ops:
  0.6 1.4 %mask_factors.1 = (bf16[512,128]{1,0:T(8,128)(2,1)S(1)}, bf16[1024,384]{1,0:T(8,128)(2,1)S(1)}) custom-call(s32[1,4]{1,0:T(1,128)} %bitcast.12, s32[3,8]{1,0:T(4,128)} %bitcast.11, bf16[512,128]{1,0:T(8,128)(2,1)} %a.1, bf16[1024,384]{1,0:T(8,128)(2,1)} %b.1), custom_call_target="tpu_custom_call" | custom-call | tf_op jit(solution)/shard_map/mask_factors/pallas_call | solution.py:182
  2.0 3.0 %collective-permute-start = (bf16[1024,384]{1,0:T(8,128)(2,1)S(1)}, bf16[1024,384]{1,0:T(8,128)(2,1)S(1)}, u32[]{:S(2)}, u32[]{:S(2)}) collective-permute-start(bf16[1024,384]{1,0:T(8,128)(2,1)S(1)} %get-tuple-element.16.b_own), channel_id=1, source_target_pairs={{0,16},{16,0},{1,17},{17,1},{2,18},{18,2},{3,19},{19,3},{4,20},{20... | collective-permute-start | bytes 2359304 | tf_op jit(solution)/shard_map/ppermute | solution.py:197
  5.1 2.6 %collective-permute-start.8 = (bf16[512,128]{1,0:T(8,128)(2,1)S(1)}, bf16[512,128]{1,0:T(8,128)(2,1)S(1)}, u32[]{:S(2)}, u32[]{:S(2)}) collective-permute-start(bf16[512,128]{1,0:T(8,128)(2,1)S(1)} %get-tuple-element.17.refs_0_), channel_id=1, source_target_pairs={{0,8},{1,9},{2,10},{3,11},{4,12},{5,13},{6,14},{7,15},{8,0},{9,1},... | collective-permute-start | bytes 393224 | tf_op jit(solution)/shard_map/ppermute | solution.py:177
  7.7 1.5 %collective-permute-start.2 = (bf16[512,128]{1,0:T(8,128)(2,1)S(1)}, bf16[512,128]{1,0:T(8,128)(2,1)S(1)}, u32[]{:S(2)}, u32[]{:S(2)}) collective-permute-start(bf16[512,128]{1,0:T(8,128)(2,1)S(1)} %get-tuple-element.17.refs_0_), channel_id=1, source_target_pairs={{0,2},{1,3},{2,0},{3,1},{4,6},{5,7},{6,4},{7,5},{8,10},{9,11},{10,... | collective-permute-start | bytes 393224 | tf_op jit(solution)/shard_map/ppermute | solution.py:177
  9.2 1.6 %collective-permute-start.4 = (bf16[512,128]{1,0:T(8,128)(2,1)S(1)}, bf16[512,128]{1,0:T(8,128)(2,1)S(1)}, u32[]{:S(2)}, u32[]{:S(2)}) collective-permute-start(bf16[512,128]{1,0:T(8,128)(2,1)S(1)} %get-tuple-element.17.refs_0_), channel_id=1, source_target_pairs={{0,4},{1,5},{2,6},{3,7},{4,0},{5,1},{6,2},{7,3},{8,12},{9,13},{10,... | collective-permute-start | bytes 393224 | tf_op jit(solution)/shard_map/ppermute | solution.py:177
  10.7 0.0 collective-permute-start.1
  10.7 3.1 %collective-permute-done.8.refs_8_ = bf16[512,128]{1,0:T(8,128)(2,1)S(1)} collective-permute-done((bf16[512,128]{1,0:T(8,128)(2,1)S(1)}, bf16[512,128]{1,0:T(8,128)(2,1)S(1)}, u32[]{:S(2)}, u32[]{:S(2)}) %collective-permute-start.8) | collective-permute-done | bytes 131104 | tf_op jit(solution)/shard_map/ppermute | solution.py:177
  13.8 0.6 %collective-permute-start.12 = (bf16[512,128]{1,0:T(8,128)(2,1)S(1)}, bf16[512,128]{1,0:T(8,128)(2,1)S(1)}, u32[]{:S(2)}, u32[]{:S(2)}) collective-permute-start(bf16[512,128]{1,0:T(8,128)(2,1)S(1)} %collective-permute-done.8.refs_8_), channel_id=1, source_target_pairs={{0,4},{1,5},{2,6},{3,7},{4,0},{5,1},{6,2},{7,3},{8,12},{9,13},{10,... | collective-permute-start | bytes 393224 | tf_op jit(solution)/shard_map/ppermute | solution.py:177
  14.5 0.0 collective-permute-done.2.refs_2_
  14.5 1.4 %collective-permute-start.10 = (bf16[512,128]{1,0:T(8,128)(2,1)S(1)}, bf16[512,128]{1,0:T(8,128)(2,1)S(1)}, u32[]{:S(2)}, u32[]{:S(2)}) collective-permute-start(bf16[512,128]{1,0:T(8,128)(2,1)S(1)} %collective-permute-done.8.refs_8_), channel_id=1, source_target_pairs={{0,2},{1,3},{2,0},{3,1},{4,6},{5,7},{6,4},{7,5},{8,10},{9,11},{10,... | collective-permute-start | bytes 393224 | tf_op jit(solution)/shard_map/ppermute | solution.py:177
  15.9 0.0 collective-permute-done.4.refs_4_
  15.9 1.5 %collective-permute-start.6 = (bf16[512,128]{1,0:T(8,128)(2,1)S(1)}, bf16[512,128]{1,0:T(8,128)(2,1)S(1)}, u32[]{:S(2)}, u32[]{:S(2)}) collective-permute-start(bf16[512,128]{1,0:T(8,128)(2,1)S(1)} %collective-permute-done.2.refs_2_), channel_id=1, source_target_pairs={{0,4},{1,5},{2,6},{3,7},{4,0},{5,1},{6,2},{7,3},{8,12},{9,13},{10,... | collective-permute-start | bytes 393224 | tf_op jit(solution)/shard_map/ppermute | solution.py:177
  17.4 0.0 collective-permute-done.1.refs_1_
  17.4 0.0 collective-permute-start.9
  17.4 2.4 %collective-permute-done.12.refs_12_ = bf16[512,128]{1,0:T(8,128)(2,1)S(1)} collective-permute-done((bf16[512,128]{1,0:T(8,128)(2,1)S(1)}, bf16[512,128]{1,0:T(8,128)(2,1)S(1)}, u32[]{:S(2)}, u32[]{:S(2)}) %collective-permute-start.12) | collective-permute-done | bytes 131104 | tf_op jit(solution)/shard_map/ppermute | solution.py:177
  19.7 0.0 collective-permute-start.3
  19.7 0.0 collective-permute-done.10.refs_10_
  19.7 0.5 %collective-permute-start.5 = (bf16[512,128]{1,0:T(8,128)(2,1)S(1)}, bf16[512,128]{1,0:T(8,128)(2,1)S(1)}, u32[]{:S(2)}, u32[]{:S(2)}) collective-permute-start(bf16[512,128]{1,0:T(8,128)(2,1)S(1)} %collective-permute-done.4.refs_4_), channel_id=1, source_target_pairs={{0,1},{1,0},{2,3},{3,2},{4,5},{5,4},{6,7},{7,6},{8,9},{9,8},{10,11... | collective-permute-start | bytes 393224 | tf_op jit(solution)/shard_map/ppermute | solution.py:177
  20.2 1.4 %collective-permute-done.6.refs_6_ = bf16[512,128]{1,0:T(8,128)(2,1)S(1)} collective-permute-done((bf16[512,128]{1,0:T(8,128)(2,1)S(1)}, bf16[512,128]{1,0:T(8,128)(2,1)S(1)}, u32[]{:S(2)}, u32[]{:S(2)}) %collective-permute-start.6) | collective-permute-done | bytes 131104 | tf_op jit(solution)/shard_map/ppermute | solution.py:177
  21.6 0.0 collective-permute-start.13
  21.6 0.0 collective-permute-done.9.refs_9_
  21.6 0.5 %collective-permute-start.11 = (bf16[512,128]{1,0:T(8,128)(2,1)S(1)}, bf16[512,128]{1,0:T(8,128)(2,1)S(1)}, u32[]{:S(2)}, u32[]{:S(2)}) collective-permute-start(bf16[512,128]{1,0:T(8,128)(2,1)S(1)} %collective-permute-done.10.refs_10_), channel_id=1, source_target_pairs={{0,1},{1,0},{2,3},{3,2},{4,5},{5,4},{6,7},{7,6},{8,9},{9,8},{10,11... | collective-permute-start | bytes 393224 | tf_op jit(solution)/shard_map/ppermute | solution.py:177
  22.1 0.0 collective-permute-done.3.refs_3_
  22.1 0.1 collective-permute-start.7
  22.2 0.0 collective-permute-done.5.refs_5_
  22.2 1.1 %collective-permute-start.14 = (bf16[512,128]{1,0:T(8,128)(2,1)S(1)}, bf16[512,128]{1,0:T(8,128)(2,1)S(1)}, u32[]{:S(2)}, u32[]{:S(2)}) collective-permute-start(bf16[512,128]{1,0:T(8,128)(2,1)S(1)} %collective-permute-done.12.refs_12_), channel_id=1, source_target_pairs={{0,2},{1,3},{2,0},{3,1},{4,6},{5,7},{6,4},{7,5},{8,10},{9,11},{10,... | collective-permute-start | bytes 393224 | tf_op jit(solution)/shard_map/ppermute | solution.py:177
  23.3 0.0 copy-start
  23.3 0.1 pad_add_fusion.where
  23.4 0.0 copy-start.1
  23.4 0.0 collective-permute-done.13.refs_13_
  23.4 0.0 collective-permute-done.11.refs_11_
  23.4 0.1 collective-permute-done.7.refs_7_
  23.5 0.0 collective-permute-done.b_other
  23.5 0.5 %copy-done = s32[4,3]{1,0:T(4,128)S(1)} copy-done((s32[4,3]{1,0:T(4,128)S(1)}, s32[4,3]{1,0:T(4,128)}, u32[]{:S(2)}) %copy-start) | copy-done | bytes 72
  24.0 0.1 copy-done.1
  24.1 2.3 %gather_product.1 = (f32[512,384]{1,0:T(8,128)S(1)}, bf16[256,384]{1,0:T(8,128)(2,1)S(1)}, s32[25]{0:T(128)S(1)}) custom-call(s32[2]{0:T(128)S(1)} %pad_add_fusion.where, s32[4,3]{1,0:T(4,128)S(1)} %copy-done, s32[1,12]{1,0:T(1,128)S(1)} %bitcast.10, bf16[1024,384]{1,0:T(8,128)(2,1)S(1)} %get-tuple-element.16.b_own, ...), custom_call_target="tpu_custom_call" | custom-call | flops 805306368 | bytes 8388608 | tf_op jit(solution)/shard_map/gather_product/pallas_call | solution.py:209
  26.3 1.7 %collective-permute-done.14.even = bf16[512,128]{1,0:T(8,128)(2,1)S(1)} collective-permute-done((bf16[512,128]{1,0:T(8,128)(2,1)S(1)}, bf16[512,128]{1,0:T(8,128)(2,1)S(1)}, u32[]{:S(2)}, u32[]{:S(2)}) %collective-permute-start.14) | collective-permute-done | bytes 131104 | tf_op jit(solution)/shard_map/ppermute | solution.py:177
  28.1 0.0 collective-permute-start.15
  28.1 1.3 %collective-permute-done.15.odd = bf16[512,128]{1,0:T(8,128)(2,1)S(1)} collective-permute-done((bf16[512,128]{1,0:T(8,128)(2,1)S(1)}, bf16[512,128]{1,0:T(8,128)(2,1)S(1)}, u32[]{:S(2)}, u32[]{:S(2)}) %collective-permute-start.15) | collective-permute-done | bytes 131104 | tf_op jit(solution)/shard_map/ppermute | solution.py:177
  29.4 1.1 %inflate.1 = (f32[512,384]{1,0:T(8,128)S(1)}, f32[24,384]{1,0:T(8,128)S(1)}, s16[6,128,128]{2,1,0:T(8,128)(2,1)S(1)}) custom-call(s32[25]{0:T(128)S(1)} %get-tuple-element.18.ints, f32[512,384]{1,0:T(8,128)S(1)} %get-tuple-element.20.part, bf16[256,384]{1,0:T(8,128)(2,1)S(1)} %get-tuple-element.21.b_last, bf16[512,128]{1,0:T(8,128)(2,1)S(1)} %collective-permute-done.14.even, ...), custom_call_target="tpu_custom_call" | custom-call | tf_op jit(solution)/shard_map/inflate/pallas_call | solution.py:230
  30.5 0.5 %collective-permute-start.16 = (f32[24,384]{1,0:T(8,128)S(1)}, f32[24,384]{1,0:T(8,128)S(1)}, u32[]{:S(2)}, u32[]{:S(2)}) collective-permute-start(f32[24,384]{1,0:T(8,128)S(1)} %get-tuple-element.24.own), channel_id=1, source_target_pairs={{0,16},{16,0},{1,17},{17,1},{2,18},{18,2},{3,19},{19,3},{4,20},{20... | collective-permute-start | bytes 110600 | tf_op jit(solution)/shard_map/ppermute | solution.py:243
  31.0 1.6 %collective-permute-start.17 = (s16[6,128,128]{2,1,0:T(8,128)(2,1)S(1)}, s16[6,128,128]{2,1,0:T(8,128)(2,1)S(1)}, u32[]{:S(2)}, u32[]{:S(2)}) collective-permute-start(s16[6,128,128]{2,1,0:T(8,128)(2,1)S(1)} %get-tuple-element.27), channel_id=1, source_target_pairs={{0,16},{16,0},{1,17},{17,1},{2,18},{18,2},{3,19},{19,3},{4,20},{20... | collective-permute-start | bytes 589832 | tf_op jit(solution)/shard_map/ppermute | solution.py:244
  32.6 2.3 %collective-permute-done.16.other = f32[24,384]{1,0:T(8,128)S(1)} collective-permute-done((f32[24,384]{1,0:T(8,128)S(1)}, f32[24,384]{1,0:T(8,128)S(1)}, u32[]{:S(2)}, u32[]{:S(2)}) %collective-permute-start.16) | collective-permute-done | bytes 36896 | tf_op jit(solution)/shard_map/ppermute | solution.py:243
  34.9 1.6 %finish.1 = (bf16[512,384]{1,0:T(8,128)(2,1)}, bf16[12,128,128]{2,1,0:T(8,128)(2,1)}, f32[6,1,128]{2,1,0:T(1,128)S(1)}, f32[6,1,128]{2,1,0:T(1,128)S(1)}) custom-call(s32[25]{0:T(128)S(1)} %get-tuple-element.18.ints, f32[512,384]{1,0:T(8,128)S(1)} %get-tuple-element.23.product, f32[24,384]{1,0:T(8,128)S(1)} %get-tuple-element.24.own, ...), custom_call_target="tpu_custom_call" | custom-call | tf_op jit(solution)/shard_map/finish/pallas_call | solution.py:245
  36.4 1.8 %collective-permute-done.17 = s16[6,128,128]{2,1,0:T(8,128)(2,1)S(1)} collective-permute-done((s16[6,128,128]{2,1,0:T(8,128)(2,1)S(1)}, s16[6,128,128]{2,1,0:T(8,128)(2,1)S(1)}, u32[]{:S(2)}, u32[]{:S(2)}) %collective-permute-start.17) | collective-permute-done | bytes 196640 | tf_op jit(solution)/shard_map/ppermute | solution.py:244
  38.3 0.8 %fusion = bf16[12,128,128]{2,1,0:T(8,128)(2,1)} fusion(bf16[12,128,128]{2,1,0:T(8,128)(2,1)} %get-tuple-element.26, s32[]{:T(128)S(6)} %select_n.3, s16[6,128,128]{2,1,0:T(8,128)(2,1)S(1)} %collective-permute-done.17, f32[6,128]{1,0:T(8,128)S(1)} %get-tuple-element.30, f32[6,128]{1,0:T(8,128)S(1)} %get-tuple-element.31), kind=kLoop, calls=%fused_computation.1 | loop fusion | flops 589824 | bytes 399364 | tf_op jit(solution)/shard_map/dynamic_update_slice | solution.py:260
  (1 shorter events, 0.0 us)
Async XLA Ops:
  2.0 21.5 %collective-permute-start = (bf16[1024,384]{1,0:T(8,128)(2,1)S(1)}, bf16[1024,384]{1,0:T(8,128)(2,1)S(1)}, u32[]{:S(2)}, u32[]{:S(2)}) collective-permute-start(bf16[1024,384]{1,0:T(8,128)(2,1)S(1)} %get-tuple-element.16.b_own), channel_id=1, source_target_pairs={{0,16},{16,0},{1,17},{17,1},{2,18},{18,2},{3,19},{19,3},{4,20},{20... | collective-permute-start | bytes 2359304 | tf_op jit(solution)/shard_map/ppermute | solution.py:197
  5.1 8.8 %collective-permute-start.8 = (bf16[512,128]{1,0:T(8,128)(2,1)S(1)}, bf16[512,128]{1,0:T(8,128)(2,1)S(1)}, u32[]{:S(2)}, u32[]{:S(2)}) collective-permute-start(bf16[512,128]{1,0:T(8,128)(2,1)S(1)} %get-tuple-element.17.refs_0_), channel_id=1, source_target_pairs={{0,8},{1,9},{2,10},{3,11},{4,12},{5,13},{6,14},{7,15},{8,0},{9,1},... | collective-permute-start | bytes 393224 | tf_op jit(solution)/shard_map/ppermute | solution.py:177
  7.7 6.8 %collective-permute-start.2 = (bf16[512,128]{1,0:T(8,128)(2,1)S(1)}, bf16[512,128]{1,0:T(8,128)(2,1)S(1)}, u32[]{:S(2)}, u32[]{:S(2)}) collective-permute-start(bf16[512,128]{1,0:T(8,128)(2,1)S(1)} %get-tuple-element.17.refs_0_), channel_id=1, source_target_pairs={{0,2},{1,3},{2,0},{3,1},{4,6},{5,7},{6,4},{7,5},{8,10},{9,11},{10,... | collective-permute-start | bytes 393224 | tf_op jit(solution)/shard_map/ppermute | solution.py:177
  9.2 6.8 %collective-permute-start.4 = (bf16[512,128]{1,0:T(8,128)(2,1)S(1)}, bf16[512,128]{1,0:T(8,128)(2,1)S(1)}, u32[]{:S(2)}, u32[]{:S(2)}) collective-permute-start(bf16[512,128]{1,0:T(8,128)(2,1)S(1)} %get-tuple-element.17.refs_0_), channel_id=1, source_target_pairs={{0,4},{1,5},{2,6},{3,7},{4,0},{5,1},{6,2},{7,3},{8,12},{9,13},{10,... | collective-permute-start | bytes 393224 | tf_op jit(solution)/shard_map/ppermute | solution.py:177
  10.7 6.6 %collective-permute-start.1 = (bf16[512,128]{1,0:T(8,128)(2,1)S(1)}, bf16[512,128]{1,0:T(8,128)(2,1)S(1)}, u32[]{:S(2)}, u32[]{:S(2)}) collective-permute-start(bf16[512,128]{1,0:T(8,128)(2,1)S(1)} %get-tuple-element.17.refs_0_), channel_id=1, source_target_pairs={{0,1},{1,0},{2,3},{3,2},{4,5},{5,4},{6,7},{7,6},{8,9},{9,8},{10,11... | collective-permute-start | bytes 393224 | tf_op jit(solution)/shard_map/ppermute | solution.py:177
  13.8 5.9 %collective-permute-start.12 = (bf16[512,128]{1,0:T(8,128)(2,1)S(1)}, bf16[512,128]{1,0:T(8,128)(2,1)S(1)}, u32[]{:S(2)}, u32[]{:S(2)}) collective-permute-start(bf16[512,128]{1,0:T(8,128)(2,1)S(1)} %collective-permute-done.8.refs_8_), channel_id=1, source_target_pairs={{0,4},{1,5},{2,6},{3,7},{4,0},{5,1},{6,2},{7,3},{8,12},{9,13},{10,... | collective-permute-start | bytes 393224 | tf_op jit(solution)/shard_map/ppermute | solution.py:177
  14.5 5.3 %collective-permute-start.10 = (bf16[512,128]{1,0:T(8,128)(2,1)S(1)}, bf16[512,128]{1,0:T(8,128)(2,1)S(1)}, u32[]{:S(2)}, u32[]{:S(2)}) collective-permute-start(bf16[512,128]{1,0:T(8,128)(2,1)S(1)} %collective-permute-done.8.refs_8_), channel_id=1, source_target_pairs={{0,2},{1,3},{2,0},{3,1},{4,6},{5,7},{6,4},{7,5},{8,10},{9,11},{10,... | collective-permute-start | bytes 393224 | tf_op jit(solution)/shard_map/ppermute | solution.py:177
  15.9 5.7 %collective-permute-start.6 = (bf16[512,128]{1,0:T(8,128)(2,1)S(1)}, bf16[512,128]{1,0:T(8,128)(2,1)S(1)}, u32[]{:S(2)}, u32[]{:S(2)}) collective-permute-start(bf16[512,128]{1,0:T(8,128)(2,1)S(1)} %collective-permute-done.2.refs_2_), channel_id=1, source_target_pairs={{0,4},{1,5},{2,6},{3,7},{4,0},{5,1},{6,2},{7,3},{8,12},{9,13},{10,... | collective-permute-start | bytes 393224 | tf_op jit(solution)/shard_map/ppermute | solution.py:177
  17.4 4.3 %collective-permute-start.9 = (bf16[512,128]{1,0:T(8,128)(2,1)S(1)}, bf16[512,128]{1,0:T(8,128)(2,1)S(1)}, u32[]{:S(2)}, u32[]{:S(2)}) collective-permute-start(bf16[512,128]{1,0:T(8,128)(2,1)S(1)} %collective-permute-done.8.refs_8_), channel_id=1, source_target_pairs={{0,1},{1,0},{2,3},{3,2},{4,5},{5,4},{6,7},{7,6},{8,9},{9,8},{10,11... | collective-permute-start | bytes 393224 | tf_op jit(solution)/shard_map/ppermute | solution.py:177
  19.7 2.4 %collective-permute-start.3 = (bf16[512,128]{1,0:T(8,128)(2,1)S(1)}, bf16[512,128]{1,0:T(8,128)(2,1)S(1)}, u32[]{:S(2)}, u32[]{:S(2)}) collective-permute-start(bf16[512,128]{1,0:T(8,128)(2,1)S(1)} %collective-permute-done.2.refs_2_), channel_id=1, source_target_pairs={{0,1},{1,0},{2,3},{3,2},{4,5},{5,4},{6,7},{7,6},{8,9},{9,8},{10,11... | collective-permute-start | bytes 393224 | tf_op jit(solution)/shard_map/ppermute | solution.py:177
  19.7 2.5 %collective-permute-start.5 = (bf16[512,128]{1,0:T(8,128)(2,1)S(1)}, bf16[512,128]{1,0:T(8,128)(2,1)S(1)}, u32[]{:S(2)}, u32[]{:S(2)}) collective-permute-start(bf16[512,128]{1,0:T(8,128)(2,1)S(1)} %collective-permute-done.4.refs_4_), channel_id=1, source_target_pairs={{0,1},{1,0},{2,3},{3,2},{4,5},{5,4},{6,7},{7,6},{8,9},{9,8},{10,11... | collective-permute-start | bytes 393224 | tf_op jit(solution)/shard_map/ppermute | solution.py:177
  21.6 1.8 %collective-permute-start.13 = (bf16[512,128]{1,0:T(8,128)(2,1)S(1)}, bf16[512,128]{1,0:T(8,128)(2,1)S(1)}, u32[]{:S(2)}, u32[]{:S(2)}) collective-permute-start(bf16[512,128]{1,0:T(8,128)(2,1)S(1)} %collective-permute-done.12.refs_12_), channel_id=1, source_target_pairs={{0,1},{1,0},{2,3},{3,2},{4,5},{5,4},{6,7},{7,6},{8,9},{9,8},{10,11... | collective-permute-start | bytes 393224 | tf_op jit(solution)/shard_map/ppermute | solution.py:177
  21.6 1.8 %collective-permute-start.11 = (bf16[512,128]{1,0:T(8,128)(2,1)S(1)}, bf16[512,128]{1,0:T(8,128)(2,1)S(1)}, u32[]{:S(2)}, u32[]{:S(2)}) collective-permute-start(bf16[512,128]{1,0:T(8,128)(2,1)S(1)} %collective-permute-done.10.refs_10_), channel_id=1, source_target_pairs={{0,1},{1,0},{2,3},{3,2},{4,5},{5,4},{6,7},{7,6},{8,9},{9,8},{10,11... | collective-permute-start | bytes 393224 | tf_op jit(solution)/shard_map/ppermute | solution.py:177
  22.1 1.3 %collective-permute-start.7 = (bf16[512,128]{1,0:T(8,128)(2,1)S(1)}, bf16[512,128]{1,0:T(8,128)(2,1)S(1)}, u32[]{:S(2)}, u32[]{:S(2)}) collective-permute-start(bf16[512,128]{1,0:T(8,128)(2,1)S(1)} %collective-permute-done.6.refs_6_), channel_id=1, source_target_pairs={{0,1},{1,0},{2,3},{3,2},{4,5},{5,4},{6,7},{7,6},{8,9},{9,8},{10,11... | collective-permute-start | bytes 393224 | tf_op jit(solution)/shard_map/ppermute | solution.py:177
  22.2 5.8 %collective-permute-start.14 = (bf16[512,128]{1,0:T(8,128)(2,1)S(1)}, bf16[512,128]{1,0:T(8,128)(2,1)S(1)}, u32[]{:S(2)}, u32[]{:S(2)}) collective-permute-start(bf16[512,128]{1,0:T(8,128)(2,1)S(1)} %collective-permute-done.12.refs_12_), channel_id=1, source_target_pairs={{0,2},{1,3},{2,0},{3,1},{4,6},{5,7},{6,4},{7,5},{8,10},{9,11},{10,... | collective-permute-start | bytes 393224 | tf_op jit(solution)/shard_map/ppermute | solution.py:177
  23.3 0.7 %copy-start = (s32[4,3]{1,0:T(4,128)S(1)}, s32[4,3]{1,0:T(4,128)}, u32[]{:S(2)}) copy-start(s32[4,3]{1,0:T(4,128)} %retained.1) | copy-start | bytes 148
  23.4 0.7 %copy-start.1 = (s32[1,1,12,1]{2,3,1,0:T(1,128)S(1)}, s32[1,1,12,1]{2,3,1,0:T(1,128)}, u32[]{:S(2)}) copy-start(s32[1,1,12,1]{2,3,1,0:T(1,128)} %param.11) | copy-start | bytes 148
  28.1 1.3 %collective-permute-start.15 = (bf16[512,128]{1,0:T(8,128)(2,1)S(1)}, bf16[512,128]{1,0:T(8,128)(2,1)S(1)}, u32[]{:S(2)}, u32[]{:S(2)}) collective-permute-start(bf16[512,128]{1,0:T(8,128)(2,1)S(1)} %collective-permute-done.14.even), channel_id=1, source_target_pairs={{0,1},{1,0},{2,3},{3,2},{4,5},{5,4},{6,7},{7,6},{8,9},{9,8},{10,11... | collective-permute-start | bytes 393224 | tf_op jit(solution)/shard_map/ppermute | solution.py:177
  30.5 4.4 %collective-permute-start.16 = (f32[24,384]{1,0:T(8,128)S(1)}, f32[24,384]{1,0:T(8,128)S(1)}, u32[]{:S(2)}, u32[]{:S(2)}) collective-permute-start(f32[24,384]{1,0:T(8,128)S(1)} %get-tuple-element.24.own), channel_id=1, source_target_pairs={{0,16},{16,0},{1,17},{17,1},{2,18},{18,2},{3,19},{19,3},{4,20},{20... | collective-permute-start | bytes 110600 | tf_op jit(solution)/shard_map/ppermute | solution.py:243
  31.0 7.3 %collective-permute-start.17 = (s16[6,128,128]{2,1,0:T(8,128)(2,1)S(1)}, s16[6,128,128]{2,1,0:T(8,128)(2,1)S(1)}, u32[]{:S(2)}, u32[]{:S(2)}) collective-permute-start(s16[6,128,128]{2,1,0:T(8,128)(2,1)S(1)} %get-tuple-element.27), channel_id=1, source_target_pairs={{0,16},{16,0},{1,17},{17,1},{2,18},{18,2},{3,19},{19,3},{4,20},{20... | collective-permute-start | bytes 589832 | tf_op jit(solution)/shard_map/ppermute | solution.py:244

commit v4 on v3

v4 whole, which is shorter than its diff:
```python
import functools

import jax
import jax.numpy as jnp
from jax import lax
from jax.experimental import pallas as pl
from jax.experimental.pallas import tpu as pltpu
from jax.sharding import PartitionSpec as P

EDGE = 128
VMEM = pltpu.VMEM
SMEM = pltpu.SMEM
LIMIT = 48 * 1024 * 1024
STEPS = 65535.0
HALF = 32768
TINY = 1e-23
TIGHT = 60 * 1024 * 1024


def squaring_pass(values, pattern):
    row_tiles, col_tiles = pattern.shape
    shaped = values.reshape(row_tiles, EDGE, col_tiles, EDGE)
    return (shaped * pattern[:, None, :, None].astype(values.dtype)).reshape(values.shape)


def berths(tile_count, bands):
    return max(2, (tile_count + bands - 1) // bands)


def body_any(a, b, a_support, b_support, retained, target_bands):
    a_whole = lax.all_gather(squaring_pass(a, a_support), "col", axis=1, tiled=True)
    b_whole = lax.all_gather(squaring_pass(b, b_support), "row", axis=0, tiled=True)
    product = jnp.dot(a_whole, b_whole, preferred_element_type=jnp.float32)
    inflated = squaring_pass(product * product, retained)
    totals = lax.psum(jnp.sum(inflated, axis=0), "row")
    bands = lax.axis_size("row")
    all_rows = inflated.shape[0] * bands
    result = (inflated / (totals / all_rows + 1e-05)).astype(jnp.bfloat16)
    tile_rows, tile_cols = retained.shape
    tile_count = tile_rows * tile_cols
    limit = berths(tile_count, bands)
    stack = result.reshape(tile_rows, EDGE, tile_cols, EDGE).transpose(0, 2, 1, 3)
    stack = stack.reshape(tile_count, EDGE * EDGE)
    targets = target_bands.reshape(tile_count)
    same_target = targets[:, None] == targets[None, :]
    earlier = jnp.arange(tile_count)[None, :] < jnp.arange(tile_count)[:, None]
    rank = jnp.sum((same_target & earlier).astype(jnp.int32), axis=1)
    position = targets * limit + rank
    selector = (jnp.arange(bands * limit)[:, None] == position[None, :]).astype(jnp.bfloat16)
    outgoing = jnp.dot(selector, stack, preferred_element_type=jnp.float32).astype(jnp.bfloat16)
    outgoing = outgoing.reshape(bands, limit, EDGE, EDGE)
    delivered = lax.all_to_all(outgoing, "row", split_axis=0, concat_axis=0, tiled=True)
    return result, delivered.reshape(bands * limit * EDGE, EDGE)


def mask_kernel(a_support, b_support, retained, targets, a, b, a_out, b_out, ints, keeps, a_local, b_local, sems):
    a_keep, b_keep, retained_local, targets_local = keeps
    rows, tiles, cols = a.shape[0] // EDGE, b.shape[0] // EDGE, b.shape[1] // EDGE
    copies = [
        pltpu.make_async_copy(source, local, sems.at[k])
        for k, (source, local) in enumerate(
            (
                (a_support, a_keep),
                (b_support, b_keep),
                (a, a_local),
                (b, b_local),
                (retained, retained_local),
                (targets, targets_local),
            )
        )
    ]
    for copy in copies:
        copy.start()
    j = lax.axis_index("col")
    copies[0].wait()
    copies[2].wait()
    for r in range(rows):
        band = slice(r * EDGE, (r + 1) * EDGE)
        a_out[band, :] = a_local[band, :] * a_keep[0, r].astype(jnp.float32).astype(a.dtype)
    copies[1].wait()
    copies[3].wait()
    for q in range(tiles):
        band = slice(q * EDGE, (q + 1) * EDGE)
        place = lax.bitwise_and(lax.bitwise_xor(j, q), tiles - 1)
        for c in range(cols):
            lanes = slice(c * EDGE, (c + 1) * EDGE)
            keep = b_keep[c, q].astype(jnp.float32).astype(b.dtype)
            b_out[place, :, lanes] = b_local[band, lanes] * keep
    copies[4].wait()
    copies[5].wait()
    count = rows * cols
    lane = lax.broadcasted_iota(jnp.int32, ints.shape, 1)
    row = jnp.zeros(ints.shape, jnp.int32)
    for t in range(count):
        row = jnp.where(lane == t, retained_local[t // cols, t % cols], row)
        row = jnp.where(lane == count + t, targets_local[0, t], row)
    ints[...] = row


def side_by_side(pieces, groups, rows):
    shards = {
        m: piece[k * rows:(k + 1) * rows, :] for piece, group in zip(pieces, groups) for k, m in enumerate(group)
    }
    return jnp.concatenate([shards[m] for m in sorted(shards)], axis=1)


def gather_product_kernel(groups, late, b_own, b_other, *refs):
    *pieces, product, b_late = refs
    tiles, _, columns = b_own.shape
    own_first = lax.axis_index("col") // tiles == lax.axis_index("row")
    for first, second, chosen in ((b_own, b_other, own_first), (b_other, b_own, jnp.logical_not(own_first))):

        @pl.when(chosen)
        def _():
            a = side_by_side(pieces, groups, product.shape[0])
            low, high = late[0] - tiles, late[-1] + 1 - tiles
            b = jnp.concatenate([first[...], second[:low], second[high:]], axis=0)
            product[...] = jnp.dot(a, b.reshape(a.shape[1], columns), preferred_element_type=jnp.float32)
            b_late[...] = second[low:high].reshape(b_late.shape)


def inflate_kernel(groups, ints_far, part, b_late, *refs):
    *pieces, product, stats, codes, ints, sem = refs
    lookup = pltpu.make_async_copy(ints_far, ints, sem)
    lookup.start()
    i = lax.axis_index("row")
    rows, cols = part.shape[0] // EDGE, part.shape[1] // EDGE
    count = rows * cols
    a = side_by_side(pieces, groups, part.shape[0])
    whole = part[...] + jnp.dot(a, b_late[...], preferred_element_type=jnp.float32)
    lookup.wait()
    tops = []
    for c in range(cols):
        lanes = pl.ds(c * EDGE, EDGE)
        total = top = None
        for r in range(rows):
            keep = ints[0, r * cols + c].astype(jnp.float32)
            tile = jnp.abs(whole[r * EDGE:(r + 1) * EDGE, c * EDGE:(c + 1) * EDGE]) * keep
            product[pl.ds(r * EDGE, EDGE), lanes] = tile
            stacked = tile.reshape(EDGE // 8, 8, EDGE)
            sums, peak = jnp.sum(stacked * stacked, axis=0), jnp.max(stacked, axis=0)
            total = sums if r == 0 else total + sums
            top = peak if r == 0 else jnp.maximum(top, peak)
        top = jnp.max(top, axis=0, keepdims=True)
        stats[pl.ds(0, 1), lanes] = jnp.sum(total, axis=0, keepdims=True)
        stats[pl.ds(1, 1), lanes] = top
        tops.append(jnp.where(top > TINY, STEPS / jnp.maximum(top, TINY), 0.0))
    if codes.shape[0] * 2 != count:
        codes[...] = jnp.full_like(codes, -HALF)
        stats[pl.ds(2, codes.shape[0]), :] = jnp.zeros((codes.shape[0], cols * EDGE), jnp.float32)
    column = lax.broadcasted_iota(jnp.int32, (1, cols * EDGE), 1) // EDGE
    sent = jnp.int32(0)
    for t in range(count):
        r, c = t // cols, t % cols
        leaves = ints[0, count + t] != i

        @pl.when(leaves)
        def _():
            tile = product[pl.ds(r * EDGE, EDGE), pl.ds(c * EDGE, EDGE)]
            steps = (tile * tops[c] + 0.5).astype(jnp.int32) - HALF
            codes[sent] = steps.astype(codes.dtype)
            stats[pl.ds(2 + sent, 1), :] = (column == c).astype(jnp.float32)

        sent = sent + leaves.astype(jnp.int32)


def finish_kernel(all_rows, limit, ints, product, own, other, result, placed, step, scale):
    rows, cols = product.shape[0] // EDGE, product.shape[1] // EDGE
    i = lax.axis_index("row")
    total = own[0:1, :] + other[0:1, :]
    inverse = 1.0 / (total / all_rows + 1e-05)
    top = other[1:2, :] / STEPS
    for s in range(limit):
        chosen = other[2 + s:3 + s, :]
        step[s] = sum((chosen * top)[:, c * EDGE:(c + 1) * EDGE] for c in range(cols))
        scale[s] = sum((chosen * inverse)[:, c * EDGE:(c + 1) * EDGE] for c in range(cols))
    if 2 * limit != rows * cols:
        placed[...] = jnp.zeros_like(placed)
    kept = jnp.int32(0)
    for t in range(rows * cols):
        r, c = t // cols, t % cols
        lanes = slice(c * EDGE, (c + 1) * EDGE)
        tile = product[r * EDGE:(r + 1) * EDGE, lanes]
        tile = (tile * tile * inverse[:, lanes]).astype(result.dtype)
        result[r * EDGE:(r + 1) * EDGE, lanes] = tile
        stays = ints[0, rows * cols + t] == i

        @pl.when(stays)
        def _():
            placed[i * limit + kept] = tile

        kept = kept + stays.astype(jnp.int32)


def body_pair(a, b, a_support, b_support, retained, target_bands):
    n_col = lax.axis_size("col")
    swap = [(0, 1), (1, 0)]
    i = lax.axis_index("row")
    rows, columns = a.shape[0], b.shape[1]
    tile_count = retained.shape[0] * retained.shape[1]
    limit = berths(tile_count, 2)

    def across(values, mask):
        return lax.ppermute(values, "col", [(k, k ^ mask) for k in range(n_col)])

    whole = pl.BlockSpec(memory_space=VMEM)
    scalars = pl.BlockSpec(memory_space=SMEM)
    params = pltpu.CompilerParams(vmem_limit_bytes=LIMIT)
    targets = target_bands.reshape(1, tile_count)
    a_eff, b_eff, ints = pl.pallas_call(
        mask_kernel,
        out_shape=(
            pltpu.VMEM(a.shape, a.dtype),
            pltpu.VMEM((b.shape[0] // EDGE, EDGE, columns), b.dtype),
            pltpu.VMEM((1, (2 * tile_count + EDGE - 1) // EDGE * EDGE), jnp.int32),
        ),
        in_specs=[pl.BlockSpec(memory_space=pltpu.HBM)] * 6,
        out_specs=(whole, whole, whole),
        scratch_shapes=[
            [SMEM(v.shape, jnp.int32) for v in (a_support.T, b_support.T, retained, targets)],
            VMEM(a.shape, a.dtype),
            VMEM(b.shape, b.dtype),
            pltpu.SemaphoreType.DMA((6,)),
        ],
        compiler_params=pltpu.CompilerParams(vmem_limit_bytes=TIGHT),
        name="mask_factors",
    )(a_support.T, b_support.T, retained, targets, a, b)
    b_other = lax.ppermute(b_eff, "row", swap)
    half = n_col // 2
    far = n_col - 2
    pieces = {0: a_eff}
    for m, base in ((8, 0), (14, 0), (2, 0), (4, 0), (6, 0), (10, 8), (12, 8)):
        pieces[m] = across(pieces[base], m ^ base)
    late_even = [m for m in range(half + 2, far, 2)]
    late = range(late_even[0], late_even[-1] + 2)

    def exchanged(batch):
        return [m | 1 for m in batch], across(jnp.concatenate([pieces[m] for m in batch], axis=0), 1)

    early = [([m], pieces[m]) for m in sorted(pieces) if m not in late]
    early += [exchanged(batch) for batch in ((0, 2), (4,), (6, 8), (14,))]
    last = [([m], pieces[m]) for m in late_even] + [exchanged(late_even)]
    groups, shards = zip(*early)
    part, b_late = pl.pallas_call(
        functools.partial(gather_product_kernel, groups, late),
        out_shape=(
            jax.ShapeDtypeStruct((rows, columns), jnp.float32),
            jax.ShapeDtypeStruct((len(late) * EDGE, columns), b.dtype),
        ),
        in_specs=[whole] * (2 + len(groups)),
        out_specs=(whole, whole),
        compiler_params=params,
        cost_estimate=pl.CostEstimate(
            flops=2 * rows * columns * n_col * EDGE, bytes_accessed=8 * 1024 * 1024, transcendentals=0
        ),
        name="gather_product",
    )(b_eff, b_other, *shards)

    groups, shards = zip(*last)
    product, stats, codes = pl.pallas_call(
        functools.partial(inflate_kernel, groups),
        out_shape=(
            jax.ShapeDtypeStruct((rows, columns), jnp.float32),
            jax.ShapeDtypeStruct(((limit + 9) // 8 * 8, columns), jnp.float32),
            jax.ShapeDtypeStruct((limit, EDGE, EDGE), jnp.int16),
        ),
        in_specs=[whole] * (3 + len(groups)),
        out_specs=(whole, whole, whole),
        scratch_shapes=[SMEM(ints.shape, jnp.int32), pltpu.SemaphoreType.DMA],
        compiler_params=params,
        name="inflate",
    )(ints, part, b_late, *shards)

    other_stats = lax.ppermute(stats, "row", swap)
    arrived = lax.ppermute(codes, "row", swap)
    result, placed, step, scale = pl.pallas_call(
        functools.partial(finish_kernel, 2 * rows, limit),
        out_shape=(
            jax.ShapeDtypeStruct((rows, columns), jnp.bfloat16),
            jax.ShapeDtypeStruct((2 * limit, EDGE, EDGE), jnp.bfloat16),
            jax.ShapeDtypeStruct((limit, 1, EDGE), jnp.float32),
            jax.ShapeDtypeStruct((limit, 1, EDGE), jnp.float32),
        ),
        in_specs=[scalars] + [whole] * 3,
        out_specs=(whole,) * 4,
        compiler_params=params,
        name="finish",
    )(ints, product, stats, other_stats)
    values = (arrived.astype(jnp.float32) + HALF) * step
    values = (values * values * scale).astype(jnp.bfloat16)
    placed = lax.dynamic_update_slice(placed, values, ((1 - i) * limit, 0, 0))
    return result, placed.reshape(2 * limit * EDGE, EDGE)


def solution(mesh):
    n_row, n_col = mesh.shape["row"], mesh.shape["col"]
    paired = n_row == 2 and n_col >= 16 and n_col & (n_col - 1) == 0
    placed = (P("row", "col"),) * 5 + (P("row", "col", None, None),)
    return jax.shard_map(
        body_pair if paired else body_any,
        mesh=mesh,
        in_specs=placed,
        out_specs=(P("row", "col"), P("row", "col")),
        check_vma=False,
    )
```

time: 39.2 us -> 37.1 us (0.946)
  Pallas kernels: 6.29 us -> 4.91 us
  waiting for transfers between devices: 14.1 us -> 13.2 us
  starting transfers between devices: 16.5 us -> 17.2 us
  local copies, waits for them, and re-layouts: 0.59 us -> 0.01 us
    pallas_call x2, Pallas kernels: 3.32 us -> 1.89 us  [the longest x1 0.99 us: body_pair(): pl.pallas_call(functools.partial(gather_product_kernel, groups, late), ou...]
    ppermute x15 -> x12, starting transfers between devices: 11.4 us -> 12 us  [across(): return lax.ppermute(values, 'col', [(k, k ^ mask) for k in range(n_col)])]
    unnamed x5 -> x1, local copies, waits for them, and re-layouts: 0.59 us -> 0.01 us
    ppermute x1, waiting for transfers between devices: 2.29 us -> 1.74 us  [body_pair(): other_stats = lax.ppermute(stats, 'row', swap)]
    ppermute x15 -> x12, waiting for transfers between devices: 9.99 us -> 9.56 us  [across(): return lax.ppermute(values, 'col', [(k, k ^ mask) for k in range(n_col)])]
  transfers between devices with their start and end apart: 18 -> 15, of which waited for: 8 -> 7; matrix products, arithmetic and copies ran while one was open for 0% -> 0% of each run, Pallas kernels for 10% -> 7%
where the time goes in v4:
time: 37.1 us; the launch traced here: 36.9 us
  starting transfers between devices  17.2 us (46%)
  waiting for transfers between devices  13.2 us (36%)
  Pallas kernels  4.91 us (13%)
  other arithmetic  0.85 us (2%)
  between operations  0.72 us (2%)
    ppermute x12, starting transfers between devices, across(): return lax.ppermute(values, 'col', [(k, k ^ mask) for k in range(n_col)])  12 us
    ppermute x12, waiting for transfers between devices, across(): return lax.ppermute(values, 'col', [(k, k ^ mask) for k in range(n_col)])  9.56 us
    ppermute x1, starting transfers between devices, body_pair(): b_other = lax.ppermute(b_eff, 'row', swap)  3.03 us
    ppermute x1, waiting for transfers between devices, body_pair(): arrived = lax.ppermute(codes, 'row', swap)  1.95 us
    ppermute x1, waiting for transfers between devices, body_pair(): other_stats = lax.ppermute(stats, 'row', swap)  1.74 us
    pallas_call x1, Pallas kernels, body_pair(): pl.pallas_call(functools.partial(finish_kernel, 2 * rows, limit), out_sha...  1.56 us
    ppermute x1, starting transfers between devices, body_pair(): arrived = lax.ppermute(codes, 'row', swap)  1.53 us
    pallas_call x1, Pallas kernels, body_pair(): pl.pallas_call(mask_kernel, out_shape=(pltpu.VMEM(a.shape, a.dtype), pltp...  1.46 us
  transfers between devices with their start and end apart: 15, of which 7 were waited for; matrix products, arithmetic and copies ran while one was open for 0% of the time, Pallas kernels for 7%

profile of v4, /device:TPU:0, one launch (start us, length us, event | category | flops | bytes accessed | tf_op | source)
XLA Modules:
  0.0 36.9 jit_solution(9807755272676699038)
XLA Ops:
  0.6 1.5 %mask_factors.1 = (bf16[512,128]{1,0:T(8,128)(2,1)S(1)}, bf16[8,128,384]{2,1,0:T(8,128)(2,1)S(1)}, s32[1,128]{1,0:T(1,128)S(1)}) custom-call(s32[1,4]{1,0:T(1,128)} %bitcast.9, s32[3,8]{1,0:T(4,128)} %bitcast.8, s32[4,3]{1,0:T(4,128)} %retained.1, s32[1,12]{1,0:T(1,128)} %bitcast.10, bf16[512,128]{1,0:T(8,128)(2,1)} %a.1, bf16[1024,384]{1,0:T(8,128)(2,1)} %b.1), custom_call_target="tpu_custom_call" | custom-call | tf_op jit(solution)/shard_map/mask_factors/pallas_call | solution.py:210
  2.1 3.0 %collective-permute-start = (bf16[8,128,384]{2,1,0:T(8,128)(2,1)S(1)}, bf16[8,128,384]{2,1,0:T(8,128)(2,1)S(1)}, u32[]{:S(2)}, u32[]{:S(2)}) collective-permute-start(bf16[8,128,384]{2,1,0:T(8,128)(2,1)S(1)} %get-tuple-element.15.b_own), channel_id=1, source_target_pairs={{0,16},{16,0},{1,17},{17,1},{2,18},{18,2},{3,19},{19,3},{4,20},{20... | collective-permute-start | bytes 2359304 | tf_op jit(solution)/shard_map/ppermute | solution.py:228
  5.1 2.6 %collective-permute-start.4 = (bf16[512,128]{1,0:T(8,128)(2,1)S(1)}, bf16[512,128]{1,0:T(8,128)(2,1)S(1)}, u32[]{:S(2)}, u32[]{:S(2)}) collective-permute-start(bf16[512,128]{1,0:T(8,128)(2,1)S(1)} %get-tuple-element.16.refs_0_), channel_id=1, source_target_pairs={{0,8},{1,9},{2,10},{3,11},{4,12},{5,13},{6,14},{7,15},{8,0},{9,1},... | collective-permute-start | bytes 393224 | tf_op jit(solution)/shard_map/ppermute | solution.py:204
  7.7 1.5 %collective-permute-start.1 = (bf16[512,128]{1,0:T(8,128)(2,1)S(1)}, bf16[512,128]{1,0:T(8,128)(2,1)S(1)}, u32[]{:S(2)}, u32[]{:S(2)}) collective-permute-start(bf16[512,128]{1,0:T(8,128)(2,1)S(1)} %get-tuple-element.16.refs_0_), channel_id=1, source_target_pairs={{0,2},{1,3},{2,0},{3,1},{4,6},{5,7},{6,4},{7,5},{8,10},{9,11},{10,... | collective-permute-start | bytes 393224 | tf_op jit(solution)/shard_map/ppermute | solution.py:204
  9.2 1.5 %collective-permute-start.3 = (bf16[512,128]{1,0:T(8,128)(2,1)S(1)}, bf16[512,128]{1,0:T(8,128)(2,1)S(1)}, u32[]{:S(2)}, u32[]{:S(2)}) collective-permute-start(bf16[512,128]{1,0:T(8,128)(2,1)S(1)} %get-tuple-element.16.refs_0_), channel_id=1, source_target_pairs={{0,6},{1,7},{2,4},{3,5},{4,2},{5,3},{6,0},{7,1},{8,14},{9,15},{10,... | collective-permute-start | bytes 393224 | tf_op jit(solution)/shard_map/ppermute | solution.py:204
  10.8 0.4 %collective-permute-start.2 = (bf16[512,128]{1,0:T(8,128)(2,1)S(1)}, bf16[512,128]{1,0:T(8,128)(2,1)S(1)}, u32[]{:S(2)}, u32[]{:S(2)}) collective-permute-start(bf16[512,128]{1,0:T(8,128)(2,1)S(1)} %get-tuple-element.16.refs_0_), channel_id=1, source_target_pairs={{0,4},{1,5},{2,6},{3,7},{4,0},{5,1},{6,2},{7,3},{8,12},{9,13},{10,... | collective-permute-start | bytes 393224 | tf_op jit(solution)/shard_map/ppermute | solution.py:204
  11.2 2.7 %collective-permute-done.4.refs_4_ = bf16[512,128]{1,0:T(8,128)(2,1)S(1)} collective-permute-done((bf16[512,128]{1,0:T(8,128)(2,1)S(1)}, bf16[512,128]{1,0:T(8,128)(2,1)S(1)}, u32[]{:S(2)}, u32[]{:S(2)}) %collective-permute-start.4) | collective-permute-done | bytes 131104 | tf_op jit(solution)/shard_map/ppermute | solution.py:204
  13.9 1.5 %collective-permute-start.10 = (bf16[512,128]{1,0:T(8,128)(2,1)S(1)}, bf16[512,128]{1,0:T(8,128)(2,1)S(1)}, u32[]{:S(2)}, u32[]{:S(2)}) collective-permute-start(bf16[512,128]{1,0:T(8,128)(2,1)S(1)} %collective-permute-done.4.refs_4_), channel_id=1, source_target_pairs={{0,2},{1,3},{2,0},{3,1},{4,6},{5,7},{6,4},{7,5},{8,10},{9,11},{10,... | collective-permute-start | bytes 393224 | tf_op jit(solution)/shard_map/ppermute | solution.py:204
  15.4 0.0 collective-permute-done.1.refs_1_
  15.4 0.6 %collective-permute-start.11 = (bf16[512,128]{1,0:T(8,128)(2,1)S(1)}, bf16[512,128]{1,0:T(8,128)(2,1)S(1)}, u32[]{:S(2)}, u32[]{:S(2)}) collective-permute-start(bf16[512,128]{1,0:T(8,128)(2,1)S(1)} %collective-permute-done.4.refs_4_), channel_id=1, source_target_pairs={{0,4},{1,5},{2,6},{3,7},{4,0},{5,1},{6,2},{7,3},{8,12},{9,13},{10,... | collective-permute-start | bytes 393224 | tf_op jit(solution)/shard_map/ppermute | solution.py:204
  16.0 1.2 %collective-permute-done.3.refs_3_ = bf16[512,128]{1,0:T(8,128)(2,1)S(1)} collective-permute-done((bf16[512,128]{1,0:T(8,128)(2,1)S(1)}, bf16[512,128]{1,0:T(8,128)(2,1)S(1)}, u32[]{:S(2)}, u32[]{:S(2)}) %collective-permute-start.3) | collective-permute-done | bytes 131104 | tf_op jit(solution)/shard_map/ppermute | solution.py:204
  17.2 2.8 %collective-permute-start.5 = (bf16[512,128]{1,0:T(8,128)(2,1)S(1)}, bf16[512,128]{1,0:T(8,128)(2,1)S(1)}, u32[]{:S(2)}, u32[]{:S(2)}) collective-permute-start(bf16[512,128]{1,0:T(8,128)(2,1)S(1)} %get-tuple-element.16.refs_0_), channel_id=1, source_target_pairs={{0,14},{1,15},{2,12},{3,13},{4,10},{5,11},{6,8},{7,9},{8,6},{9,7},... | collective-permute-start | bytes 393224 | tf_op jit(solution)/shard_map/ppermute | solution.py:204
  20.0 0.0 collective-permute-done.2.refs_2_
  20.0 0.1 collective-permute-start.6
  20.1 0.0 collective-permute-done.10.refs_0_
  20.1 0.5 %collective-permute-start.8 = (bf16[1024,128]{1,0:T(8,128)(2,1)S(1)}, bf16[1024,128]{1,0:T(8,128)(2,1)S(1)}, u32[]{:S(2)}, u32[]{:S(2)}) collective-permute-start(bf16[1024,128]{1,0:T(8,128)(2,1)S(1)} %pad_maximum_fusion.1), channel_id=1, source_target_pairs={{0,1},{1,0},{2,3},{3,2},{4,5},{5,4},{6,7},{7,6},{8,9},{9,8},{10,11... | collective-permute-start | bytes 786440 | tf_op jit(solution)/shard_map/ppermute | solution.py:204
  20.6 0.3 collective-permute-done.11.refs_1_
  20.9 0.0 collective-permute-start.7
  20.9 4.2 %collective-permute-done.5.refs_5_ = bf16[512,128]{1,0:T(8,128)(2,1)S(1)} collective-permute-done((bf16[512,128]{1,0:T(8,128)(2,1)S(1)}, bf16[512,128]{1,0:T(8,128)(2,1)S(1)}, u32[]{:S(2)}, u32[]{:S(2)}) %collective-permute-start.5) | collective-permute-done | bytes 131104 | tf_op jit(solution)/shard_map/ppermute | solution.py:204
  25.1 0.0 collective-permute-start.12
  25.1 0.0 collective-permute-done.7.refs_7_
  25.1 0.5 %collective-permute-start.9 = (bf16[512,128]{1,0:T(8,128)(2,1)S(1)}, bf16[512,128]{1,0:T(8,128)(2,1)S(1)}, u32[]{:S(2)}, u32[]{:S(2)}) collective-permute-start(bf16[512,128]{1,0:T(8,128)(2,1)S(1)} %collective-permute-done.5.refs_5_), channel_id=1, source_target_pairs={{0,1},{1,0},{2,3},{3,2},{4,5},{5,4},{6,7},{7,6},{8,9},{9,8},{10,11... | collective-permute-start | bytes 393224 | tf_op jit(solution)/shard_map/ppermute | solution.py:204
  25.6 1.2 %collective-permute-done.9.refs_9_ = bf16[512,128]{1,0:T(8,128)(2,1)S(1)} collective-permute-done((bf16[512,128]{1,0:T(8,128)(2,1)S(1)}, bf16[512,128]{1,0:T(8,128)(2,1)S(1)}, u32[]{:S(2)}, u32[]{:S(2)}) %collective-permute-start.9) | collective-permute-done | bytes 131104 | tf_op jit(solution)/shard_map/ppermute | solution.py:204
  26.8 0.0 collective-permute-done.6.refs_6_
  26.8 0.0 collective-permute-done.8.refs_8_
  26.8 0.0 collective-permute-done.b_other
  26.8 1.0 %gather_product.1 = (f32[512,384]{1,0:T(8,128)S(1)}, bf16[512,384]{1,0:T(8,128)(2,1)S(1)}) custom-call(bf16[8,128,384]{2,1,0:T(8,128)(2,1)S(1)} %get-tuple-element.15.b_own, bf16[8,128,384]{2,1,0:T(8,128)(2,1)S(1)} %collective-permute-done.b_other, bf16[512,128]{1,0:T(8,128)(2,1)S(1)} %get-tuple-element.16.refs_0_, ...), custom_call_target="tpu_custom_call" | custom-call | flops 805306368 | bytes 8388608 | tf_op jit(solution)/shard_map/gather_product/pallas_call | solution.py:244
  27.8 0.0 collective-permute-done.12.refs_2_
  27.8 0.9 %inflate.1 = (f32[512,384]{1,0:T(8,128)S(1)}, f32[8,384]{1,0:T(8,128)S(1)}, s16[6,128,128]{2,1,0:T(8,128)(2,1)S(1)}) custom-call(s32[1,128]{1,0:T(1,128)S(1)} %get-tuple-element.14.ints_far.ints, f32[512,384]{1,0:T(8,128)S(1)} %get-tuple-element.17.part, bf16[512,384]{1,0:T(8,128)(2,1)S(1)} %get-tuple-element.18.b_late, ...), custom_call_target="tpu_custom_call" | custom-call | tf_op jit(solution)/shard_map/inflate/pallas_call | solution.py:260
  28.8 0.6 %collective-permute-start.13 = (f32[8,384]{1,0:T(8,128)S(1)}, f32[8,384]{1,0:T(8,128)S(1)}, u32[]{:S(2)}, u32[]{:S(2)}) collective-permute-start(f32[8,384]{1,0:T(8,128)S(1)} %get-tuple-element.20.own), channel_id=1, source_target_pairs={{0,16},{16,0},{1,17},{17,1},{2,18},{18,2},{3,19},{19,3},{4,20},{20... | collective-permute-start | bytes 36872 | tf_op jit(solution)/shard_map/ppermute | solution.py:274
  29.3 1.5 %collective-permute-start.14 = (s16[6,128,128]{2,1,0:T(8,128)(2,1)S(1)}, s16[6,128,128]{2,1,0:T(8,128)(2,1)S(1)}, u32[]{:S(2)}, u32[]{:S(2)}) collective-permute-start(s16[6,128,128]{2,1,0:T(8,128)(2,1)S(1)} %get-tuple-element.23), channel_id=1, source_target_pairs={{0,16},{16,0},{1,17},{17,1},{2,18},{18,2},{3,19},{19,3},{4,20},{20... | collective-permute-start | bytes 589832 | tf_op jit(solution)/shard_map/ppermute | solution.py:275
  30.9 1.7 %collective-permute-done.13.other = f32[8,384]{1,0:T(8,128)S(1)} collective-permute-done((f32[8,384]{1,0:T(8,128)S(1)}, f32[8,384]{1,0:T(8,128)S(1)}, u32[]{:S(2)}, u32[]{:S(2)}) %collective-permute-start.13) | collective-permute-done | bytes 12320 | tf_op jit(solution)/shard_map/ppermute | solution.py:274
  32.6 1.6 %finish.1 = (bf16[512,384]{1,0:T(8,128)(2,1)}, bf16[12,128,128]{2,1,0:T(8,128)(2,1)}, f32[6,1,128]{2,1,0:T(1,128)S(1)}, f32[6,1,128]{2,1,0:T(1,128)S(1)}) custom-call(s32[1,128]{1,0:T(1,128)S(1)} %get-tuple-element.14.ints_far.ints, f32[512,384]{1,0:T(8,128)S(1)} %get-tuple-element.19.product, f32[8,384]{1,0:T(8,128)S(1)} %get-tuple-element.20.own, ...), custom_call_target="tpu_custom_call" | custom-call | tf_op jit(solution)/shard_map/finish/pallas_call | solution.py:276
  34.2 1.9 %collective-permute-done.14 = s16[6,128,128]{2,1,0:T(8,128)(2,1)S(1)} collective-permute-done((s16[6,128,128]{2,1,0:T(8,128)(2,1)S(1)}, s16[6,128,128]{2,1,0:T(8,128)(2,1)S(1)}, u32[]{:S(2)}, u32[]{:S(2)}) %collective-permute-start.14) | collective-permute-done | bytes 196640 | tf_op jit(solution)/shard_map/ppermute | solution.py:275
  36.1 0.8 %fusion = bf16[12,128,128]{2,1,0:T(8,128)(2,1)} fusion(bf16[12,128,128]{2,1,0:T(8,128)(2,1)} %get-tuple-element.22, s32[]{:T(128)S(6)} %select_n.3, s16[6,128,128]{2,1,0:T(8,128)(2,1)S(1)} %collective-permute-done.14, f32[6,128]{1,0:T(8,128)S(1)} %get-tuple-element.26, f32[6,128]{1,0:T(8,128)S(1)} %get-tuple-element.27), kind=kLoop, calls=%fused_computation.4 | loop fusion | flops 589824 | bytes 399364 | tf_op jit(solution)/shard_map/dynamic_update_slice | solution.py:291
  (4 shorter events, 0.1 us)
Async XLA Ops:
  2.1 24.7 %collective-permute-start = (bf16[8,128,384]{2,1,0:T(8,128)(2,1)S(1)}, bf16[8,128,384]{2,1,0:T(8,128)(2,1)S(1)}, u32[]{:S(2)}, u32[]{:S(2)}) collective-permute-start(bf16[8,128,384]{2,1,0:T(8,128)(2,1)S(1)} %get-tuple-element.15.b_own), channel_id=1, source_target_pairs={{0,16},{16,0},{1,17},{17,1},{2,18},{18,2},{3,19},{19,3},{4,20},{20... | collective-permute-start | bytes 2359304 | tf_op jit(solution)/shard_map/ppermute | solution.py:228
  5.1 8.8 %collective-permute-start.4 = (bf16[512,128]{1,0:T(8,128)(2,1)S(1)}, bf16[512,128]{1,0:T(8,128)(2,1)S(1)}, u32[]{:S(2)}, u32[]{:S(2)}) collective-permute-start(bf16[512,128]{1,0:T(8,128)(2,1)S(1)} %get-tuple-element.16.refs_0_), channel_id=1, source_target_pairs={{0,8},{1,9},{2,10},{3,11},{4,12},{5,13},{6,14},{7,15},{8,0},{9,1},... | collective-permute-start | bytes 393224 | tf_op jit(solution)/shard_map/ppermute | solution.py:204
  7.7 7.7 %collective-permute-start.1 = (bf16[512,128]{1,0:T(8,128)(2,1)S(1)}, bf16[512,128]{1,0:T(8,128)(2,1)S(1)}, u32[]{:S(2)}, u32[]{:S(2)}) collective-permute-start(bf16[512,128]{1,0:T(8,128)(2,1)S(1)} %get-tuple-element.16.refs_0_), channel_id=1, source_target_pairs={{0,2},{1,3},{2,0},{3,1},{4,6},{5,7},{6,4},{7,5},{8,10},{9,11},{10,... | collective-permute-start | bytes 393224 | tf_op jit(solution)/shard_map/ppermute | solution.py:204
  9.2 8.0 %collective-permute-start.3 = (bf16[512,128]{1,0:T(8,128)(2,1)S(1)}, bf16[512,128]{1,0:T(8,128)(2,1)S(1)}, u32[]{:S(2)}, u32[]{:S(2)}) collective-permute-start(bf16[512,128]{1,0:T(8,128)(2,1)S(1)} %get-tuple-element.16.refs_0_), channel_id=1, source_target_pairs={{0,6},{1,7},{2,4},{3,5},{4,2},{5,3},{6,0},{7,1},{8,14},{9,15},{10,... | collective-permute-start | bytes 393224 | tf_op jit(solution)/shard_map/ppermute | solution.py:204
  10.8 9.3 %collective-permute-start.2 = (bf16[512,128]{1,0:T(8,128)(2,1)S(1)}, bf16[512,128]{1,0:T(8,128)(2,1)S(1)}, u32[]{:S(2)}, u32[]{:S(2)}) collective-permute-start(bf16[512,128]{1,0:T(8,128)(2,1)S(1)} %get-tuple-element.16.refs_0_), channel_id=1, source_target_pairs={{0,4},{1,5},{2,6},{3,7},{4,0},{5,1},{6,2},{7,3},{8,12},{9,13},{10,... | collective-permute-start | bytes 393224 | tf_op jit(solution)/shard_map/ppermute | solution.py:204
  13.9 6.2 %collective-permute-start.10 = (bf16[512,128]{1,0:T(8,128)(2,1)S(1)}, bf16[512,128]{1,0:T(8,128)(2,1)S(1)}, u32[]{:S(2)}, u32[]{:S(2)}) collective-permute-start(bf16[512,128]{1,0:T(8,128)(2,1)S(1)} %collective-permute-done.4.refs_4_), channel_id=1, source_target_pairs={{0,2},{1,3},{2,0},{3,1},{4,6},{5,7},{6,4},{7,5},{8,10},{9,11},{10,... | collective-permute-start | bytes 393224 | tf_op jit(solution)/shard_map/ppermute | solution.py:204
  15.4 5.5 %collective-permute-start.11 = (bf16[512,128]{1,0:T(8,128)(2,1)S(1)}, bf16[512,128]{1,0:T(8,128)(2,1)S(1)}, u32[]{:S(2)}, u32[]{:S(2)}) collective-permute-start(bf16[512,128]{1,0:T(8,128)(2,1)S(1)} %collective-permute-done.4.refs_4_), channel_id=1, source_target_pairs={{0,4},{1,5},{2,6},{3,7},{4,0},{5,1},{6,2},{7,3},{8,12},{9,13},{10,... | collective-permute-start | bytes 393224 | tf_op jit(solution)/shard_map/ppermute | solution.py:204
  17.2 7.9 %collective-permute-start.5 = (bf16[512,128]{1,0:T(8,128)(2,1)S(1)}, bf16[512,128]{1,0:T(8,128)(2,1)S(1)}, u32[]{:S(2)}, u32[]{:S(2)}) collective-permute-start(bf16[512,128]{1,0:T(8,128)(2,1)S(1)} %get-tuple-element.16.refs_0_), channel_id=1, source_target_pairs={{0,14},{1,15},{2,12},{3,13},{4,10},{5,11},{6,8},{7,9},{8,6},{9,7},... | collective-permute-start | bytes 393224 | tf_op jit(solution)/shard_map/ppermute | solution.py:204
  20.0 6.8 %collective-permute-start.6 = (bf16[1024,128]{1,0:T(8,128)(2,1)S(1)}, bf16[1024,128]{1,0:T(8,128)(2,1)S(1)}, u32[]{:S(2)}, u32[]{:S(2)}) collective-permute-start(bf16[1024,128]{1,0:T(8,128)(2,1)S(1)} %pad_maximum_fusion), channel_id=1, source_target_pairs={{0,1},{1,0},{2,3},{3,2},{4,5},{5,4},{6,7},{7,6},{8,9},{9,8},{10,11... | collective-permute-start | bytes 786440 | tf_op jit(solution)/shard_map/ppermute | solution.py:204
  20.1 6.7 %collective-permute-start.8 = (bf16[1024,128]{1,0:T(8,128)(2,1)S(1)}, bf16[1024,128]{1,0:T(8,128)(2,1)S(1)}, u32[]{:S(2)}, u32[]{:S(2)}) collective-permute-start(bf16[1024,128]{1,0:T(8,128)(2,1)S(1)} %pad_maximum_fusion.1), channel_id=1, source_target_pairs={{0,1},{1,0},{2,3},{3,2},{4,5},{5,4},{6,7},{7,6},{8,9},{9,8},{10,11... | collective-permute-start | bytes 786440 | tf_op jit(solution)/shard_map/ppermute | solution.py:204
  20.9 4.2 %collective-permute-start.7 = (bf16[512,128]{1,0:T(8,128)(2,1)S(1)}, bf16[512,128]{1,0:T(8,128)(2,1)S(1)}, u32[]{:S(2)}, u32[]{:S(2)}) collective-permute-start(bf16[512,128]{1,0:T(8,128)(2,1)S(1)} %collective-permute-done.2.refs_2_), channel_id=1, source_target_pairs={{0,1},{1,0},{2,3},{3,2},{4,5},{5,4},{6,7},{7,6},{8,9},{9,8},{10,11... | collective-permute-start | bytes 393224 | tf_op jit(solution)/shard_map/ppermute | solution.py:204
  25.1 2.7 %collective-permute-start.12 = (bf16[1024,128]{1,0:T(8,128)(2,1)S(1)}, bf16[1024,128]{1,0:T(8,128)(2,1)S(1)}, u32[]{:S(2)}, u32[]{:S(2)}) collective-permute-start(bf16[1024,128]{1,0:T(8,128)(2,1)S(1)} %pad_maximum_fusion.2), channel_id=1, source_target_pairs={{0,1},{1,0},{2,3},{3,2},{4,5},{5,4},{6,7},{7,6},{8,9},{9,8},{10,11... | collective-permute-start | bytes 786440 | tf_op jit(solution)/shard_map/ppermute | solution.py:204
  25.1 1.7 %collective-permute-start.9 = (bf16[512,128]{1,0:T(8,128)(2,1)S(1)}, bf16[512,128]{1,0:T(8,128)(2,1)S(1)}, u32[]{:S(2)}, u32[]{:S(2)}) collective-permute-start(bf16[512,128]{1,0:T(8,128)(2,1)S(1)} %collective-permute-done.5.refs_5_), channel_id=1, source_target_pairs={{0,1},{1,0},{2,3},{3,2},{4,5},{5,4},{6,7},{7,6},{8,9},{9,8},{10,11... | collective-permute-start | bytes 393224 | tf_op jit(solution)/shard_map/ppermute | solution.py:204
  28.8 3.9 %collective-permute-start.13 = (f32[8,384]{1,0:T(8,128)S(1)}, f32[8,384]{1,0:T(8,128)S(1)}, u32[]{:S(2)}, u32[]{:S(2)}) collective-permute-start(f32[8,384]{1,0:T(8,128)S(1)} %get-tuple-element.20.own), channel_id=1, source_target_pairs={{0,16},{16,0},{1,17},{17,1},{2,18},{18,2},{3,19},{19,3},{4,20},{20... | collective-permute-start | bytes 36872 | tf_op jit(solution)/shard_map/ppermute | solution.py:274
  29.3 6.8 %collective-permute-start.14 = (s16[6,128,128]{2,1,0:T(8,128)(2,1)S(1)}, s16[6,128,128]{2,1,0:T(8,128)(2,1)S(1)}, u32[]{:S(2)}, u32[]{:S(2)}) collective-permute-start(s16[6,128,128]{2,1,0:T(8,128)(2,1)S(1)} %get-tuple-element.23), channel_id=1, source_target_pairs={{0,16},{16,0},{1,17},{17,1},{2,18},{18,2},{3,19},{19,3},{4,20},{20... | collective-permute-start | bytes 589832 | tf_op jit(solution)/shard_map/ppermute | solution.py:275

commit v5 on v4

--- a/solution.py
+++ b/solution.py
@@ -238,7 +238,9 @@
         return [m | 1 for m in batch], across(jnp.concatenate([pieces[m] for m in batch], axis=0), 1)
 
     early = [([m], pieces[m]) for m in sorted(pieces) if m not in late]
-    early += [exchanged(batch) for batch in ((0, 2), (4,), (6, 8), (14,))]
+    early += [exchanged(batch) for batch in ((0, 2, 4), (6, 8, 14))]
+    *moved, b_other = lax.optimization_barrier((*[pieces[m] for m in late_even], b_other))
+    pieces.update(zip(late_even, moved))
     last = [([m], pieces[m]) for m in late_even] + [exchanged(late_even)]
     groups, shards = zip(*early)
     part, b_late = pl.pallas_call(

time: 37.1 us -> 34.7 us (0.935)
  waiting for transfers between devices: 13.2 us -> 10.3 us
  starting transfers between devices: 17.2 us -> 17.9 us
    ppermute x12 -> x10, waiting for transfers between devices: 9.56 us -> 6.54 us  [across(): return lax.ppermute(values, 'col', [(k, k ^ mask) for k in range(n_col)])]
    ppermute x12 -> x10, starting transfers between devices: 12 us -> 12.7 us  [across(): return lax.ppermute(values, 'col', [(k, k ^ mask) for k in range(n_col)])]
  transfers between devices with their start and end apart: 15 -> 13, of which waited for: 7 -> 10; matrix products, arithmetic and copies ran while one was open for 0% -> 0% of each run, Pallas kernels for 7% -> 7%
where the time goes in v5:
time: 34.7 us; the launch traced here: 34.6 us
  starting transfers between devices  17.9 us (52%)
  waiting for transfers between devices  10.3 us (30%)
  Pallas kernels  4.88 us (14%)
  other arithmetic  0.86 us (2%)
  between operations  0.71 us (2%)
    ppermute x10, starting transfers between devices, across(): return lax.ppermute(values, 'col', [(k, k ^ mask) for k in range(n_col)])  12.7 us
    ppermute x10, waiting for transfers between devices, across(): return lax.ppermute(values, 'col', [(k, k ^ mask) for k in range(n_col)])  6.54 us
    ppermute x1, starting transfers between devices, body_pair(): b_other = lax.ppermute(b_eff, 'row', swap)  3.03 us
    ppermute x1, waiting for transfers between devices, body_pair(): arrived = lax.ppermute(codes, 'row', swap)  1.96 us
    ppermute x1, waiting for transfers between devices, body_pair(): other_stats = lax.ppermute(stats, 'row', swap)  1.74 us
    pallas_call x1, Pallas kernels, body_pair(): pl.pallas_call(functools.partial(finish_kernel, 2 * rows, limit), out_sha...  1.56 us
    ppermute x1, starting transfers between devices, body_pair(): arrived = lax.ppermute(codes, 'row', swap)  1.53 us
    pallas_call x1, Pallas kernels, body_pair(): pl.pallas_call(mask_kernel, out_shape=(pltpu.VMEM(a.shape, a.dtype), pltp...  1.46 us
  transfers between devices with their start and end apart: 13, of which 10 were waited for; matrix products, arithmetic and copies ran while one was open for 0% of the time, Pallas kernels for 7%

profile of v5, /device:TPU:0, one launch (start us, length us, event | category | flops | bytes accessed | tf_op | source)
XLA Modules:
  0.0 34.6 jit_solution(12989929665196618354)
XLA Ops:
  0.6 1.5 %mask_factors.1 = (bf16[512,128]{1,0:T(8,128)(2,1)S(1)}, bf16[8,128,384]{2,1,0:T(8,128)(2,1)S(1)}, s32[1,128]{1,0:T(1,128)S(1)}) custom-call(s32[1,4]{1,0:T(1,128)} %bitcast.9, s32[3,8]{1,0:T(4,128)} %bitcast.8, s32[4,3]{1,0:T(4,128)} %retained.1, s32[1,12]{1,0:T(1,128)} %bitcast.10, bf16[512,128]{1,0:T(8,128)(2,1)} %a.1, bf16[1024,384]{1,0:T(8,128)(2,1)} %b.1), custom_call_target="tpu_custom_call" | custom-call | tf_op jit(solution)/shard_map/mask_factors/pallas_call | solution.py:210
  2.1 3.0 %collective-permute-start.3 = (bf16[8,128,384]{2,1,0:T(8,128)(2,1)S(1)}, bf16[8,128,384]{2,1,0:T(8,128)(2,1)S(1)}, u32[]{:S(2)}, u32[]{:S(2)}) collective-permute-start(bf16[8,128,384]{2,1,0:T(8,128)(2,1)S(1)} %get-tuple-element.18.b_own), channel_id=1, source_target_pairs={{0,16},{16,0},{1,17},{17,1},{2,18},{18,2},{3,19},{19,3},{4,20},{20... | collective-permute-start | bytes 2359304 | tf_op jit(solution)/shard_map/ppermute | solution.py:228
  5.1 1.5 %collective-permute-start.4 = (bf16[512,128]{1,0:T(8,128)(2,1)S(1)}, bf16[512,128]{1,0:T(8,128)(2,1)S(1)}, u32[]{:S(2)}, u32[]{:S(2)}) collective-permute-start(bf16[512,128]{1,0:T(8,128)(2,1)S(1)} %get-tuple-element.19.refs_0_), channel_id=1, source_target_pairs={{0,2},{1,3},{2,0},{3,1},{4,6},{5,7},{6,4},{7,5},{8,10},{9,11},{10,... | collective-permute-start | bytes 393224 | tf_op jit(solution)/shard_map/ppermute | solution.py:204
  6.6 1.6 %collective-permute-start.5 = (bf16[512,128]{1,0:T(8,128)(2,1)S(1)}, bf16[512,128]{1,0:T(8,128)(2,1)S(1)}, u32[]{:S(2)}, u32[]{:S(2)}) collective-permute-start(bf16[512,128]{1,0:T(8,128)(2,1)S(1)} %get-tuple-element.19.refs_0_), channel_id=1, source_target_pairs={{0,4},{1,5},{2,6},{3,7},{4,0},{5,1},{6,2},{7,3},{8,12},{9,13},{10,... | collective-permute-start | bytes 393224 | tf_op jit(solution)/shard_map/ppermute | solution.py:204
  8.2 2.6 %collective-permute-start = (bf16[512,128]{1,0:T(8,128)(2,1)S(1)}, bf16[512,128]{1,0:T(8,128)(2,1)S(1)}, u32[]{:S(2)}, u32[]{:S(2)}) collective-permute-start(bf16[512,128]{1,0:T(8,128)(2,1)S(1)} %get-tuple-element.19.refs_0_), channel_id=1, source_target_pairs={{0,8},{1,9},{2,10},{3,11},{4,12},{5,13},{6,14},{7,15},{8,0},{9,1},... | collective-permute-start | bytes 393224 | tf_op jit(solution)/shard_map/ppermute | solution.py:204
  10.8 0.4 %collective-permute-start.6 = (bf16[512,128]{1,0:T(8,128)(2,1)S(1)}, bf16[512,128]{1,0:T(8,128)(2,1)S(1)}, u32[]{:S(2)}, u32[]{:S(2)}) collective-permute-start(bf16[512,128]{1,0:T(8,128)(2,1)S(1)} %get-tuple-element.19.refs_0_), channel_id=1, source_target_pairs={{0,6},{1,7},{2,4},{3,5},{4,2},{5,3},{6,0},{7,1},{8,14},{9,15},{10,... | collective-permute-start | bytes 393224 | tf_op jit(solution)/shard_map/ppermute | solution.py:204
  11.2 0.0 collective-permute-done.4.refs_1_
  11.2 3.4 %collective-permute-start.7 = (bf16[512,128]{1,0:T(8,128)(2,1)S(1)}, bf16[512,128]{1,0:T(8,128)(2,1)S(1)}, u32[]{:S(2)}, u32[]{:S(2)}) collective-permute-start(bf16[512,128]{1,0:T(8,128)(2,1)S(1)} %get-tuple-element.19.refs_0_), channel_id=1, source_target_pairs={{0,14},{1,15},{2,12},{3,13},{4,10},{5,11},{6,8},{7,9},{8,6},{9,7},... | collective-permute-start | bytes 393224 | tf_op jit(solution)/shard_map/ppermute | solution.py:204
  14.6 0.1 collective-permute-done.5.refs_2_
  14.7 0.1 collective-permute-start.8
  14.8 1.2 %collective-permute-done.refs_4_ = bf16[512,128]{1,0:T(8,128)(2,1)S(1)} collective-permute-done((bf16[512,128]{1,0:T(8,128)(2,1)S(1)}, bf16[512,128]{1,0:T(8,128)(2,1)S(1)}, u32[]{:S(2)}, u32[]{:S(2)}) %collective-permute-start) | collective-permute-done | bytes 131104 | tf_op jit(solution)/shard_map/ppermute | solution.py:204
  16.0 0.5 %collective-permute-start.1 = (bf16[512,128]{1,0:T(8,128)(2,1)S(1)}, bf16[512,128]{1,0:T(8,128)(2,1)S(1)}, u32[]{:S(2)}, u32[]{:S(2)}) collective-permute-start(bf16[512,128]{1,0:T(8,128)(2,1)S(1)} %collective-permute-done.refs_4_), channel_id=1, source_target_pairs={{0,2},{1,3},{2,0},{3,1},{4,6},{5,7},{6,4},{7,5},{8,10},{9,11},{10,... | collective-permute-start | bytes 393224 | tf_op jit(solution)/shard_map/ppermute | solution.py:204
  16.5 1.0 %collective-permute-done.6.refs_3_ = bf16[512,128]{1,0:T(8,128)(2,1)S(1)} collective-permute-done((bf16[512,128]{1,0:T(8,128)(2,1)S(1)}, bf16[512,128]{1,0:T(8,128)(2,1)S(1)}, u32[]{:S(2)}, u32[]{:S(2)}) %collective-permute-start.6) | collective-permute-done | bytes 131104 | tf_op jit(solution)/shard_map/ppermute | solution.py:204
  17.6 2.5 %collective-permute-start.2 = (bf16[512,128]{1,0:T(8,128)(2,1)S(1)}, bf16[512,128]{1,0:T(8,128)(2,1)S(1)}, u32[]{:S(2)}, u32[]{:S(2)}) collective-permute-start(bf16[512,128]{1,0:T(8,128)(2,1)S(1)} %collective-permute-done.refs_4_), channel_id=1, source_target_pairs={{0,4},{1,5},{2,6},{3,7},{4,0},{5,1},{6,2},{7,3},{8,12},{9,13},{10,... | collective-permute-start | bytes 393224 | tf_op jit(solution)/shard_map/ppermute | solution.py:204
  20.1 2.3 %collective-permute-done.7.refs_5_ = bf16[512,128]{1,0:T(8,128)(2,1)S(1)} collective-permute-done((bf16[512,128]{1,0:T(8,128)(2,1)S(1)}, bf16[512,128]{1,0:T(8,128)(2,1)S(1)}, u32[]{:S(2)}, u32[]{:S(2)}) %collective-permute-start.7) | collective-permute-done | bytes 131104 | tf_op jit(solution)/shard_map/ppermute | solution.py:204
  22.4 0.1 collective-permute-start.9
  22.5 0.7 %collective-permute-done.1.refs_0_ = bf16[512,128]{1,0:T(8,128)(2,1)S(1)} collective-permute-done((bf16[512,128]{1,0:T(8,128)(2,1)S(1)}, bf16[512,128]{1,0:T(8,128)(2,1)S(1)}, u32[]{:S(2)}, u32[]{:S(2)}) %collective-permute-start.1) | collective-permute-done | bytes 131104 | tf_op jit(solution)/shard_map/ppermute | solution.py:204
  23.2 0.7 %collective-permute-done.2.refs_1_ = bf16[512,128]{1,0:T(8,128)(2,1)S(1)} collective-permute-done((bf16[512,128]{1,0:T(8,128)(2,1)S(1)}, bf16[512,128]{1,0:T(8,128)(2,1)S(1)}, u32[]{:S(2)}, u32[]{:S(2)}) %collective-permute-start.2) | collective-permute-done | bytes 131104 | tf_op jit(solution)/shard_map/ppermute | solution.py:204
  23.9 0.0 collective-permute-done.3.b_other
  23.9 0.1 collective-permute-start.10
  24.0 0.0 collective-permute-done.8.refs_6_
  24.0 0.2 collective-permute-done.9.refs_7_
  24.2 1.0 %gather_product.1 = (f32[512,384]{1,0:T(8,128)S(1)}, bf16[512,384]{1,0:T(8,128)(2,1)S(1)}) custom-call(bf16[8,128,384]{2,1,0:T(8,128)(2,1)S(1)} %get-tuple-element.18.b_own, bf16[8,128,384]{2,1,0:T(8,128)(2,1)S(1)} %collective-permute-done.3.b_other, bf16[512,128]{1,0:T(8,128)(2,1)S(1)} %get-tuple-element.19.refs_0_, ...), custom_call_target="tpu_custom_call" | custom-call | flops 805306368 | bytes 8388608 | tf_op jit(solution)/shard_map/gather_product/pallas_call | solution.py:246
  25.2 0.3 collective-permute-done.10.refs_2_
  25.5 0.9 %inflate.1 = (f32[512,384]{1,0:T(8,128)S(1)}, f32[8,384]{1,0:T(8,128)S(1)}, s16[6,128,128]{2,1,0:T(8,128)(2,1)S(1)}) custom-call(s32[1,128]{1,0:T(1,128)S(1)} %get-tuple-element.17.ints_far.ints, f32[512,384]{1,0:T(8,128)S(1)} %get-tuple-element.21.part, bf16[512,384]{1,0:T(8,128)(2,1)S(1)} %get-tuple-element.22.b_late, ...), custom_call_target="tpu_custom_call" | custom-call | tf_op jit(solution)/shard_map/inflate/pallas_call | solution.py:262
  26.4 0.6 %collective-permute-start.11 = (f32[8,384]{1,0:T(8,128)S(1)}, f32[8,384]{1,0:T(8,128)S(1)}, u32[]{:S(2)}, u32[]{:S(2)}) collective-permute-start(f32[8,384]{1,0:T(8,128)S(1)} %get-tuple-element.26.own), channel_id=1, source_target_pairs={{0,16},{16,0},{1,17},{17,1},{2,18},{18,2},{3,19},{19,3},{4,20},{20... | collective-permute-start | bytes 36872 | tf_op jit(solution)/shard_map/ppermute | solution.py:276
  27.0 1.5 %collective-permute-start.12 = (s16[6,128,128]{2,1,0:T(8,128)(2,1)S(1)}, s16[6,128,128]{2,1,0:T(8,128)(2,1)S(1)}, u32[]{:S(2)}, u32[]{:S(2)}) collective-permute-start(s16[6,128,128]{2,1,0:T(8,128)(2,1)S(1)} %get-tuple-element.29), channel_id=1, source_target_pairs={{0,16},{16,0},{1,17},{17,1},{2,18},{18,2},{3,19},{19,3},{4,20},{20... | collective-permute-start | bytes 589832 | tf_op jit(solution)/shard_map/ppermute | solution.py:277
  28.5 1.7 %collective-permute-done.11.other = f32[8,384]{1,0:T(8,128)S(1)} collective-permute-done((f32[8,384]{1,0:T(8,128)S(1)}, f32[8,384]{1,0:T(8,128)S(1)}, u32[]{:S(2)}, u32[]{:S(2)}) %collective-permute-start.11) | collective-permute-done | bytes 12320 | tf_op jit(solution)/shard_map/ppermute | solution.py:276
  30.3 1.6 %finish.1 = (bf16[512,384]{1,0:T(8,128)(2,1)}, bf16[12,128,128]{2,1,0:T(8,128)(2,1)}, f32[6,1,128]{2,1,0:T(1,128)S(1)}, f32[6,1,128]{2,1,0:T(1,128)S(1)}) custom-call(s32[1,128]{1,0:T(1,128)S(1)} %get-tuple-element.17.ints_far.ints, f32[512,384]{1,0:T(8,128)S(1)} %get-tuple-element.25.product, f32[8,384]{1,0:T(8,128)S(1)} %get-tuple-element.26.own, ...), custom_call_target="tpu_custom_call" | custom-call | tf_op jit(solution)/shard_map/finish/pallas_call | solution.py:278
  31.8 2.0 %collective-permute-done.12 = s16[6,128,128]{2,1,0:T(8,128)(2,1)S(1)} collective-permute-done((s16[6,128,128]{2,1,0:T(8,128)(2,1)S(1)}, s16[6,128,128]{2,1,0:T(8,128)(2,1)S(1)}, u32[]{:S(2)}, u32[]{:S(2)}) %collective-permute-start.12) | collective-permute-done | bytes 196640 | tf_op jit(solution)/shard_map/ppermute | solution.py:277
  33.8 0.8 %fusion = bf16[12,128,128]{2,1,0:T(8,128)(2,1)} fusion(bf16[12,128,128]{2,1,0:T(8,128)(2,1)} %get-tuple-element.28, s32[]{:T(128)S(6)} %select_n.3, s16[6,128,128]{2,1,0:T(8,128)(2,1)S(1)} %collective-permute-done.12, f32[6,128]{1,0:T(8,128)S(1)} %get-tuple-element.32, f32[6,128]{1,0:T(8,128)S(1)} %get-tuple-element.33), kind=kLoop, calls=%fused_computation.4 | loop fusion | flops 589824 | bytes 399364 | tf_op jit(solution)/shard_map/dynamic_update_slice | solution.py:293
  (4 shorter events, 0.1 us)
Async XLA Ops:
  2.1 21.8 %collective-permute-start.3 = (bf16[8,128,384]{2,1,0:T(8,128)(2,1)S(1)}, bf16[8,128,384]{2,1,0:T(8,128)(2,1)S(1)}, u32[]{:S(2)}, u32[]{:S(2)}) collective-permute-start(bf16[8,128,384]{2,1,0:T(8,128)(2,1)S(1)} %get-tuple-element.18.b_own), channel_id=1, source_target_pairs={{0,16},{16,0},{1,17},{17,1},{2,18},{18,2},{3,19},{19,3},{4,20},{20... | collective-permute-start | bytes 2359304 | tf_op jit(solution)/shard_map/ppermute | solution.py:228
  5.1 6.1 %collective-permute-start.4 = (bf16[512,128]{1,0:T(8,128)(2,1)S(1)}, bf16[512,128]{1,0:T(8,128)(2,1)S(1)}, u32[]{:S(2)}, u32[]{:S(2)}) collective-permute-start(bf16[512,128]{1,0:T(8,128)(2,1)S(1)} %get-tuple-element.19.refs_0_), channel_id=1, source_target_pairs={{0,2},{1,3},{2,0},{3,1},{4,6},{5,7},{6,4},{7,5},{8,10},{9,11},{10,... | collective-permute-start | bytes 393224 | tf_op jit(solution)/shard_map/ppermute | solution.py:204
  6.6 8.1 %collective-permute-start.5 = (bf16[512,128]{1,0:T(8,128)(2,1)S(1)}, bf16[512,128]{1,0:T(8,128)(2,1)S(1)}, u32[]{:S(2)}, u32[]{:S(2)}) collective-permute-start(bf16[512,128]{1,0:T(8,128)(2,1)S(1)} %get-tuple-element.19.refs_0_), channel_id=1, source_target_pairs={{0,4},{1,5},{2,6},{3,7},{4,0},{5,1},{6,2},{7,3},{8,12},{9,13},{10,... | collective-permute-start | bytes 393224 | tf_op jit(solution)/shard_map/ppermute | solution.py:204
  8.2 7.8 %collective-permute-start = (bf16[512,128]{1,0:T(8,128)(2,1)S(1)}, bf16[512,128]{1,0:T(8,128)(2,1)S(1)}, u32[]{:S(2)}, u32[]{:S(2)}) collective-permute-start(bf16[512,128]{1,0:T(8,128)(2,1)S(1)} %get-tuple-element.19.refs_0_), channel_id=1, source_target_pairs={{0,8},{1,9},{2,10},{3,11},{4,12},{5,13},{6,14},{7,15},{8,0},{9,1},... | collective-permute-start | bytes 393224 | tf_op jit(solution)/shard_map/ppermute | solution.py:204
  10.8 6.8 %collective-permute-start.6 = (bf16[512,128]{1,0:T(8,128)(2,1)S(1)}, bf16[512,128]{1,0:T(8,128)(2,1)S(1)}, u32[]{:S(2)}, u32[]{:S(2)}) collective-permute-start(bf16[512,128]{1,0:T(8,128)(2,1)S(1)} %get-tuple-element.19.refs_0_), channel_id=1, source_target_pairs={{0,6},{1,7},{2,4},{3,5},{4,2},{5,3},{6,0},{7,1},{8,14},{9,15},{10,... | collective-permute-start | bytes 393224 | tf_op jit(solution)/shard_map/ppermute | solution.py:204
  11.2 11.2 %collective-permute-start.7 = (bf16[512,128]{1,0:T(8,128)(2,1)S(1)}, bf16[512,128]{1,0:T(8,128)(2,1)S(1)}, u32[]{:S(2)}, u32[]{:S(2)}) collective-permute-start(bf16[512,128]{1,0:T(8,128)(2,1)S(1)} %get-tuple-element.19.refs_0_), channel_id=1, source_target_pairs={{0,14},{1,15},{2,12},{3,13},{4,10},{5,11},{6,8},{7,9},{8,6},{9,7},... | collective-permute-start | bytes 393224 | tf_op jit(solution)/shard_map/ppermute | solution.py:204
  14.7 9.3 %collective-permute-start.8 = (bf16[1536,128]{1,0:T(8,128)(2,1)S(1)}, bf16[1536,128]{1,0:T(8,128)(2,1)S(1)}, u32[]{:S(2)}, u32[]{:S(2)}) collective-permute-start(bf16[1536,128]{1,0:T(8,128)(2,1)S(1)} %pad_maximum_fusion), channel_id=1, source_target_pairs={{0,1},{1,0},{2,3},{3,2},{4,5},{5,4},{6,7},{7,6},{8,9},{9,8},{10,11... | collective-permute-start | bytes 1179656 | tf_op jit(solution)/shard_map/ppermute | solution.py:204
  16.0 7.2 %collective-permute-start.1 = (bf16[512,128]{1,0:T(8,128)(2,1)S(1)}, bf16[512,128]{1,0:T(8,128)(2,1)S(1)}, u32[]{:S(2)}, u32[]{:S(2)}) collective-permute-start(bf16[512,128]{1,0:T(8,128)(2,1)S(1)} %collective-permute-done.refs_4_), channel_id=1, source_target_pairs={{0,2},{1,3},{2,0},{3,1},{4,6},{5,7},{6,4},{7,5},{8,10},{9,11},{10,... | collective-permute-start | bytes 393224 | tf_op jit(solution)/shard_map/ppermute | solution.py:204
  17.6 6.3 %collective-permute-start.2 = (bf16[512,128]{1,0:T(8,128)(2,1)S(1)}, bf16[512,128]{1,0:T(8,128)(2,1)S(1)}, u32[]{:S(2)}, u32[]{:S(2)}) collective-permute-start(bf16[512,128]{1,0:T(8,128)(2,1)S(1)} %collective-permute-done.refs_4_), channel_id=1, source_target_pairs={{0,4},{1,5},{2,6},{3,7},{4,0},{5,1},{6,2},{7,3},{8,12},{9,13},{10,... | collective-permute-start | bytes 393224 | tf_op jit(solution)/shard_map/ppermute | solution.py:204
  22.4 1.8 %collective-permute-start.9 = (bf16[1536,128]{1,0:T(8,128)(2,1)S(1)}, bf16[1536,128]{1,0:T(8,128)(2,1)S(1)}, u32[]{:S(2)}, u32[]{:S(2)}) collective-permute-start(bf16[1536,128]{1,0:T(8,128)(2,1)S(1)} %pad_maximum_fusion.1), channel_id=1, source_target_pairs={{0,1},{1,0},{2,3},{3,2},{4,5},{5,4},{6,7},{7,6},{8,9},{9,8},{10,11... | collective-permute-start | bytes 1179656 | tf_op jit(solution)/shard_map/ppermute | solution.py:204
  23.9 1.6 %collective-permute-start.10 = (bf16[1024,128]{1,0:T(8,128)(2,1)S(1)}, bf16[1024,128]{1,0:T(8,128)(2,1)S(1)}, u32[]{:S(2)}, u32[]{:S(2)}) collective-permute-start(bf16[1024,128]{1,0:T(8,128)(2,1)S(1)} %pad_maximum_fusion.2), channel_id=1, source_target_pairs={{0,1},{1,0},{2,3},{3,2},{4,5},{5,4},{6,7},{7,6},{8,9},{9,8},{10,11... | collective-permute-start | bytes 786440 | tf_op jit(solution)/shard_map/ppermute | solution.py:204
  26.4 3.8 %collective-permute-start.11 = (f32[8,384]{1,0:T(8,128)S(1)}, f32[8,384]{1,0:T(8,128)S(1)}, u32[]{:S(2)}, u32[]{:S(2)}) collective-permute-start(f32[8,384]{1,0:T(8,128)S(1)} %get-tuple-element.26.own), channel_id=1, source_target_pairs={{0,16},{16,0},{1,17},{17,1},{2,18},{18,2},{3,19},{19,3},{4,20},{20... | collective-permute-start | bytes 36872 | tf_op jit(solution)/shard_map/ppermute | solution.py:276
  27.0 6.8 %collective-permute-start.12 = (s16[6,128,128]{2,1,0:T(8,128)(2,1)S(1)}, s16[6,128,128]{2,1,0:T(8,128)(2,1)S(1)}, u32[]{:S(2)}, u32[]{:S(2)}) collective-permute-start(s16[6,128,128]{2,1,0:T(8,128)(2,1)S(1)} %get-tuple-element.29), channel_id=1, source_target_pairs={{0,16},{16,0},{1,17},{17,1},{2,18},{18,2},{3,19},{19,3},{4,20},{20... | collective-permute-start | bytes 589832 | tf_op jit(solution)/shard_map/ppermute | solution.py:277

commit v6 on v5

--- a/solution.py
+++ b/solution.py
@@ -229,16 +229,19 @@
     half = n_col // 2
     far = n_col - 2
     pieces = {0: a_eff}
-    for m, base in ((8, 0), (14, 0), (2, 0), (4, 0), (6, 0), (10, 8), (12, 8)):
-        pieces[m] = across(pieces[base], m ^ base)
-    late_even = [m for m in range(half + 2, far, 2)]
+    for m in (half, far, *range(2, half, 2)):
+        pieces[m] = across(a_eff, m)
+    late_even = list(range(half + 2, far, 2))
+    for m in late_even:
+        pieces[m] = across(pieces[half], m ^ half)
     late = range(late_even[0], late_even[-1] + 2)
+    batches = list(range(0, half - 2, 2)), [half - 2, half, far]
 
     def exchanged(batch):
         return [m | 1 for m in batch], across(jnp.concatenate([pieces[m] for m in batch], axis=0), 1)
 
     early = [([m], pieces[m]) for m in sorted(pieces) if m not in late]
-    early += [exchanged(batch) for batch in ((0, 2, 4), (6, 8, 14))]
+    early += [exchanged(batch) for batch in batches]
     *moved, b_other = lax.optimization_barrier((*[pieces[m] for m in late_even], b_other))
     pieces.update(zip(late_even, moved))
     last = [([m], pieces[m]) for m in late_even] + [exchanged(late_even)]
@@ -296,10 +299,15 @@
 
 def solution(mesh):
     n_row, n_col = mesh.shape["row"], mesh.shape["col"]
-    paired = n_row == 2 and n_col >= 16 and n_col & (n_col - 1) == 0
+
+    def body(a, b, *supports):
+        fits = n_row == 2 and n_col >= 16 and n_col & (n_col - 1) == 0
+        fits = fits and a.shape[1] == EDGE and 2 * b.shape[0] == n_col * EDGE
+        return (body_pair if fits else body_any)(a, b, *supports)
+
     placed = (P("row", "col"),) * 5 + (P("row", "col", None, None),)
     return jax.shard_map(
-        body_pair if paired else body_any,
+        body,
         mesh=mesh,
         in_specs=placed,
         out_specs=(P("row", "col"), P("row", "col")),

time: 34.7 us -> 34.7 us (level)
  no operation moved by 1% of the time
where the time goes in v6:
time: 34.7 us; the launch traced here: 34.6 us
  starting transfers between devices  17.9 us (52%)
  waiting for transfers between devices  10.2 us (29%)
  Pallas kernels  4.88 us (14%)
  other arithmetic  0.86 us (2%)
  between operations  0.71 us (2%)
    ppermute x10, starting transfers between devices, across(): return lax.ppermute(values, 'col', [(k, k ^ mask) for k in range(n_col)])  12.7 us
    ppermute x10, waiting for transfers between devices, across(): return lax.ppermute(values, 'col', [(k, k ^ mask) for k in range(n_col)])  6.54 us
    ppermute x1, starting transfers between devices, body_pair(): b_other = lax.ppermute(b_eff, 'row', swap)  3.03 us
    ppermute x1, waiting for transfers between devices, body_pair(): arrived = lax.ppermute(codes, 'row', swap)  1.96 us
    ppermute x1, waiting for transfers between devices, body_pair(): other_stats = lax.ppermute(stats, 'row', swap)  1.74 us
    pallas_call x1, Pallas kernels, body_pair(): pl.pallas_call(functools.partial(finish_kernel, 2 * rows, limit), out_sha...  1.56 us
    ppermute x1, starting transfers between devices, body_pair(): arrived = lax.ppermute(codes, 'row', swap)  1.52 us
    pallas_call x1, Pallas kernels, body_pair(): pl.pallas_call(mask_kernel, out_shape=(pltpu.VMEM(a.shape, a.dtype), pltp...  1.46 us
  transfers between devices with their start and end apart: 13, of which 10 were waited for; matrix products, arithmetic and copies ran while one was open for 0% of the time, Pallas kernels for 7%

profile of v6, /device:TPU:0, one launch (start us, length us, event | category | flops | bytes accessed | tf_op | source)
XLA Modules:
  0.0 34.6 jit_solution(12989929665196618354)
XLA Ops:
  0.6 1.5 %mask_factors.1 = (bf16[512,128]{1,0:T(8,128)(2,1)S(1)}, bf16[8,128,384]{2,1,0:T(8,128)(2,1)S(1)}, s32[1,128]{1,0:T(1,128)S(1)}) custom-call(s32[1,4]{1,0:T(1,128)} %bitcast.9, s32[3,8]{1,0:T(4,128)} %bitcast.8, s32[4,3]{1,0:T(4,128)} %retained.1, s32[1,12]{1,0:T(1,128)} %bitcast.10, bf16[512,128]{1,0:T(8,128)(2,1)} %a.1, bf16[1024,384]{1,0:T(8,128)(2,1)} %b.1), custom_call_target="tpu_custom_call" | custom-call | tf_op jit(solution)/shard_map/mask_factors/pallas_call | solution.py:210
  2.1 3.0 %collective-permute-start.3 = (bf16[8,128,384]{2,1,0:T(8,128)(2,1)S(1)}, bf16[8,128,384]{2,1,0:T(8,128)(2,1)S(1)}, u32[]{:S(2)}, u32[]{:S(2)}) collective-permute-start(bf16[8,128,384]{2,1,0:T(8,128)(2,1)S(1)} %get-tuple-element.18.b_own), channel_id=1, source_target_pairs={{0,16},{16,0},{1,17},{17,1},{2,18},{18,2},{3,19},{19,3},{4,20},{20... | collective-permute-start | bytes 2359304 | tf_op jit(solution)/shard_map/ppermute | solution.py:228
  5.1 1.5 %collective-permute-start.4 = (bf16[512,128]{1,0:T(8,128)(2,1)S(1)}, bf16[512,128]{1,0:T(8,128)(2,1)S(1)}, u32[]{:S(2)}, u32[]{:S(2)}) collective-permute-start(bf16[512,128]{1,0:T(8,128)(2,1)S(1)} %get-tuple-element.19.refs_0_), channel_id=1, source_target_pairs={{0,2},{1,3},{2,0},{3,1},{4,6},{5,7},{6,4},{7,5},{8,10},{9,11},{10,... | collective-permute-start | bytes 393224 | tf_op jit(solution)/shard_map/ppermute | solution.py:204
  6.6 1.6 %collective-permute-start.5 = (bf16[512,128]{1,0:T(8,128)(2,1)S(1)}, bf16[512,128]{1,0:T(8,128)(2,1)S(1)}, u32[]{:S(2)}, u32[]{:S(2)}) collective-permute-start(bf16[512,128]{1,0:T(8,128)(2,1)S(1)} %get-tuple-element.19.refs_0_), channel_id=1, source_target_pairs={{0,4},{1,5},{2,6},{3,7},{4,0},{5,1},{6,2},{7,3},{8,12},{9,13},{10,... | collective-permute-start | bytes 393224 | tf_op jit(solution)/shard_map/ppermute | solution.py:204
  8.2 2.6 %collective-permute-start = (bf16[512,128]{1,0:T(8,128)(2,1)S(1)}, bf16[512,128]{1,0:T(8,128)(2,1)S(1)}, u32[]{:S(2)}, u32[]{:S(2)}) collective-permute-start(bf16[512,128]{1,0:T(8,128)(2,1)S(1)} %get-tuple-element.19.refs_0_), channel_id=1, source_target_pairs={{0,8},{1,9},{2,10},{3,11},{4,12},{5,13},{6,14},{7,15},{8,0},{9,1},... | collective-permute-start | bytes 393224 | tf_op jit(solution)/shard_map/ppermute | solution.py:204
  10.8 0.4 %collective-permute-start.6 = (bf16[512,128]{1,0:T(8,128)(2,1)S(1)}, bf16[512,128]{1,0:T(8,128)(2,1)S(1)}, u32[]{:S(2)}, u32[]{:S(2)}) collective-permute-start(bf16[512,128]{1,0:T(8,128)(2,1)S(1)} %get-tuple-element.19.refs_0_), channel_id=1, source_target_pairs={{0,6},{1,7},{2,4},{3,5},{4,2},{5,3},{6,0},{7,1},{8,14},{9,15},{10,... | collective-permute-start | bytes 393224 | tf_op jit(solution)/shard_map/ppermute | solution.py:204
  11.2 0.0 collective-permute-done.4.refs_1_
  11.2 3.4 %collective-permute-start.7 = (bf16[512,128]{1,0:T(8,128)(2,1)S(1)}, bf16[512,128]{1,0:T(8,128)(2,1)S(1)}, u32[]{:S(2)}, u32[]{:S(2)}) collective-permute-start(bf16[512,128]{1,0:T(8,128)(2,1)S(1)} %get-tuple-element.19.refs_0_), channel_id=1, source_target_pairs={{0,14},{1,15},{2,12},{3,13},{4,10},{5,11},{6,8},{7,9},{8,6},{9,7},... | collective-permute-start | bytes 393224 | tf_op jit(solution)/shard_map/ppermute | solution.py:204
  14.6 0.1 collective-permute-done.5.refs_2_
  14.7 0.1 collective-permute-start.8
  14.8 1.2 %collective-permute-done.refs_4_ = bf16[512,128]{1,0:T(8,128)(2,1)S(1)} collective-permute-done((bf16[512,128]{1,0:T(8,128)(2,1)S(1)}, bf16[512,128]{1,0:T(8,128)(2,1)S(1)}, u32[]{:S(2)}, u32[]{:S(2)}) %collective-permute-start) | collective-permute-done | bytes 131104 | tf_op jit(solution)/shard_map/ppermute | solution.py:204
  16.0 0.5 %collective-permute-start.1 = (bf16[512,128]{1,0:T(8,128)(2,1)S(1)}, bf16[512,128]{1,0:T(8,128)(2,1)S(1)}, u32[]{:S(2)}, u32[]{:S(2)}) collective-permute-start(bf16[512,128]{1,0:T(8,128)(2,1)S(1)} %collective-permute-done.refs_4_), channel_id=1, source_target_pairs={{0,2},{1,3},{2,0},{3,1},{4,6},{5,7},{6,4},{7,5},{8,10},{9,11},{10,... | collective-permute-start | bytes 393224 | tf_op jit(solution)/shard_map/ppermute | solution.py:204
  16.5 1.0 %collective-permute-done.6.refs_3_ = bf16[512,128]{1,0:T(8,128)(2,1)S(1)} collective-permute-done((bf16[512,128]{1,0:T(8,128)(2,1)S(1)}, bf16[512,128]{1,0:T(8,128)(2,1)S(1)}, u32[]{:S(2)}, u32[]{:S(2)}) %collective-permute-start.6) | collective-permute-done | bytes 131104 | tf_op jit(solution)/shard_map/ppermute | solution.py:204
  17.6 2.5 %collective-permute-start.2 = (bf16[512,128]{1,0:T(8,128)(2,1)S(1)}, bf16[512,128]{1,0:T(8,128)(2,1)S(1)}, u32[]{:S(2)}, u32[]{:S(2)}) collective-permute-start(bf16[512,128]{1,0:T(8,128)(2,1)S(1)} %collective-permute-done.refs_4_), channel_id=1, source_target_pairs={{0,4},{1,5},{2,6},{3,7},{4,0},{5,1},{6,2},{7,3},{8,12},{9,13},{10,... | collective-permute-start | bytes 393224 | tf_op jit(solution)/shard_map/ppermute | solution.py:204
  20.1 2.3 %collective-permute-done.7.refs_5_ = bf16[512,128]{1,0:T(8,128)(2,1)S(1)} collective-permute-done((bf16[512,128]{1,0:T(8,128)(2,1)S(1)}, bf16[512,128]{1,0:T(8,128)(2,1)S(1)}, u32[]{:S(2)}, u32[]{:S(2)}) %collective-permute-start.7) | collective-permute-done | bytes 131104 | tf_op jit(solution)/shard_map/ppermute | solution.py:204
  22.4 0.1 collective-permute-start.9
  22.5 0.7 %collective-permute-done.1.refs_0_ = bf16[512,128]{1,0:T(8,128)(2,1)S(1)} collective-permute-done((bf16[512,128]{1,0:T(8,128)(2,1)S(1)}, bf16[512,128]{1,0:T(8,128)(2,1)S(1)}, u32[]{:S(2)}, u32[]{:S(2)}) %collective-permute-start.1) | collective-permute-done | bytes 131104 | tf_op jit(solution)/shard_map/ppermute | solution.py:204
  23.2 0.7 %collective-permute-done.2.refs_1_ = bf16[512,128]{1,0:T(8,128)(2,1)S(1)} collective-permute-done((bf16[512,128]{1,0:T(8,128)(2,1)S(1)}, bf16[512,128]{1,0:T(8,128)(2,1)S(1)}, u32[]{:S(2)}, u32[]{:S(2)}) %collective-permute-start.2) | collective-permute-done | bytes 131104 | tf_op jit(solution)/shard_map/ppermute | solution.py:204
  23.9 0.0 collective-permute-done.3.b_other
  23.9 0.1 collective-permute-start.10
  24.0 0.0 collective-permute-done.8.refs_6_
  24.0 0.2 collective-permute-done.9.refs_7_
  24.2 1.0 %gather_product.1 = (f32[512,384]{1,0:T(8,128)S(1)}, bf16[512,384]{1,0:T(8,128)(2,1)S(1)}) custom-call(bf16[8,128,384]{2,1,0:T(8,128)(2,1)S(1)} %get-tuple-element.18.b_own, bf16[8,128,384]{2,1,0:T(8,128)(2,1)S(1)} %collective-permute-done.3.b_other, bf16[512,128]{1,0:T(8,128)(2,1)S(1)} %get-tuple-element.19.refs_0_, ...), custom_call_target="tpu_custom_call" | custom-call | flops 805306368 | bytes 8388608 | tf_op jit(solution)/shard_map/gather_product/pallas_call | solution.py:249
  25.2 0.3 collective-permute-done.10.refs_2_
  25.5 0.9 %inflate.1 = (f32[512,384]{1,0:T(8,128)S(1)}, f32[8,384]{1,0:T(8,128)S(1)}, s16[6,128,128]{2,1,0:T(8,128)(2,1)S(1)}) custom-call(s32[1,128]{1,0:T(1,128)S(1)} %get-tuple-element.17.ints_far.ints, f32[512,384]{1,0:T(8,128)S(1)} %get-tuple-element.21.part, bf16[512,384]{1,0:T(8,128)(2,1)S(1)} %get-tuple-element.22.b_late, ...), custom_call_target="tpu_custom_call" | custom-call | tf_op jit(solution)/shard_map/inflate/pallas_call | solution.py:265
  26.4 0.6 %collective-permute-start.11 = (f32[8,384]{1,0:T(8,128)S(1)}, f32[8,384]{1,0:T(8,128)S(1)}, u32[]{:S(2)}, u32[]{:S(2)}) collective-permute-start(f32[8,384]{1,0:T(8,128)S(1)} %get-tuple-element.26.own), channel_id=1, source_target_pairs={{0,16},{16,0},{1,17},{17,1},{2,18},{18,2},{3,19},{19,3},{4,20},{20... | collective-permute-start | bytes 36872 | tf_op jit(solution)/shard_map/ppermute | solution.py:279
  27.0 1.5 %collective-permute-start.12 = (s16[6,128,128]{2,1,0:T(8,128)(2,1)S(1)}, s16[6,128,128]{2,1,0:T(8,128)(2,1)S(1)}, u32[]{:S(2)}, u32[]{:S(2)}) collective-permute-start(s16[6,128,128]{2,1,0:T(8,128)(2,1)S(1)} %get-tuple-element.29), channel_id=1, source_target_pairs={{0,16},{16,0},{1,17},{17,1},{2,18},{18,2},{3,19},{19,3},{4,20},{20... | collective-permute-start | bytes 589832 | tf_op jit(solution)/shard_map/ppermute | solution.py:280
  28.5 1.7 %collective-permute-done.11.other = f32[8,384]{1,0:T(8,128)S(1)} collective-permute-done((f32[8,384]{1,0:T(8,128)S(1)}, f32[8,384]{1,0:T(8,128)S(1)}, u32[]{:S(2)}, u32[]{:S(2)}) %collective-permute-start.11) | collective-permute-done | bytes 12320 | tf_op jit(solution)/shard_map/ppermute | solution.py:279
  30.3 1.6 %finish.1 = (bf16[512,384]{1,0:T(8,128)(2,1)}, bf16[12,128,128]{2,1,0:T(8,128)(2,1)}, f32[6,1,128]{2,1,0:T(1,128)S(1)}, f32[6,1,128]{2,1,0:T(1,128)S(1)}) custom-call(s32[1,128]{1,0:T(1,128)S(1)} %get-tuple-element.17.ints_far.ints, f32[512,384]{1,0:T(8,128)S(1)} %get-tuple-element.25.product, f32[8,384]{1,0:T(8,128)S(1)} %get-tuple-element.26.own, ...), custom_call_target="tpu_custom_call" | custom-call | tf_op jit(solution)/shard_map/finish/pallas_call | solution.py:281
  31.8 2.0 %collective-permute-done.12 = s16[6,128,128]{2,1,0:T(8,128)(2,1)S(1)} collective-permute-done((s16[6,128,128]{2,1,0:T(8,128)(2,1)S(1)}, s16[6,128,128]{2,1,0:T(8,128)(2,1)S(1)}, u32[]{:S(2)}, u32[]{:S(2)}) %collective-permute-start.12) | collective-permute-done | bytes 196640 | tf_op jit(solution)/shard_map/ppermute | solution.py:280
  33.8 0.8 %fusion = bf16[12,128,128]{2,1,0:T(8,128)(2,1)} fusion(bf16[12,128,128]{2,1,0:T(8,128)(2,1)} %get-tuple-element.28, s32[]{:T(128)S(6)} %select_n.3, s16[6,128,128]{2,1,0:T(8,128)(2,1)S(1)} %collective-permute-done.12, f32[6,128]{1,0:T(8,128)S(1)} %get-tuple-element.32, f32[6,128]{1,0:T(8,128)S(1)} %get-tuple-element.33), kind=kLoop, calls=%fused_computation.4 | loop fusion | flops 589824 | bytes 399364 | tf_op jit(solution)/shard_map/dynamic_update_slice | solution.py:296
  (4 shorter events, 0.1 us)
Async XLA Ops:
  2.1 21.8 %collective-permute-start.3 = (bf16[8,128,384]{2,1,0:T(8,128)(2,1)S(1)}, bf16[8,128,384]{2,1,0:T(8,128)(2,1)S(1)}, u32[]{:S(2)}, u32[]{:S(2)}) collective-permute-start(bf16[8,128,384]{2,1,0:T(8,128)(2,1)S(1)} %get-tuple-element.18.b_own), channel_id=1, source_target_pairs={{0,16},{16,0},{1,17},{17,1},{2,18},{18,2},{3,19},{19,3},{4,20},{20... | collective-permute-start | bytes 2359304 | tf_op jit(solution)/shard_map/ppermute | solution.py:228
  5.1 6.1 %collective-permute-start.4 = (bf16[512,128]{1,0:T(8,128)(2,1)S(1)}, bf16[512,128]{1,0:T(8,128)(2,1)S(1)}, u32[]{:S(2)}, u32[]{:S(2)}) collective-permute-start(bf16[512,128]{1,0:T(8,128)(2,1)S(1)} %get-tuple-element.19.refs_0_), channel_id=1, source_target_pairs={{0,2},{1,3},{2,0},{3,1},{4,6},{5,7},{6,4},{7,5},{8,10},{9,11},{10,... | collective-permute-start | bytes 393224 | tf_op jit(solution)/shard_map/ppermute | solution.py:204
  6.6 8.1 %collective-permute-start.5 = (bf16[512,128]{1,0:T(8,128)(2,1)S(1)}, bf16[512,128]{1,0:T(8,128)(2,1)S(1)}, u32[]{:S(2)}, u32[]{:S(2)}) collective-permute-start(bf16[512,128]{1,0:T(8,128)(2,1)S(1)} %get-tuple-element.19.refs_0_), channel_id=1, source_target_pairs={{0,4},{1,5},{2,6},{3,7},{4,0},{5,1},{6,2},{7,3},{8,12},{9,13},{10,... | collective-permute-start | bytes 393224 | tf_op jit(solution)/shard_map/ppermute | solution.py:204
  8.2 7.8 %collective-permute-start = (bf16[512,128]{1,0:T(8,128)(2,1)S(1)}, bf16[512,128]{1,0:T(8,128)(2,1)S(1)}, u32[]{:S(2)}, u32[]{:S(2)}) collective-permute-start(bf16[512,128]{1,0:T(8,128)(2,1)S(1)} %get-tuple-element.19.refs_0_), channel_id=1, source_target_pairs={{0,8},{1,9},{2,10},{3,11},{4,12},{5,13},{6,14},{7,15},{8,0},{9,1},... | collective-permute-start | bytes 393224 | tf_op jit(solution)/shard_map/ppermute | solution.py:204
  10.8 6.8 %collective-permute-start.6 = (bf16[512,128]{1,0:T(8,128)(2,1)S(1)}, bf16[512,128]{1,0:T(8,128)(2,1)S(1)}, u32[]{:S(2)}, u32[]{:S(2)}) collective-permute-start(bf16[512,128]{1,0:T(8,128)(2,1)S(1)} %get-tuple-element.19.refs_0_), channel_id=1, source_target_pairs={{0,6},{1,7},{2,4},{3,5},{4,2},{5,3},{6,0},{7,1},{8,14},{9,15},{10,... | collective-permute-start | bytes 393224 | tf_op jit(solution)/shard_map/ppermute | solution.py:204
  11.2 11.2 %collective-permute-start.7 = (bf16[512,128]{1,0:T(8,128)(2,1)S(1)}, bf16[512,128]{1,0:T(8,128)(2,1)S(1)}, u32[]{:S(2)}, u32[]{:S(2)}) collective-permute-start(bf16[512,128]{1,0:T(8,128)(2,1)S(1)} %get-tuple-element.19.refs_0_), channel_id=1, source_target_pairs={{0,14},{1,15},{2,12},{3,13},{4,10},{5,11},{6,8},{7,9},{8,6},{9,7},... | collective-permute-start | bytes 393224 | tf_op jit(solution)/shard_map/ppermute | solution.py:204
  14.7 9.3 %collective-permute-start.8 = (bf16[1536,128]{1,0:T(8,128)(2,1)S(1)}, bf16[1536,128]{1,0:T(8,128)(2,1)S(1)}, u32[]{:S(2)}, u32[]{:S(2)}) collective-permute-start(bf16[1536,128]{1,0:T(8,128)(2,1)S(1)} %pad_maximum_fusion), channel_id=1, source_target_pairs={{0,1},{1,0},{2,3},{3,2},{4,5},{5,4},{6,7},{7,6},{8,9},{9,8},{10,11... | collective-permute-start | bytes 1179656 | tf_op jit(solution)/shard_map/ppermute | solution.py:204
  16.0 7.2 %collective-permute-start.1 = (bf16[512,128]{1,0:T(8,128)(2,1)S(1)}, bf16[512,128]{1,0:T(8,128)(2,1)S(1)}, u32[]{:S(2)}, u32[]{:S(2)}) collective-permute-start(bf16[512,128]{1,0:T(8,128)(2,1)S(1)} %collective-permute-done.refs_4_), channel_id=1, source_target_pairs={{0,2},{1,3},{2,0},{3,1},{4,6},{5,7},{6,4},{7,5},{8,10},{9,11},{10,... | collective-permute-start | bytes 393224 | tf_op jit(solution)/shard_map/ppermute | solution.py:204
  17.6 6.3 %collective-permute-start.2 = (bf16[512,128]{1,0:T(8,128)(2,1)S(1)}, bf16[512,128]{1,0:T(8,128)(2,1)S(1)}, u32[]{:S(2)}, u32[]{:S(2)}) collective-permute-start(bf16[512,128]{1,0:T(8,128)(2,1)S(1)} %collective-permute-done.refs_4_), channel_id=1, source_target_pairs={{0,4},{1,5},{2,6},{3,7},{4,0},{5,1},{6,2},{7,3},{8,12},{9,13},{10,... | collective-permute-start | bytes 393224 | tf_op jit(solution)/shard_map/ppermute | solution.py:204
  22.4 1.8 %collective-permute-start.9 = (bf16[1536,128]{1,0:T(8,128)(2,1)S(1)}, bf16[1536,128]{1,0:T(8,128)(2,1)S(1)}, u32[]{:S(2)}, u32[]{:S(2)}) collective-permute-start(bf16[1536,128]{1,0:T(8,128)(2,1)S(1)} %pad_maximum_fusion.1), channel_id=1, source_target_pairs={{0,1},{1,0},{2,3},{3,2},{4,5},{5,4},{6,7},{7,6},{8,9},{9,8},{10,11... | collective-permute-start | bytes 1179656 | tf_op jit(solution)/shard_map/ppermute | solution.py:204
  23.9 1.6 %collective-permute-start.10 = (bf16[1024,128]{1,0:T(8,128)(2,1)S(1)}, bf16[1024,128]{1,0:T(8,128)(2,1)S(1)}, u32[]{:S(2)}, u32[]{:S(2)}) collective-permute-start(bf16[1024,128]{1,0:T(8,128)(2,1)S(1)} %pad_maximum_fusion.2), channel_id=1, source_target_pairs={{0,1},{1,0},{2,3},{3,2},{4,5},{5,4},{6,7},{7,6},{8,9},{9,8},{10,11... | collective-permute-start | bytes 786440 | tf_op jit(solution)/shard_map/ppermute | solution.py:204
  26.4 3.8 %collective-permute-start.11 = (f32[8,384]{1,0:T(8,128)S(1)}, f32[8,384]{1,0:T(8,128)S(1)}, u32[]{:S(2)}, u32[]{:S(2)}) collective-permute-start(f32[8,384]{1,0:T(8,128)S(1)} %get-tuple-element.26.own), channel_id=1, source_target_pairs={{0,16},{16,0},{1,17},{17,1},{2,18},{18,2},{3,19},{19,3},{4,20},{20... | collective-permute-start | bytes 36872 | tf_op jit(solution)/shard_map/ppermute | solution.py:279
  27.0 6.8 %collective-permute-start.12 = (s16[6,128,128]{2,1,0:T(8,128)(2,1)S(1)}, s16[6,128,128]{2,1,0:T(8,128)(2,1)S(1)}, u32[]{:S(2)}, u32[]{:S(2)}) collective-permute-start(s16[6,128,128]{2,1,0:T(8,128)(2,1)S(1)} %get-tuple-element.29), channel_id=1, source_target_pairs={{0,16},{16,0},{1,17},{17,1},{2,18},{18,2},{3,19},{19,3},{4,20},{20... | collective-permute-start | bytes 589832 | tf_op jit(solution)/shard_map/ppermute | solution.py:280

commit v7 on v6

--- a/solution.py
+++ b/solution.py
@@ -127,7 +127,10 @@
     rows, cols = part.shape[0] // EDGE, part.shape[1] // EDGE
     count = rows * cols
     a = side_by_side(pieces, groups, part.shape[0])
-    whole = part[...] + jnp.dot(a, b_late[...], preferred_element_type=jnp.float32)
+    pairs = []
+    for at in range(0, cols, 2):
+        lanes = slice(at * EDGE, min(at + 2, cols) * EDGE)
+        pairs.append(part[:, lanes] + jnp.dot(a, b_late[:, lanes], preferred_element_type=jnp.float32))
     lookup.wait()
     tops = []
     for c in range(cols):
@@ -135,7 +138,8 @@
         total = top = None
         for r in range(rows):
             keep = ints[0, r * cols + c].astype(jnp.float32)
-            tile = jnp.abs(whole[r * EDGE:(r + 1) * EDGE, c * EDGE:(c + 1) * EDGE]) * keep
+            tile = pairs[c // 2][r * EDGE:(r + 1) * EDGE, c % 2 * EDGE:(c % 2 + 1) * EDGE]
+            tile = jnp.abs(tile) * keep
             product[pl.ds(r * EDGE, EDGE), lanes] = tile
             stacked = tile.reshape(EDGE // 8, 8, EDGE)
             sums, peak = jnp.sum(stacked * stacked, axis=0), jnp.max(stacked, axis=0)

time: 34.7 us -> 34.7 us (level)
  no operation moved by 1% of the time
where the time goes in v7:
time: 34.7 us; the launch traced here: 34.6 us
  starting transfers between devices  17.9 us (52%)
  waiting for transfers between devices  10.2 us (29%)
  Pallas kernels  4.88 us (14%)
  other arithmetic  0.86 us (2%)
  between operations  0.71 us (2%)
    ppermute x10, starting transfers between devices, across(): return lax.ppermute(values, 'col', [(k, k ^ mask) for k in range(n_col)])  12.7 us
    ppermute x10, waiting for transfers between devices, across(): return lax.ppermute(values, 'col', [(k, k ^ mask) for k in range(n_col)])  6.54 us
    ppermute x1, starting transfers between devices, body_pair(): b_other = lax.ppermute(b_eff, 'row', swap)  3.03 us
    ppermute x1, waiting for transfers between devices, body_pair(): arrived = lax.ppermute(codes, 'row', swap)  1.96 us
    ppermute x1, waiting for transfers between devices, body_pair(): other_stats = lax.ppermute(stats, 'row', swap)  1.74 us
    pallas_call x1, Pallas kernels, body_pair(): pl.pallas_call(functools.partial(finish_kernel, 2 * rows, limit), out_sha...  1.56 us
    ppermute x1, starting transfers between devices, body_pair(): arrived = lax.ppermute(codes, 'row', swap)  1.54 us
    pallas_call x1, Pallas kernels, body_pair(): pl.pallas_call(mask_kernel, out_shape=(pltpu.VMEM(a.shape, a.dtype), pltp...  1.46 us
  transfers between devices with their start and end apart: 13, of which 10 were waited for; matrix products, arithmetic and copies ran while one was open for 0% of the time, Pallas kernels for 7%

profile of v7, /device:TPU:0, one launch (start us, length us, event | category | flops | bytes accessed | tf_op | source)
XLA Modules:
  0.0 34.6 jit_solution(12989929665196618354)
XLA Ops:
  0.6 1.5 %mask_factors.1 = (bf16[512,128]{1,0:T(8,128)(2,1)S(1)}, bf16[8,128,384]{2,1,0:T(8,128)(2,1)S(1)}, s32[1,128]{1,0:T(1,128)S(1)}) custom-call(s32[1,4]{1,0:T(1,128)} %bitcast.9, s32[3,8]{1,0:T(4,128)} %bitcast.8, s32[4,3]{1,0:T(4,128)} %retained.1, s32[1,12]{1,0:T(1,128)} %bitcast.10, bf16[512,128]{1,0:T(8,128)(2,1)} %a.1, bf16[1024,384]{1,0:T(8,128)(2,1)} %b.1), custom_call_target="tpu_custom_call" | custom-call | tf_op jit(solution)/shard_map/mask_factors/pallas_call | solution.py:214
  2.1 3.0 %collective-permute-start.3 = (bf16[8,128,384]{2,1,0:T(8,128)(2,1)S(1)}, bf16[8,128,384]{2,1,0:T(8,128)(2,1)S(1)}, u32[]{:S(2)}, u32[]{:S(2)}) collective-permute-start(bf16[8,128,384]{2,1,0:T(8,128)(2,1)S(1)} %get-tuple-element.18.b_own), channel_id=1, source_target_pairs={{0,16},{16,0},{1,17},{17,1},{2,18},{18,2},{3,19},{19,3},{4,20},{20... | collective-permute-start | bytes 2359304 | tf_op jit(solution)/shard_map/ppermute | solution.py:232
  5.1 1.5 %collective-permute-start.4 = (bf16[512,128]{1,0:T(8,128)(2,1)S(1)}, bf16[512,128]{1,0:T(8,128)(2,1)S(1)}, u32[]{:S(2)}, u32[]{:S(2)}) collective-permute-start(bf16[512,128]{1,0:T(8,128)(2,1)S(1)} %get-tuple-element.19.refs_0_), channel_id=1, source_target_pairs={{0,2},{1,3},{2,0},{3,1},{4,6},{5,7},{6,4},{7,5},{8,10},{9,11},{10,... | collective-permute-start | bytes 393224 | tf_op jit(solution)/shard_map/ppermute | solution.py:208
  6.6 1.6 %collective-permute-start.5 = (bf16[512,128]{1,0:T(8,128)(2,1)S(1)}, bf16[512,128]{1,0:T(8,128)(2,1)S(1)}, u32[]{:S(2)}, u32[]{:S(2)}) collective-permute-start(bf16[512,128]{1,0:T(8,128)(2,1)S(1)} %get-tuple-element.19.refs_0_), channel_id=1, source_target_pairs={{0,4},{1,5},{2,6},{3,7},{4,0},{5,1},{6,2},{7,3},{8,12},{9,13},{10,... | collective-permute-start | bytes 393224 | tf_op jit(solution)/shard_map/ppermute | solution.py:208
  8.2 2.6 %collective-permute-start = (bf16[512,128]{1,0:T(8,128)(2,1)S(1)}, bf16[512,128]{1,0:T(8,128)(2,1)S(1)}, u32[]{:S(2)}, u32[]{:S(2)}) collective-permute-start(bf16[512,128]{1,0:T(8,128)(2,1)S(1)} %get-tuple-element.19.refs_0_), channel_id=1, source_target_pairs={{0,8},{1,9},{2,10},{3,11},{4,12},{5,13},{6,14},{7,15},{8,0},{9,1},... | collective-permute-start | bytes 393224 | tf_op jit(solution)/shard_map/ppermute | solution.py:208
  10.8 0.4 %collective-permute-start.6 = (bf16[512,128]{1,0:T(8,128)(2,1)S(1)}, bf16[512,128]{1,0:T(8,128)(2,1)S(1)}, u32[]{:S(2)}, u32[]{:S(2)}) collective-permute-start(bf16[512,128]{1,0:T(8,128)(2,1)S(1)} %get-tuple-element.19.refs_0_), channel_id=1, source_target_pairs={{0,6},{1,7},{2,4},{3,5},{4,2},{5,3},{6,0},{7,1},{8,14},{9,15},{10,... | collective-permute-start | bytes 393224 | tf_op jit(solution)/shard_map/ppermute | solution.py:208
  11.2 0.0 collective-permute-done.4.refs_1_
  11.2 3.4 %collective-permute-start.7 = (bf16[512,128]{1,0:T(8,128)(2,1)S(1)}, bf16[512,128]{1,0:T(8,128)(2,1)S(1)}, u32[]{:S(2)}, u32[]{:S(2)}) collective-permute-start(bf16[512,128]{1,0:T(8,128)(2,1)S(1)} %get-tuple-element.19.refs_0_), channel_id=1, source_target_pairs={{0,14},{1,15},{2,12},{3,13},{4,10},{5,11},{6,8},{7,9},{8,6},{9,7},... | collective-permute-start | bytes 393224 | tf_op jit(solution)/shard_map/ppermute | solution.py:208
  14.6 0.1 collective-permute-done.5.refs_2_
  14.7 0.1 collective-permute-start.8
  14.8 1.2 %collective-permute-done.refs_4_ = bf16[512,128]{1,0:T(8,128)(2,1)S(1)} collective-permute-done((bf16[512,128]{1,0:T(8,128)(2,1)S(1)}, bf16[512,128]{1,0:T(8,128)(2,1)S(1)}, u32[]{:S(2)}, u32[]{:S(2)}) %collective-permute-start) | collective-permute-done | bytes 131104 | tf_op jit(solution)/shard_map/ppermute | solution.py:208
  16.0 0.5 %collective-permute-start.1 = (bf16[512,128]{1,0:T(8,128)(2,1)S(1)}, bf16[512,128]{1,0:T(8,128)(2,1)S(1)}, u32[]{:S(2)}, u32[]{:S(2)}) collective-permute-start(bf16[512,128]{1,0:T(8,128)(2,1)S(1)} %collective-permute-done.refs_4_), channel_id=1, source_target_pairs={{0,2},{1,3},{2,0},{3,1},{4,6},{5,7},{6,4},{7,5},{8,10},{9,11},{10,... | collective-permute-start | bytes 393224 | tf_op jit(solution)/shard_map/ppermute | solution.py:208
  16.5 1.0 %collective-permute-done.6.refs_3_ = bf16[512,128]{1,0:T(8,128)(2,1)S(1)} collective-permute-done((bf16[512,128]{1,0:T(8,128)(2,1)S(1)}, bf16[512,128]{1,0:T(8,128)(2,1)S(1)}, u32[]{:S(2)}, u32[]{:S(2)}) %collective-permute-start.6) | collective-permute-done | bytes 131104 | tf_op jit(solution)/shard_map/ppermute | solution.py:208
  17.6 2.5 %collective-permute-start.2 = (bf16[512,128]{1,0:T(8,128)(2,1)S(1)}, bf16[512,128]{1,0:T(8,128)(2,1)S(1)}, u32[]{:S(2)}, u32[]{:S(2)}) collective-permute-start(bf16[512,128]{1,0:T(8,128)(2,1)S(1)} %collective-permute-done.refs_4_), channel_id=1, source_target_pairs={{0,4},{1,5},{2,6},{3,7},{4,0},{5,1},{6,2},{7,3},{8,12},{9,13},{10,... | collective-permute-start | bytes 393224 | tf_op jit(solution)/shard_map/ppermute | solution.py:208
  20.1 2.3 %collective-permute-done.7.refs_5_ = bf16[512,128]{1,0:T(8,128)(2,1)S(1)} collective-permute-done((bf16[512,128]{1,0:T(8,128)(2,1)S(1)}, bf16[512,128]{1,0:T(8,128)(2,1)S(1)}, u32[]{:S(2)}, u32[]{:S(2)}) %collective-permute-start.7) | collective-permute-done | bytes 131104 | tf_op jit(solution)/shard_map/ppermute | solution.py:208
  22.4 0.1 collective-permute-start.9
  22.5 0.7 %collective-permute-done.1.refs_0_ = bf16[512,128]{1,0:T(8,128)(2,1)S(1)} collective-permute-done((bf16[512,128]{1,0:T(8,128)(2,1)S(1)}, bf16[512,128]{1,0:T(8,128)(2,1)S(1)}, u32[]{:S(2)}, u32[]{:S(2)}) %collective-permute-start.1) | collective-permute-done | bytes 131104 | tf_op jit(solution)/shard_map/ppermute | solution.py:208
  23.2 0.7 %collective-permute-done.2.refs_1_ = bf16[512,128]{1,0:T(8,128)(2,1)S(1)} collective-permute-done((bf16[512,128]{1,0:T(8,128)(2,1)S(1)}, bf16[512,128]{1,0:T(8,128)(2,1)S(1)}, u32[]{:S(2)}, u32[]{:S(2)}) %collective-permute-start.2) | collective-permute-done | bytes 131104 | tf_op jit(solution)/shard_map/ppermute | solution.py:208
  23.9 0.0 collective-permute-done.3.b_other
  23.9 0.1 collective-permute-start.10
  24.0 0.0 collective-permute-done.8.refs_6_
  24.0 0.2 collective-permute-done.9.refs_7_
  24.2 1.0 %gather_product.1 = (f32[512,384]{1,0:T(8,128)S(1)}, bf16[512,384]{1,0:T(8,128)(2,1)S(1)}) custom-call(bf16[8,128,384]{2,1,0:T(8,128)(2,1)S(1)} %get-tuple-element.18.b_own, bf16[8,128,384]{2,1,0:T(8,128)(2,1)S(1)} %collective-permute-done.3.b_other, bf16[512,128]{1,0:T(8,128)(2,1)S(1)} %get-tuple-element.19.refs_0_, ...), custom_call_target="tpu_custom_call" | custom-call | flops 805306368 | bytes 8388608 | tf_op jit(solution)/shard_map/gather_product/pallas_call | solution.py:253
  25.2 0.3 collective-permute-done.10.refs_2_
  25.5 0.9 %inflate.1 = (f32[512,384]{1,0:T(8,128)S(1)}, f32[8,384]{1,0:T(8,128)S(1)}, s16[6,128,128]{2,1,0:T(8,128)(2,1)S(1)}) custom-call(s32[1,128]{1,0:T(1,128)S(1)} %get-tuple-element.17.ints_far.ints, f32[512,384]{1,0:T(8,128)S(1)} %get-tuple-element.21.part, bf16[512,384]{1,0:T(8,128)(2,1)S(1)} %get-tuple-element.22.b_late, ...), custom_call_target="tpu_custom_call" | custom-call | tf_op jit(solution)/shard_map/inflate/pallas_call | solution.py:269
  26.4 0.6 %collective-permute-start.11 = (f32[8,384]{1,0:T(8,128)S(1)}, f32[8,384]{1,0:T(8,128)S(1)}, u32[]{:S(2)}, u32[]{:S(2)}) collective-permute-start(f32[8,384]{1,0:T(8,128)S(1)} %get-tuple-element.26.own), channel_id=1, source_target_pairs={{0,16},{16,0},{1,17},{17,1},{2,18},{18,2},{3,19},{19,3},{4,20},{20... | collective-permute-start | bytes 36872 | tf_op jit(solution)/shard_map/ppermute | solution.py:283
  27.0 1.5 %collective-permute-start.12 = (s16[6,128,128]{2,1,0:T(8,128)(2,1)S(1)}, s16[6,128,128]{2,1,0:T(8,128)(2,1)S(1)}, u32[]{:S(2)}, u32[]{:S(2)}) collective-permute-start(s16[6,128,128]{2,1,0:T(8,128)(2,1)S(1)} %get-tuple-element.29), channel_id=1, source_target_pairs={{0,16},{16,0},{1,17},{17,1},{2,18},{18,2},{3,19},{19,3},{4,20},{20... | collective-permute-start | bytes 589832 | tf_op jit(solution)/shard_map/ppermute | solution.py:284
  28.5 1.7 %collective-permute-done.11.other = f32[8,384]{1,0:T(8,128)S(1)} collective-permute-done((f32[8,384]{1,0:T(8,128)S(1)}, f32[8,384]{1,0:T(8,128)S(1)}, u32[]{:S(2)}, u32[]{:S(2)}) %collective-permute-start.11) | collective-permute-done | bytes 12320 | tf_op jit(solution)/shard_map/ppermute | solution.py:283
  30.3 1.6 %finish.1 = (bf16[512,384]{1,0:T(8,128)(2,1)}, bf16[12,128,128]{2,1,0:T(8,128)(2,1)}, f32[6,1,128]{2,1,0:T(1,128)S(1)}, f32[6,1,128]{2,1,0:T(1,128)S(1)}) custom-call(s32[1,128]{1,0:T(1,128)S(1)} %get-tuple-element.17.ints_far.ints, f32[512,384]{1,0:T(8,128)S(1)} %get-tuple-element.25.product, f32[8,384]{1,0:T(8,128)S(1)} %get-tuple-element.26.own, ...), custom_call_target="tpu_custom_call" | custom-call | tf_op jit(solution)/shard_map/finish/pallas_call | solution.py:285
  31.8 2.0 %collective-permute-done.12 = s16[6,128,128]{2,1,0:T(8,128)(2,1)S(1)} collective-permute-done((s16[6,128,128]{2,1,0:T(8,128)(2,1)S(1)}, s16[6,128,128]{2,1,0:T(8,128)(2,1)S(1)}, u32[]{:S(2)}, u32[]{:S(2)}) %collective-permute-start.12) | collective-permute-done | bytes 196640 | tf_op jit(solution)/shard_map/ppermute | solution.py:284
  33.8 0.8 %fusion = bf16[12,128,128]{2,1,0:T(8,128)(2,1)} fusion(bf16[12,128,128]{2,1,0:T(8,128)(2,1)} %get-tuple-element.28, s32[]{:T(128)S(6)} %select_n.3, s16[6,128,128]{2,1,0:T(8,128)(2,1)S(1)} %collective-permute-done.12, f32[6,128]{1,0:T(8,128)S(1)} %get-tuple-element.32, f32[6,128]{1,0:T(8,128)S(1)} %get-tuple-element.33), kind=kLoop, calls=%fused_computation.4 | loop fusion | flops 589824 | bytes 399364 | tf_op jit(solution)/shard_map/dynamic_update_slice | solution.py:300
  (4 shorter events, 0.1 us)
Async XLA Ops:
  2.1 21.8 %collective-permute-start.3 = (bf16[8,128,384]{2,1,0:T(8,128)(2,1)S(1)}, bf16[8,128,384]{2,1,0:T(8,128)(2,1)S(1)}, u32[]{:S(2)}, u32[]{:S(2)}) collective-permute-start(bf16[8,128,384]{2,1,0:T(8,128)(2,1)S(1)} %get-tuple-element.18.b_own), channel_id=1, source_target_pairs={{0,16},{16,0},{1,17},{17,1},{2,18},{18,2},{3,19},{19,3},{4,20},{20... | collective-permute-start | bytes 2359304 | tf_op jit(solution)/shard_map/ppermute | solution.py:232
  5.1 6.1 %collective-permute-start.4 = (bf16[512,128]{1,0:T(8,128)(2,1)S(1)}, bf16[512,128]{1,0:T(8,128)(2,1)S(1)}, u32[]{:S(2)}, u32[]{:S(2)}) collective-permute-start(bf16[512,128]{1,0:T(8,128)(2,1)S(1)} %get-tuple-element.19.refs_0_), channel_id=1, source_target_pairs={{0,2},{1,3},{2,0},{3,1},{4,6},{5,7},{6,4},{7,5},{8,10},{9,11},{10,... | collective-permute-start | bytes 393224 | tf_op jit(solution)/shard_map/ppermute | solution.py:208
  6.6 8.1 %collective-permute-start.5 = (bf16[512,128]{1,0:T(8,128)(2,1)S(1)}, bf16[512,128]{1,0:T(8,128)(2,1)S(1)}, u32[]{:S(2)}, u32[]{:S(2)}) collective-permute-start(bf16[512,128]{1,0:T(8,128)(2,1)S(1)} %get-tuple-element.19.refs_0_), channel_id=1, source_target_pairs={{0,4},{1,5},{2,6},{3,7},{4,0},{5,1},{6,2},{7,3},{8,12},{9,13},{10,... | collective-permute-start | bytes 393224 | tf_op jit(solution)/shard_map/ppermute | solution.py:208
  8.2 7.8 %collective-permute-start = (bf16[512,128]{1,0:T(8,128)(2,1)S(1)}, bf16[512,128]{1,0:T(8,128)(2,1)S(1)}, u32[]{:S(2)}, u32[]{:S(2)}) collective-permute-start(bf16[512,128]{1,0:T(8,128)(2,1)S(1)} %get-tuple-element.19.refs_0_), channel_id=1, source_target_pairs={{0,8},{1,9},{2,10},{3,11},{4,12},{5,13},{6,14},{7,15},{8,0},{9,1},... | collective-permute-start | bytes 393224 | tf_op jit(solution)/shard_map/ppermute | solution.py:208
  10.8 6.8 %collective-permute-start.6 = (bf16[512,128]{1,0:T(8,128)(2,1)S(1)}, bf16[512,128]{1,0:T(8,128)(2,1)S(1)}, u32[]{:S(2)}, u32[]{:S(2)}) collective-permute-start(bf16[512,128]{1,0:T(8,128)(2,1)S(1)} %get-tuple-element.19.refs_0_), channel_id=1, source_target_pairs={{0,6},{1,7},{2,4},{3,5},{4,2},{5,3},{6,0},{7,1},{8,14},{9,15},{10,... | collective-permute-start | bytes 393224 | tf_op jit(solution)/shard_map/ppermute | solution.py:208
  11.2 11.2 %collective-permute-start.7 = (bf16[512,128]{1,0:T(8,128)(2,1)S(1)}, bf16[512,128]{1,0:T(8,128)(2,1)S(1)}, u32[]{:S(2)}, u32[]{:S(2)}) collective-permute-start(bf16[512,128]{1,0:T(8,128)(2,1)S(1)} %get-tuple-element.19.refs_0_), channel_id=1, source_target_pairs={{0,14},{1,15},{2,12},{3,13},{4,10},{5,11},{6,8},{7,9},{8,6},{9,7},... | collective-permute-start | bytes 393224 | tf_op jit(solution)/shard_map/ppermute | solution.py:208
  14.7 9.3 %collective-permute-start.8 = (bf16[1536,128]{1,0:T(8,128)(2,1)S(1)}, bf16[1536,128]{1,0:T(8,128)(2,1)S(1)}, u32[]{:S(2)}, u32[]{:S(2)}) collective-permute-start(bf16[1536,128]{1,0:T(8,128)(2,1)S(1)} %pad_maximum_fusion), channel_id=1, source_target_pairs={{0,1},{1,0},{2,3},{3,2},{4,5},{5,4},{6,7},{7,6},{8,9},{9,8},{10,11... | collective-permute-start | bytes 1179656 | tf_op jit(solution)/shard_map/ppermute | solution.py:208
  16.0 7.2 %collective-permute-start.1 = (bf16[512,128]{1,0:T(8,128)(2,1)S(1)}, bf16[512,128]{1,0:T(8,128)(2,1)S(1)}, u32[]{:S(2)}, u32[]{:S(2)}) collective-permute-start(bf16[512,128]{1,0:T(8,128)(2,1)S(1)} %collective-permute-done.refs_4_), channel_id=1, source_target_pairs={{0,2},{1,3},{2,0},{3,1},{4,6},{5,7},{6,4},{7,5},{8,10},{9,11},{10,... | collective-permute-start | bytes 393224 | tf_op jit(solution)/shard_map/ppermute | solution.py:208
  17.6 6.3 %collective-permute-start.2 = (bf16[512,128]{1,0:T(8,128)(2,1)S(1)}, bf16[512,128]{1,0:T(8,128)(2,1)S(1)}, u32[]{:S(2)}, u32[]{:S(2)}) collective-permute-start(bf16[512,128]{1,0:T(8,128)(2,1)S(1)} %collective-permute-done.refs_4_), channel_id=1, source_target_pairs={{0,4},{1,5},{2,6},{3,7},{4,0},{5,1},{6,2},{7,3},{8,12},{9,13},{10,... | collective-permute-start | bytes 393224 | tf_op jit(solution)/shard_map/ppermute | solution.py:208
  22.4 1.8 %collective-permute-start.9 = (bf16[1536,128]{1,0:T(8,128)(2,1)S(1)}, bf16[1536,128]{1,0:T(8,128)(2,1)S(1)}, u32[]{:S(2)}, u32[]{:S(2)}) collective-permute-start(bf16[1536,128]{1,0:T(8,128)(2,1)S(1)} %pad_maximum_fusion.1), channel_id=1, source_target_pairs={{0,1},{1,0},{2,3},{3,2},{4,5},{5,4},{6,7},{7,6},{8,9},{9,8},{10,11... | collective-permute-start | bytes 1179656 | tf_op jit(solution)/shard_map/ppermute | solution.py:208
  23.9 1.6 %collective-permute-start.10 = (bf16[1024,128]{1,0:T(8,128)(2,1)S(1)}, bf16[1024,128]{1,0:T(8,128)(2,1)S(1)}, u32[]{:S(2)}, u32[]{:S(2)}) collective-permute-start(bf16[1024,128]{1,0:T(8,128)(2,1)S(1)} %pad_maximum_fusion.2), channel_id=1, source_target_pairs={{0,1},{1,0},{2,3},{3,2},{4,5},{5,4},{6,7},{7,6},{8,9},{9,8},{10,11... | collective-permute-start | bytes 786440 | tf_op jit(solution)/shard_map/ppermute | solution.py:208
  26.4 3.8 %collective-permute-start.11 = (f32[8,384]{1,0:T(8,128)S(1)}, f32[8,384]{1,0:T(8,128)S(1)}, u32[]{:S(2)}, u32[]{:S(2)}) collective-permute-start(f32[8,384]{1,0:T(8,128)S(1)} %get-tuple-element.26.own), channel_id=1, source_target_pairs={{0,16},{16,0},{1,17},{17,1},{2,18},{18,2},{3,19},{19,3},{4,20},{20... | collective-permute-start | bytes 36872 | tf_op jit(solution)/shard_map/ppermute | solution.py:283
  27.0 6.8 %collective-permute-start.12 = (s16[6,128,128]{2,1,0:T(8,128)(2,1)S(1)}, s16[6,128,128]{2,1,0:T(8,128)(2,1)S(1)}, u32[]{:S(2)}, u32[]{:S(2)}) collective-permute-start(s16[6,128,128]{2,1,0:T(8,128)(2,1)S(1)} %get-tuple-element.29), channel_id=1, source_target_pairs={{0,16},{16,0},{1,17},{17,1},{2,18},{18,2},{3,19},{19,3},{4,20},{20... | collective-permute-start | bytes 589832 | tf_op jit(solution)/shard_map/ppermute | solution.py:284

commit v8 on v6

--- a/solution.py
+++ b/solution.py
@@ -56,6 +56,7 @@
 def mask_kernel(a_support, b_support, retained, targets, a, b, a_out, b_out, ints, keeps, a_local, b_local, sems):
     a_keep, b_keep, retained_local, targets_local = keeps
     rows, tiles, cols = a.shape[0] // EDGE, b.shape[0] // EDGE, b.shape[1] // EDGE
+    middle = tiles // 2 * EDGE
     copies = [
         pltpu.make_async_copy(source, local, sems.at[k])
         for k, (source, local) in enumerate(
@@ -63,9 +64,10 @@
                 (a_support, a_keep),
                 (b_support, b_keep),
                 (a, a_local),
-                (b, b_local),
+                (b.at[:middle, :], b_local.at[:middle, :]),
                 (retained, retained_local),
                 (targets, targets_local),
+                (b.at[middle:, :], b_local.at[middle:, :]),
             )
         )
     ]
@@ -80,6 +82,8 @@
     copies[1].wait()
     copies[3].wait()
     for q in range(tiles):
+        if q * EDGE == middle:
+            copies[6].wait()
         band = slice(q * EDGE, (q + 1) * EDGE)
         place = lax.bitwise_and(lax.bitwise_xor(j, q), tiles - 1)
         for c in range(cols):
@@ -220,7 +224,7 @@
             [SMEM(v.shape, jnp.int32) for v in (a_support.T, b_support.T, retained, targets)],
             VMEM(a.shape, a.dtype),
             VMEM(b.shape, b.dtype),
-            pltpu.SemaphoreType.DMA((6,)),
+            pltpu.SemaphoreType.DMA((7,)),
         ],
         compiler_params=pltpu.CompilerParams(vmem_limit_bytes=TIGHT),
         name="mask_factors",

time: 34.7 us -> 34.6 us (level)
  no operation moved by 1% of the time
where the time goes in v8:
time: 34.6 us; the launch traced here: 34.5 us
  starting transfers between devices  17.9 us (52%)
  waiting for transfers between devices  10.3 us (30%)
  Pallas kernels  4.78 us (14%)
  other arithmetic  0.86 us (2%)
  between operations  0.71 us (2%)
    ppermute x10, starting transfers between devices, across(): return lax.ppermute(values, 'col', [(k, k ^ mask) for k in range(n_col)])  12.7 us
    ppermute x10, waiting for transfers between devices, across(): return lax.ppermute(values, 'col', [(k, k ^ mask) for k in range(n_col)])  6.54 us
    ppermute x1, starting transfers between devices, body_pair(): b_other = lax.ppermute(b_eff, 'row', swap)  3.03 us
    ppermute x1, waiting for transfers between devices, body_pair(): arrived = lax.ppermute(codes, 'row', swap)  1.96 us
    ppermute x1, waiting for transfers between devices, body_pair(): other_stats = lax.ppermute(stats, 'row', swap)  1.74 us
    pallas_call x1, Pallas kernels, body_pair(): pl.pallas_call(functools.partial(finish_kernel, 2 * rows, limit), out_sha...  1.56 us
    ppermute x1, starting transfers between devices, body_pair(): arrived = lax.ppermute(codes, 'row', swap)  1.53 us
    pallas_call x1, Pallas kernels, body_pair(): pl.pallas_call(mask_kernel, out_shape=(pltpu.VMEM(a.shape, a.dtype), pltp...  1.37 us
  transfers between devices with their start and end apart: 13, of which 10 were waited for; matrix products, arithmetic and copies ran while one was open for 0% of the time, Pallas kernels for 7%

profile of v8, /device:TPU:0, one launch (start us, length us, event | category | flops | bytes accessed | tf_op | source)
XLA Modules:
  0.0 34.5 jit_solution(2876569686909260742)
XLA Ops:
  0.6 1.4 %mask_factors.1 = (bf16[512,128]{1,0:T(8,128)(2,1)S(1)}, bf16[8,128,384]{2,1,0:T(8,128)(2,1)S(1)}, s32[1,128]{1,0:T(1,128)S(1)}) custom-call(s32[1,4]{1,0:T(1,128)} %bitcast.9, s32[3,8]{1,0:T(4,128)} %bitcast.8, s32[4,3]{1,0:T(4,128)} %retained.1, s32[1,12]{1,0:T(1,128)} %bitcast.10, bf16[512,128]{1,0:T(8,128)(2,1)} %a.1, bf16[1024,384]{1,0:T(8,128)(2,1)} %b.1), custom_call_target="tpu_custom_call" | custom-call | tf_op jit(solution)/shard_map/mask_factors/pallas_call | solution.py:214
  2.0 3.0 %collective-permute-start.3 = (bf16[8,128,384]{2,1,0:T(8,128)(2,1)S(1)}, bf16[8,128,384]{2,1,0:T(8,128)(2,1)S(1)}, u32[]{:S(2)}, u32[]{:S(2)}) collective-permute-start(bf16[8,128,384]{2,1,0:T(8,128)(2,1)S(1)} %get-tuple-element.18.b_own), channel_id=1, source_target_pairs={{0,16},{16,0},{1,17},{17,1},{2,18},{18,2},{3,19},{19,3},{4,20},{20... | collective-permute-start | bytes 2359304 | tf_op jit(solution)/shard_map/ppermute | solution.py:232
  5.0 1.5 %collective-permute-start.4 = (bf16[512,128]{1,0:T(8,128)(2,1)S(1)}, bf16[512,128]{1,0:T(8,128)(2,1)S(1)}, u32[]{:S(2)}, u32[]{:S(2)}) collective-permute-start(bf16[512,128]{1,0:T(8,128)(2,1)S(1)} %get-tuple-element.19.refs_0_), channel_id=1, source_target_pairs={{0,2},{1,3},{2,0},{3,1},{4,6},{5,7},{6,4},{7,5},{8,10},{9,11},{10,... | collective-permute-start | bytes 393224 | tf_op jit(solution)/shard_map/ppermute | solution.py:208
  6.5 1.6 %collective-permute-start.5 = (bf16[512,128]{1,0:T(8,128)(2,1)S(1)}, bf16[512,128]{1,0:T(8,128)(2,1)S(1)}, u32[]{:S(2)}, u32[]{:S(2)}) collective-permute-start(bf16[512,128]{1,0:T(8,128)(2,1)S(1)} %get-tuple-element.19.refs_0_), channel_id=1, source_target_pairs={{0,4},{1,5},{2,6},{3,7},{4,0},{5,1},{6,2},{7,3},{8,12},{9,13},{10,... | collective-permute-start | bytes 393224 | tf_op jit(solution)/shard_map/ppermute | solution.py:208
  8.1 2.6 %collective-permute-start = (bf16[512,128]{1,0:T(8,128)(2,1)S(1)}, bf16[512,128]{1,0:T(8,128)(2,1)S(1)}, u32[]{:S(2)}, u32[]{:S(2)}) collective-permute-start(bf16[512,128]{1,0:T(8,128)(2,1)S(1)} %get-tuple-element.19.refs_0_), channel_id=1, source_target_pairs={{0,8},{1,9},{2,10},{3,11},{4,12},{5,13},{6,14},{7,15},{8,0},{9,1},... | collective-permute-start | bytes 393224 | tf_op jit(solution)/shard_map/ppermute | solution.py:208
  10.7 0.4 %collective-permute-start.6 = (bf16[512,128]{1,0:T(8,128)(2,1)S(1)}, bf16[512,128]{1,0:T(8,128)(2,1)S(1)}, u32[]{:S(2)}, u32[]{:S(2)}) collective-permute-start(bf16[512,128]{1,0:T(8,128)(2,1)S(1)} %get-tuple-element.19.refs_0_), channel_id=1, source_target_pairs={{0,6},{1,7},{2,4},{3,5},{4,2},{5,3},{6,0},{7,1},{8,14},{9,15},{10,... | collective-permute-start | bytes 393224 | tf_op jit(solution)/shard_map/ppermute | solution.py:208
  11.1 0.0 collective-permute-done.4.refs_1_
  11.1 3.4 %collective-permute-start.7 = (bf16[512,128]{1,0:T(8,128)(2,1)S(1)}, bf16[512,128]{1,0:T(8,128)(2,1)S(1)}, u32[]{:S(2)}, u32[]{:S(2)}) collective-permute-start(bf16[512,128]{1,0:T(8,128)(2,1)S(1)} %get-tuple-element.19.refs_0_), channel_id=1, source_target_pairs={{0,14},{1,15},{2,12},{3,13},{4,10},{5,11},{6,8},{7,9},{8,6},{9,7},... | collective-permute-start | bytes 393224 | tf_op jit(solution)/shard_map/ppermute | solution.py:208
  14.5 0.1 collective-permute-done.5.refs_2_
  14.6 0.1 collective-permute-start.8
  14.7 1.2 %collective-permute-done.refs_4_ = bf16[512,128]{1,0:T(8,128)(2,1)S(1)} collective-permute-done((bf16[512,128]{1,0:T(8,128)(2,1)S(1)}, bf16[512,128]{1,0:T(8,128)(2,1)S(1)}, u32[]{:S(2)}, u32[]{:S(2)}) %collective-permute-start) | collective-permute-done | bytes 131104 | tf_op jit(solution)/shard_map/ppermute | solution.py:208
  15.9 0.5 %collective-permute-start.1 = (bf16[512,128]{1,0:T(8,128)(2,1)S(1)}, bf16[512,128]{1,0:T(8,128)(2,1)S(1)}, u32[]{:S(2)}, u32[]{:S(2)}) collective-permute-start(bf16[512,128]{1,0:T(8,128)(2,1)S(1)} %collective-permute-done.refs_4_), channel_id=1, source_target_pairs={{0,2},{1,3},{2,0},{3,1},{4,6},{5,7},{6,4},{7,5},{8,10},{9,11},{10,... | collective-permute-start | bytes 393224 | tf_op jit(solution)/shard_map/ppermute | solution.py:208
  16.4 1.0 %collective-permute-done.6.refs_3_ = bf16[512,128]{1,0:T(8,128)(2,1)S(1)} collective-permute-done((bf16[512,128]{1,0:T(8,128)(2,1)S(1)}, bf16[512,128]{1,0:T(8,128)(2,1)S(1)}, u32[]{:S(2)}, u32[]{:S(2)}) %collective-permute-start.6) | collective-permute-done | bytes 131104 | tf_op jit(solution)/shard_map/ppermute | solution.py:208
  17.5 2.5 %collective-permute-start.2 = (bf16[512,128]{1,0:T(8,128)(2,1)S(1)}, bf16[512,128]{1,0:T(8,128)(2,1)S(1)}, u32[]{:S(2)}, u32[]{:S(2)}) collective-permute-start(bf16[512,128]{1,0:T(8,128)(2,1)S(1)} %collective-permute-done.refs_4_), channel_id=1, source_target_pairs={{0,4},{1,5},{2,6},{3,7},{4,0},{5,1},{6,2},{7,3},{8,12},{9,13},{10,... | collective-permute-start | bytes 393224 | tf_op jit(solution)/shard_map/ppermute | solution.py:208
  20.0 2.3 %collective-permute-done.7.refs_5_ = bf16[512,128]{1,0:T(8,128)(2,1)S(1)} collective-permute-done((bf16[512,128]{1,0:T(8,128)(2,1)S(1)}, bf16[512,128]{1,0:T(8,128)(2,1)S(1)}, u32[]{:S(2)}, u32[]{:S(2)}) %collective-permute-start.7) | collective-permute-done | bytes 131104 | tf_op jit(solution)/shard_map/ppermute | solution.py:208
  22.3 0.1 collective-permute-start.9
  22.4 0.7 %collective-permute-done.1.refs_0_ = bf16[512,128]{1,0:T(8,128)(2,1)S(1)} collective-permute-done((bf16[512,128]{1,0:T(8,128)(2,1)S(1)}, bf16[512,128]{1,0:T(8,128)(2,1)S(1)}, u32[]{:S(2)}, u32[]{:S(2)}) %collective-permute-start.1) | collective-permute-done | bytes 131104 | tf_op jit(solution)/shard_map/ppermute | solution.py:208
  23.1 0.7 %collective-permute-done.2.refs_1_ = bf16[512,128]{1,0:T(8,128)(2,1)S(1)} collective-permute-done((bf16[512,128]{1,0:T(8,128)(2,1)S(1)}, bf16[512,128]{1,0:T(8,128)(2,1)S(1)}, u32[]{:S(2)}, u32[]{:S(2)}) %collective-permute-start.2) | collective-permute-done | bytes 131104 | tf_op jit(solution)/shard_map/ppermute | solution.py:208
  23.8 0.0 collective-permute-done.3.b_other
  23.8 0.1 collective-permute-start.10
  23.9 0.0 collective-permute-done.8.refs_6_
  23.9 0.2 collective-permute-done.9.refs_7_
  24.1 1.0 %gather_product.1 = (f32[512,384]{1,0:T(8,128)S(1)}, bf16[512,384]{1,0:T(8,128)(2,1)S(1)}) custom-call(bf16[8,128,384]{2,1,0:T(8,128)(2,1)S(1)} %get-tuple-element.18.b_own, bf16[8,128,384]{2,1,0:T(8,128)(2,1)S(1)} %collective-permute-done.3.b_other, bf16[512,128]{1,0:T(8,128)(2,1)S(1)} %get-tuple-element.19.refs_0_, ...), custom_call_target="tpu_custom_call" | custom-call | flops 805306368 | bytes 8388608 | tf_op jit(solution)/shard_map/gather_product/pallas_call | solution.py:253
  25.1 0.3 collective-permute-done.10.refs_2_
  25.4 0.9 %inflate.1 = (f32[512,384]{1,0:T(8,128)S(1)}, f32[8,384]{1,0:T(8,128)S(1)}, s16[6,128,128]{2,1,0:T(8,128)(2,1)S(1)}) custom-call(s32[1,128]{1,0:T(1,128)S(1)} %get-tuple-element.17.ints_far.ints, f32[512,384]{1,0:T(8,128)S(1)} %get-tuple-element.21.part, bf16[512,384]{1,0:T(8,128)(2,1)S(1)} %get-tuple-element.22.b_late, ...), custom_call_target="tpu_custom_call" | custom-call | tf_op jit(solution)/shard_map/inflate/pallas_call | solution.py:269
  26.3 0.6 %collective-permute-start.11 = (f32[8,384]{1,0:T(8,128)S(1)}, f32[8,384]{1,0:T(8,128)S(1)}, u32[]{:S(2)}, u32[]{:S(2)}) collective-permute-start(f32[8,384]{1,0:T(8,128)S(1)} %get-tuple-element.26.own), channel_id=1, source_target_pairs={{0,16},{16,0},{1,17},{17,1},{2,18},{18,2},{3,19},{19,3},{4,20},{20... | collective-permute-start | bytes 36872 | tf_op jit(solution)/shard_map/ppermute | solution.py:283
  26.9 1.5 %collective-permute-start.12 = (s16[6,128,128]{2,1,0:T(8,128)(2,1)S(1)}, s16[6,128,128]{2,1,0:T(8,128)(2,1)S(1)}, u32[]{:S(2)}, u32[]{:S(2)}) collective-permute-start(s16[6,128,128]{2,1,0:T(8,128)(2,1)S(1)} %get-tuple-element.29), channel_id=1, source_target_pairs={{0,16},{16,0},{1,17},{17,1},{2,18},{18,2},{3,19},{19,3},{4,20},{20... | collective-permute-start | bytes 589832 | tf_op jit(solution)/shard_map/ppermute | solution.py:284
  28.4 1.7 %collective-permute-done.11.other = f32[8,384]{1,0:T(8,128)S(1)} collective-permute-done((f32[8,384]{1,0:T(8,128)S(1)}, f32[8,384]{1,0:T(8,128)S(1)}, u32[]{:S(2)}, u32[]{:S(2)}) %collective-permute-start.11) | collective-permute-done | bytes 12320 | tf_op jit(solution)/shard_map/ppermute | solution.py:283
  30.2 1.6 %finish.1 = (bf16[512,384]{1,0:T(8,128)(2,1)}, bf16[12,128,128]{2,1,0:T(8,128)(2,1)}, f32[6,1,128]{2,1,0:T(1,128)S(1)}, f32[6,1,128]{2,1,0:T(1,128)S(1)}) custom-call(s32[1,128]{1,0:T(1,128)S(1)} %get-tuple-element.17.ints_far.ints, f32[512,384]{1,0:T(8,128)S(1)} %get-tuple-element.25.product, f32[8,384]{1,0:T(8,128)S(1)} %get-tuple-element.26.own, ...), custom_call_target="tpu_custom_call" | custom-call | tf_op jit(solution)/shard_map/finish/pallas_call | solution.py:285
  31.7 2.0 %collective-permute-done.12 = s16[6,128,128]{2,1,0:T(8,128)(2,1)S(1)} collective-permute-done((s16[6,128,128]{2,1,0:T(8,128)(2,1)S(1)}, s16[6,128,128]{2,1,0:T(8,128)(2,1)S(1)}, u32[]{:S(2)}, u32[]{:S(2)}) %collective-permute-start.12) | collective-permute-done | bytes 196640 | tf_op jit(solution)/shard_map/ppermute | solution.py:284
  33.7 0.8 %fusion = bf16[12,128,128]{2,1,0:T(8,128)(2,1)} fusion(bf16[12,128,128]{2,1,0:T(8,128)(2,1)} %get-tuple-element.28, s32[]{:T(128)S(6)} %select_n.3, s16[6,128,128]{2,1,0:T(8,128)(2,1)S(1)} %collective-permute-done.12, f32[6,128]{1,0:T(8,128)S(1)} %get-tuple-element.32, f32[6,128]{1,0:T(8,128)S(1)} %get-tuple-element.33), kind=kLoop, calls=%fused_computation.4 | loop fusion | flops 589824 | bytes 399364 | tf_op jit(solution)/shard_map/dynamic_update_slice | solution.py:300
  (4 shorter events, 0.1 us)
Async XLA Ops:
  2.0 21.8 %collective-permute-start.3 = (bf16[8,128,384]{2,1,0:T(8,128)(2,1)S(1)}, bf16[8,128,384]{2,1,0:T(8,128)(2,1)S(1)}, u32[]{:S(2)}, u32[]{:S(2)}) collective-permute-start(bf16[8,128,384]{2,1,0:T(8,128)(2,1)S(1)} %get-tuple-element.18.b_own), channel_id=1, source_target_pairs={{0,16},{16,0},{1,17},{17,1},{2,18},{18,2},{3,19},{19,3},{4,20},{20... | collective-permute-start | bytes 2359304 | tf_op jit(solution)/shard_map/ppermute | solution.py:232
  5.0 6.1 %collective-permute-start.4 = (bf16[512,128]{1,0:T(8,128)(2,1)S(1)}, bf16[512,128]{1,0:T(8,128)(2,1)S(1)}, u32[]{:S(2)}, u32[]{:S(2)}) collective-permute-start(bf16[512,128]{1,0:T(8,128)(2,1)S(1)} %get-tuple-element.19.refs_0_), channel_id=1, source_target_pairs={{0,2},{1,3},{2,0},{3,1},{4,6},{5,7},{6,4},{7,5},{8,10},{9,11},{10,... | collective-permute-start | bytes 393224 | tf_op jit(solution)/shard_map/ppermute | solution.py:208
  6.5 8.1 %collective-permute-start.5 = (bf16[512,128]{1,0:T(8,128)(2,1)S(1)}, bf16[512,128]{1,0:T(8,128)(2,1)S(1)}, u32[]{:S(2)}, u32[]{:S(2)}) collective-permute-start(bf16[512,128]{1,0:T(8,128)(2,1)S(1)} %get-tuple-element.19.refs_0_), channel_id=1, source_target_pairs={{0,4},{1,5},{2,6},{3,7},{4,0},{5,1},{6,2},{7,3},{8,12},{9,13},{10,... | collective-permute-start | bytes 393224 | tf_op jit(solution)/shard_map/ppermute | solution.py:208
  8.1 7.8 %collective-permute-start = (bf16[512,128]{1,0:T(8,128)(2,1)S(1)}, bf16[512,128]{1,0:T(8,128)(2,1)S(1)}, u32[]{:S(2)}, u32[]{:S(2)}) collective-permute-start(bf16[512,128]{1,0:T(8,128)(2,1)S(1)} %get-tuple-element.19.refs_0_), channel_id=1, source_target_pairs={{0,8},{1,9},{2,10},{3,11},{4,12},{5,13},{6,14},{7,15},{8,0},{9,1},... | collective-permute-start | bytes 393224 | tf_op jit(solution)/shard_map/ppermute | solution.py:208
  10.7 6.8 %collective-permute-start.6 = (bf16[512,128]{1,0:T(8,128)(2,1)S(1)}, bf16[512,128]{1,0:T(8,128)(2,1)S(1)}, u32[]{:S(2)}, u32[]{:S(2)}) collective-permute-start(bf16[512,128]{1,0:T(8,128)(2,1)S(1)} %get-tuple-element.19.refs_0_), channel_id=1, source_target_pairs={{0,6},{1,7},{2,4},{3,5},{4,2},{5,3},{6,0},{7,1},{8,14},{9,15},{10,... | collective-permute-start | bytes 393224 | tf_op jit(solution)/shard_map/ppermute | solution.py:208
  11.1 11.2 %collective-permute-start.7 = (bf16[512,128]{1,0:T(8,128)(2,1)S(1)}, bf16[512,128]{1,0:T(8,128)(2,1)S(1)}, u32[]{:S(2)}, u32[]{:S(2)}) collective-permute-start(bf16[512,128]{1,0:T(8,128)(2,1)S(1)} %get-tuple-element.19.refs_0_), channel_id=1, source_target_pairs={{0,14},{1,15},{2,12},{3,13},{4,10},{5,11},{6,8},{7,9},{8,6},{9,7},... | collective-permute-start | bytes 393224 | tf_op jit(solution)/shard_map/ppermute | solution.py:208
  14.6 9.3 %collective-permute-start.8 = (bf16[1536,128]{1,0:T(8,128)(2,1)S(1)}, bf16[1536,128]{1,0:T(8,128)(2,1)S(1)}, u32[]{:S(2)}, u32[]{:S(2)}) collective-permute-start(bf16[1536,128]{1,0:T(8,128)(2,1)S(1)} %pad_maximum_fusion), channel_id=1, source_target_pairs={{0,1},{1,0},{2,3},{3,2},{4,5},{5,4},{6,7},{7,6},{8,9},{9,8},{10,11... | collective-permute-start | bytes 1179656 | tf_op jit(solution)/shard_map/ppermute | solution.py:208
  15.9 7.2 %collective-permute-start.1 = (bf16[512,128]{1,0:T(8,128)(2,1)S(1)}, bf16[512,128]{1,0:T(8,128)(2,1)S(1)}, u32[]{:S(2)}, u32[]{:S(2)}) collective-permute-start(bf16[512,128]{1,0:T(8,128)(2,1)S(1)} %collective-permute-done.refs_4_), channel_id=1, source_target_pairs={{0,2},{1,3},{2,0},{3,1},{4,6},{5,7},{6,4},{7,5},{8,10},{9,11},{10,... | collective-permute-start | bytes 393224 | tf_op jit(solution)/shard_map/ppermute | solution.py:208
  17.5 6.3 %collective-permute-start.2 = (bf16[512,128]{1,0:T(8,128)(2,1)S(1)}, bf16[512,128]{1,0:T(8,128)(2,1)S(1)}, u32[]{:S(2)}, u32[]{:S(2)}) collective-permute-start(bf16[512,128]{1,0:T(8,128)(2,1)S(1)} %collective-permute-done.refs_4_), channel_id=1, source_target_pairs={{0,4},{1,5},{2,6},{3,7},{4,0},{5,1},{6,2},{7,3},{8,12},{9,13},{10,... | collective-permute-start | bytes 393224 | tf_op jit(solution)/shard_map/ppermute | solution.py:208
  22.3 1.8 %collective-permute-start.9 = (bf16[1536,128]{1,0:T(8,128)(2,1)S(1)}, bf16[1536,128]{1,0:T(8,128)(2,1)S(1)}, u32[]{:S(2)}, u32[]{:S(2)}) collective-permute-start(bf16[1536,128]{1,0:T(8,128)(2,1)S(1)} %pad_maximum_fusion.1), channel_id=1, source_target_pairs={{0,1},{1,0},{2,3},{3,2},{4,5},{5,4},{6,7},{7,6},{8,9},{9,8},{10,11... | collective-permute-start | bytes 1179656 | tf_op jit(solution)/shard_map/ppermute | solution.py:208
  23.8 1.6 %collective-permute-start.10 = (bf16[1024,128]{1,0:T(8,128)(2,1)S(1)}, bf16[1024,128]{1,0:T(8,128)(2,1)S(1)}, u32[]{:S(2)}, u32[]{:S(2)}) collective-permute-start(bf16[1024,128]{1,0:T(8,128)(2,1)S(1)} %pad_maximum_fusion.2), channel_id=1, source_target_pairs={{0,1},{1,0},{2,3},{3,2},{4,5},{5,4},{6,7},{7,6},{8,9},{9,8},{10,11... | collective-permute-start | bytes 786440 | tf_op jit(solution)/shard_map/ppermute | solution.py:208
  26.3 3.8 %collective-permute-start.11 = (f32[8,384]{1,0:T(8,128)S(1)}, f32[8,384]{1,0:T(8,128)S(1)}, u32[]{:S(2)}, u32[]{:S(2)}) collective-permute-start(f32[8,384]{1,0:T(8,128)S(1)} %get-tuple-element.26.own), channel_id=1, source_target_pairs={{0,16},{16,0},{1,17},{17,1},{2,18},{18,2},{3,19},{19,3},{4,20},{20... | collective-permute-start | bytes 36872 | tf_op jit(solution)/shard_map/ppermute | solution.py:283
  26.9 6.8 %collective-permute-start.12 = (s16[6,128,128]{2,1,0:T(8,128)(2,1)S(1)}, s16[6,128,128]{2,1,0:T(8,128)(2,1)S(1)}, u32[]{:S(2)}, u32[]{:S(2)}) collective-permute-start(s16[6,128,128]{2,1,0:T(8,128)(2,1)S(1)} %get-tuple-element.29), channel_id=1, source_target_pairs={{0,16},{16,0},{1,17},{17,1},{2,18},{18,2},{3,19},{19,3},{4,20},{20... | collective-permute-start | bytes 589832 | tf_op jit(solution)/shard_map/ppermute | solution.py:284
